TPU v7x, 1024 devices: a whole 4x4x32 slice. The times are simulated.
1024 devices in a mesh: expert: 64 (over z, core), tensor: 16 (over x, y).
Axes of the slice: x: 4, y: 4, z: 32, core: 2. Of those that a mesh axis runs over, the one named last changes fastest.
Arguments:
- grads: bfloat16 [16384, 7168], P('expert', 'tensor'), may hold values from -6 to 6
- routes: int32 [16384, 2], P('expert'), may hold values from 0 to 127, all different within a row; in each aligned block of 256 rows (0 to 255, 256 to 511, ...) at most 6 rows name the same one
- gates: float32 [16384, 2], P('expert'), may hold values from 0.2 to 1
- dense_down: bfloat16 [2432, 7168], P(None, 'tensor'), may hold values from -0.15625 to 0.15625
- dense_up: bfloat16 [7168, 2432], P('tensor'), may hold values from -0.0625 to 0.0625
- dense_act: bfloat16 [16384, 2432], P('expert', 'tensor'), may hold values from -6 to 6
- expert_down: bfloat16 [64, 1216, 7168], P('expert', None, 'tensor'), may hold values from -0.15625 to 0.15625
- expert_up: bfloat16 [64, 7168, 1216], P('expert', 'tensor'), may hold values from -0.0625 to 0.0625
- expert_act: bfloat16 [64, 384, 1216], P('expert', None, 'tensor'), may hold values from -6 to 6
Outputs:
- input_grad: bfloat16 [16384, 7168], P('expert', 'tensor')
Inputs may be any that keep to these rules, and one draw needn't show every extreme that they name: `routes`: each row names two different experts; ids below 32 are held here. Within the 256 tokens of one index of expert no id is named more than 6 times, a bound that some block reaches.
All inputs are finite; a program needn't handle non-finite values.
Results may differ from a plain program's by a relative error of at most 0.02.
Values may be sent and summed in bfloat16 or wider, within the bound.
No kernel may reach another device: no remote copies, remote signals or barrier semaphores. Data moves between devices by JAX's collectives and lax.ppermute only.
A program may use at most 32 MiB of HBM per device.

v0:
```python
import jax
import jax.numpy as jnp
from jax import lax
from jax.sharding import PartitionSpec as P

ALL_EXPERTS = 128
CAP = 6


def contract_last(left, right):
    return lax.dot_general(
        left, right, (((1,), (1,)), ((), ())), preferred_element_type=jnp.float32
    )


def shards(
    grads, routes, gates, dense_down, dense_up, dense_act, expert_down, expert_up, expert_act
):
    groups = lax.axis_size("expert")
    held = groups // 2
    tokens_here = grads.shape[0]
    row_width = grads.shape[1]
    route_ids = routes.reshape(-1)
    onehot = (route_ids[:, None] == jnp.arange(ALL_EXPERTS, dtype=jnp.int32)[None, :]).astype(
        jnp.int32
    )
    earlier = jnp.cumsum(onehot, axis=0) - onehot
    within = jnp.sum(earlier * onehot, axis=1)
    in_window = route_ids < held
    target = jnp.where(in_window, route_ids * CAP + within, -1)
    chooser = (jnp.arange(held * CAP, dtype=jnp.int32)[:, None] == target[None, :]).astype(
        jnp.bfloat16
    )
    routed = (
        (grads.astype(jnp.float32)[:, None, :] * gates[:, :, None])
        .astype(jnp.bfloat16)
        .reshape(-1, row_width)
    )
    outgoing = jnp.dot(chooser, routed, preferred_element_type=jnp.float32).astype(jnp.bfloat16)
    outgoing = jnp.repeat(outgoing.reshape(held, CAP, row_width), 2, axis=0)
    arrived = lax.all_to_all(outgoing, "expert", split_axis=0, concat_axis=0, tiled=True).reshape(
        groups * CAP, row_width
    )
    dense_mid = contract_last(grads, dense_down)
    expert_mid = contract_last(arrived, expert_down[0])
    dense_share, expert_share = (
        lax.psum_scatter(
            dense_mid.astype(jnp.bfloat16), "tensor", scatter_dimension=1, tiled=True
        ).astype(jnp.float32),
        lax.psum_scatter(
            expert_mid.astype(jnp.bfloat16), "tensor", scatter_dimension=1, tiled=True
        ).astype(jnp.float32),
    )
    dense_half = (dense_share * jax.nn.silu(dense_act.astype(jnp.float32))).astype(jnp.bfloat16)
    expert_half = (expert_share * jax.nn.silu(expert_act[0].astype(jnp.float32))).astype(
        jnp.bfloat16
    )
    expert_cols = expert_up[0]
    dense_sum = contract_last(lax.all_gather(dense_half, "tensor", axis=1, tiled=True), dense_up)
    expert_sum = contract_last(
        lax.all_gather(expert_half, "tensor", axis=1, tiled=True), expert_cols
    )
    expert_rows = expert_sum.astype(jnp.bfloat16).reshape(groups, CAP, row_width)
    returned = lax.all_to_all(expert_rows, "expert", split_axis=0, concat_axis=0, tiled=True)
    paired = jnp.sum(returned.reshape(held, 2, CAP, row_width).astype(jnp.float32), axis=1)
    routed_back = lax.dot_general(
        chooser.astype(jnp.float32),
        paired.reshape(held * CAP, row_width),
        (((0,), (0,)), ((), ())),
        preferred_element_type=jnp.float32,
    )
    combined = dense_sum + jnp.sum(routed_back.reshape(tokens_here, 2, row_width), axis=1)
    return combined.astype(jnp.bfloat16)


def solution(mesh):
    placed = (
        P("expert", "tensor"),
        P("expert", None),
        P("expert", None),
        P(None, "tensor"),
        P("tensor", None),
        P("expert", "tensor"),
        P("expert", None, "tensor"),
        P("expert", "tensor", None),
        P("expert", None, "tensor"),
    )
    return jax.shard_map(
        shards, mesh=mesh, in_specs=placed, out_specs=P("expert", "tensor"), check_vma=False
    )
```

profile of v0, /device:TPU:1, one launch (start us, length us, event | category | flops | bytes accessed | tf_op | source)
XLA Modules:
  0.0 339.9 jit_solution(15690372612516457602)
XLA Ops:
  6.5 1.0 copy.19
  8.4 1.1 copy.23
  9.5 1.4 mul.50
  10.8 2.0 mul.51
  17.0 30.4 %all-to-all-start = ((bf16[64,6,448]{2,1,0:T(8,128)(2,1)}), bf16[64,6,448]{2,1,0:T(8,128)(2,1)S(1)}, u32[]{:S(2)}, u32[]{:S(2)}) async-start(bf16[64,6,448]{2,1,0:T(8,128)(2,1)} %bitcast.3), calls=%async_computation | async-start | bytes 1048576 | tf_op jit(solution)/shard_map/all_to_all | solution.py:41
  47.5 2.1 convolution_convert_fusion
  49.7 61.9 %all-to-all-done = bf16[64,6,448]{2,1,0:T(8,128)(2,1)S(1)} async-done(((bf16[64,6,448]{2,1,0:T(8,128)(2,1)}), bf16[64,6,448]{2,1,0:T(8,128)(2,1)S(1)}, u32[]{:S(2)}, u32[]{:S(2)}) %all-to-all-start) | async-done | bytes 344096 | tf_op jit(solution)/shard_map/all_to_all | solution.py:41
  111.8 2.1 convolution_convert_fusion.1
  113.9 59.2 %fusion = bf16[384,96]{0,1:T(8,128)(2,1)S(1)} fusion(bf16[384,1216]{0,1:T(8,128)(2,1)S(1)} %convolution_convert_fusion.1), kind=kCustom, calls=%all-reduce-scatter | all-reduce-scatter fusion | flops 589825 | bytes 1011712
  173.1 3.4 %collective-permute-start.2 = (bf16[384,96]{0,1:T(8,128)(2,1)S(1)}, bf16[384,96]{0,1:T(8,128)(2,1)S(1)}, u32[]{:S(2)}, u32[]{:S(2)}) collective-permute-start(bf16[384,96]{0,1:T(8,128)(2,1)S(1)} %fusion), channel_id=1, source_target_pairs={{0,3},{1,4},{2,5},{3,6},{4,7},{5,8},{6,9},{7,10},{8,11},{9,12},{10... | collective-permute-start | bytes 221192
  176.5 2.3 collective-permute-start.1
  178.9 3.1 collective-permute-start
  182.0 2.5 collective-permute-start.3
  184.6 1.3 dynamic-slice.6
  186.5 1.3 concatenate
  187.9 20.2 %all-gather = bf16[16,76,384]{2,1,0:T(8,128)(2,1)S(1)} all-gather(bf16[1,76,384]{2,1,0:T(8,128)(2,1)S(1)} %fusion.22), channel_id=1, replica_groups=mesh['expert'=64,'tensor'=16] {'tensor'}, dimensions={0}, use_global_device_ids=true | all-gather | bytes 992256 | tf_op jit(solution)/shard_map/all_gather | solution.py:61
  208.0 1.1 reshape.95
  209.1 2.3 convolution_convert_fusion.2
  211.6 1.0 reshape.90
  212.6 35.9 %all-to-all-start.1 = ((bf16[64,6,448]{2,1,0:T(8,128)(2,1)}), bf16[64,6,448]{2,1,0:T(8,128)(2,1)S(1)}, u32[]{:S(2)}, u32[]{:S(2)}) async-start(bf16[64,6,448]{2,1,0:T(8,128)(2,1)} %reshape.90), calls=%async_computation.1 | async-start | bytes 1048576 | tf_op jit(solution)/shard_map/all_to_all | solution.py:64
  248.6 1.6 fusion.15
  250.5 62.0 %all-to-all-done.1 = bf16[64,6,448]{2,1,0:T(8,128)(2,1)S(1)} async-done(((bf16[64,6,448]{2,1,0:T(8,128)(2,1)}), bf16[64,6,448]{2,1,0:T(8,128)(2,1)S(1)}, u32[]{:S(2)}, u32[]{:S(2)}) %all-to-all-start.1) | async-done | bytes 344096 | tf_op jit(solution)/shard_map/all_to_all | solution.py:64
  313.2 16.5 %all-gather.3.cloned.1.call-done = bf16[256,2432]{0,1:T(8,128)(2,1)} async-done(((bf16[256,152]{0,1:T(8,128)(2,1)}), bf16[256,2432]{0,1:T(8,128)(2,1)}) %all-gather.3.cloned.1.call-update) | async-done | bytes 1245200 | tf_op jit(solution)/shard_map/all_gather | solution.py:59
  329.6 3.4 fusion.1
  (47 shorter events, 6.6 us)
Async XLA Ops:
  6.5 41.0 %copy-start = (bf16[2432,448]{0,1:T(8,128)(2,1)S(1)}, bf16[2432,448]{0,1:T(8,128)(2,1)}, u32[]{:S(2)}) copy-start(bf16[2432,448]{0,1:T(8,128)(2,1)} %param.12) | copy-start | bytes 6537220
  10.8 2.0 copy-start.5
  14.0 1.7 copy-start.4
  16.1 31.4 %copy-start.1 = (bf16[256,448]{0,1:T(8,128)(2,1)S(1)}, bf16[256,448]{0,1:T(8,128)(2,1)}, u32[]{:S(2)}) copy-start(bf16[256,448]{0,1:T(8,128)(2,1)} %param.9) | copy-start | bytes 688132
  17.0 94.5 %all-to-all-start = ((bf16[64,6,448]{2,1,0:T(8,128)(2,1)}), bf16[64,6,448]{2,1,0:T(8,128)(2,1)S(1)}, u32[]{:S(2)}, u32[]{:S(2)}) async-start(bf16[64,6,448]{2,1,0:T(8,128)(2,1)} %bitcast.3), calls=%async_computation | async-start | bytes 1048576 | tf_op jit(solution)/shard_map/all_to_all | solution.py:41
  47.4 201.1 %reduce-scatter.6.cloned.1.call-start = ((), (), s32[]{:S(2)}) async-start(), calls=%async_computation.4 | async-start | bytes 1323008
  113.9 73.9 %copy-start.3 = (bf16[1,384,76]{1,2,0:T(8,128)(2,1)S(1)}, bf16[1,384,76]{1,2,0:T(8,128)(2,1)}, u32[]{:S(2)}) copy-start(bf16[1,384,76]{1,2,0:T(8,128)(2,1)} %param.17) | copy-start | bytes 175108
  173.1 13.4 %collective-permute-start.2 = (bf16[384,96]{0,1:T(8,128)(2,1)S(1)}, bf16[384,96]{0,1:T(8,128)(2,1)S(1)}, u32[]{:S(2)}, u32[]{:S(2)}) collective-permute-start(bf16[384,96]{0,1:T(8,128)(2,1)S(1)} %fusion), channel_id=1, source_target_pairs={{0,3},{1,4},{2,5},{3,6},{4,7},{5,8},{6,9},{7,10},{8,11},{9,12},{10... | collective-permute-start | bytes 221192
  176.5 10.0 %collective-permute-start.1 = (bf16[384,96]{0,1:T(8,128)(2,1)S(1)}, bf16[384,96]{0,1:T(8,128)(2,1)S(1)}, u32[]{:S(2)}, u32[]{:S(2)}) collective-permute-start(bf16[384,96]{0,1:T(8,128)(2,1)S(1)} %fusion), channel_id=1, source_target_pairs={{0,2},{1,3},{2,4},{3,5},{4,6},{5,7},{6,8},{7,9},{8,10},{9,11},{10,... | collective-permute-start | bytes 221192
  178.9 7.6 %collective-permute-start = (bf16[384,96]{0,1:T(8,128)(2,1)S(1)}, bf16[384,96]{0,1:T(8,128)(2,1)S(1)}, u32[]{:S(2)}, u32[]{:S(2)}) collective-permute-start(bf16[384,96]{0,1:T(8,128)(2,1)S(1)} %fusion), channel_id=1, source_target_pairs={{0,1},{1,2},{2,3},{3,4},{4,5},{5,6},{6,7},{7,8},{8,9},{9,10},{10,1... | collective-permute-start | bytes 221192
  182.0 4.5 %collective-permute-start.3 = (bf16[384,12]{0,1:T(8,128)(2,1)S(1)}, bf16[384,12]{0,1:T(8,128)(2,1)S(1)}, u32[]{:S(2)}, u32[]{:S(2)}) collective-permute-start(bf16[384,12]{0,1:T(8,128)(2,1)S(1)} %slice.9), channel_id=1, source_target_pairs={{0,4},{1,5},{2,6},{3,7},{4,8},{5,9},{6,10},{7,11},{8,12},{9,13},{1... | collective-permute-start | bytes 27656
  211.4 37.1 %copy-start.2 = (bf16[256,152]{0,1:T(8,128)(2,1)S(1)}, bf16[256,152]{0,1:T(8,128)(2,1)}, u32[]{:S(2)}) copy-start(bf16[256,152]{0,1:T(8,128)(2,1)} %param.14) | copy-start | bytes 233476
  212.6 99.9 %all-to-all-start.1 = ((bf16[64,6,448]{2,1,0:T(8,128)(2,1)}), bf16[64,6,448]{2,1,0:T(8,128)(2,1)S(1)}, u32[]{:S(2)}, u32[]{:S(2)}) async-start(bf16[64,6,448]{2,1,0:T(8,128)(2,1)} %reshape.90), calls=%async_computation.1 | async-start | bytes 1048576 | tf_op jit(solution)/shard_map/all_to_all | solution.py:64
  248.5 81.1 %all-gather.3.cloned.1.call-start = ((), (), s32[]{:S(2)}) async-start(), calls=%async_computation.3 | async-start | bytes 1323008 | tf_op jit(solution)/shard_map/all_gather | solution.py:59
Sparse Core Ops, SparseCore 0:
  53.6 107.4 reduce-scatter.5
  254.3 75.2 all-gather.2
where the time goes:
time: 341 us; the launch traced here: 340 us
  waiting for transfers between devices  140 us (41%)
  blocking collectives  79.3 us (23%)
  starting transfers between devices  77.8 us (23%)
  between operations  14.4 us (4%)
  local copies, waits for them, and re-layouts  13.6 us (4%)
  matrix products  10.6 us (3%)
  other arithmetic  3.74 us (1%)
    all_to_all x1, waiting for transfers between devices, shards(): lax.all_to_all(expert_rows, 'expert', split_axis=0, concat_axis=0, tiled=...  62 us
    all_to_all x1, waiting for transfers between devices, shards(): lax.all_to_all(outgoing, 'expert', split_axis=0, concat_axis=0, tiled=True)  61.9 us
    unnamed x1, blocking collectives  59.2 us
    all_to_all x1, starting transfers between devices, shards(): lax.all_to_all(expert_rows, 'expert', split_axis=0, concat_axis=0, tiled=...  35.9 us
    all_to_all x1, starting transfers between devices, shards(): lax.all_to_all(outgoing, 'expert', split_axis=0, concat_axis=0, tiled=True)  30.4 us
    all_gather x1, blocking collectives, shards(): lax.all_gather(expert_half, 'tensor', axis=1, tiled=True)  20.2 us
    all_gather x1, waiting for transfers between devices, shards(): lax.all_gather(dense_half, 'tensor', axis=1, tiled=True)  16.5 us
    unnamed x5, starting transfers between devices  11.4 us
  transfers between devices with their start and end apart: 8, of which 3 were waited for; matrix products, arithmetic and copies ran while one was open for 22% of the time, Pallas kernels for 0%

commit v1 on v0

v1 whole, which is shorter than its diff:
```python
import jax
import jax.numpy as jnp
from jax import lax
from jax.sharding import Mesh, PartitionSpec as P

CAP = 6
SWAP = [(0, 1), (1, 0)]


def contract_last(left, right):
    return lax.dot_general(
        left, right, (((1,), (1,)), ((), ())), preferred_element_type=jnp.float32
    )


def shards(
    grads, routes, gates, dense_down, dense_up, dense_act, expert_down, expert_up, expert_act
):
    held = lax.axis_size("z")
    parts = lax.axis_size("t")
    tokens, width = grads.shape
    half = expert_down.shape[1]
    piece = half // parts
    slots = held * CAP
    core = lax.axis_index("c")

    down_other = lax.ppermute(expert_down[0], "c", SWAP)
    up_other = lax.ppermute(expert_up[0], "c", SWAP)
    act_other = lax.ppermute(expert_act[0], "c", SWAP)

    ids = routes.T
    experts = jnp.arange(held, dtype=jnp.int32)[:, None]
    first, second = ids[0:1] == experts, ids[1:2] == experts
    named = (first | second).astype(jnp.bfloat16)
    before = (jnp.arange(tokens)[:, None] < jnp.arange(tokens)[None, :]).astype(jnp.bfloat16)
    rank = jnp.dot(named, before, preferred_element_type=jnp.float32).astype(jnp.int32)
    place = experts * CAP + rank + 1
    slot_ids = jnp.arange(slots, dtype=jnp.int32)[:, None]
    hit_first = (jnp.sum(jnp.where(first, place, 0), axis=0, keepdims=True) - 1) == slot_ids
    hit_second = (jnp.sum(jnp.where(second, place, 0), axis=0, keepdims=True) - 1) == slot_ids
    gate_rows = gates.T
    slot_gate = jnp.sum(
        jnp.where(hit_first, gate_rows[0:1], 0.0) + jnp.where(hit_second, gate_rows[1:2], 0.0),
        axis=1,
        keepdims=True,
    )
    chooser = (hit_first | hit_second).astype(jnp.bfloat16)
    outgoing = (
        jnp.dot(chooser, grads, preferred_element_type=jnp.float32) * slot_gate
    ).astype(jnp.bfloat16)
    arrived = lax.all_to_all(outgoing.reshape(held, CAP, width), "z", 0, 0, tiled=True).reshape(
        slots, width
    )

    def interleaved(own, other):
        return jnp.concatenate(
            [own.reshape(parts, piece, width), other.reshape(parts, piece, width)], axis=1
        ).reshape(2 * half, width)

    down_both = interleaved(expert_down[0], down_other)
    up_both = interleaved(expert_up[0].T, up_other.T)
    act_both = jnp.concatenate([expert_act[0].T, act_other.T], axis=0)
    act_rows = lax.dynamic_index_in_dim(
        act_both.reshape(2 * piece, held, 2, CAP), core, axis=2, keepdims=False
    ).reshape(2 * piece, slots)
    act = jnp.concatenate([act_rows, dense_act.T], axis=1).astype(jnp.float32)

    mid = jnp.concatenate(
        [contract_last(down_both, arrived), contract_last(dense_down, grads)], axis=1
    ).astype(jnp.bfloat16)
    shares = lax.all_to_all(
        mid.reshape(parts, 2 * piece, slots + tokens), "t", 0, 0, tiled=True
    )
    total = jnp.sum(shares.astype(jnp.float32), axis=0)
    hidden = (total * jax.nn.silu(act)).astype(jnp.bfloat16)
    full = lax.all_gather(hidden, "t", axis=0, tiled=True)

    rows = lax.dot_general(
        full[:, :slots], up_both, (((0,), (0,)), ((), ())), preferred_element_type=jnp.float32
    ).astype(jnp.bfloat16)
    returned = lax.all_to_all(rows.reshape(held, CAP, width), "z", 0, 0, tiled=True).reshape(
        slots, width
    )
    dense_sum = lax.dot_general(
        full[:, slots:], dense_up, (((0,), (1,)), ((), ())), preferred_element_type=jnp.float32
    )
    routed_back = lax.dot_general(
        chooser, returned, (((0,), (0,)), ((), ())), preferred_element_type=jnp.float32
    )
    return (dense_sum + routed_back).astype(jnp.bfloat16)


def solution(mesh):
    groups, parts = mesh.devices.shape
    split = Mesh(mesh.devices.reshape(groups // 2, 2, parts), ("z", "c", "t"))
    blocks = ("z", "c")
    placed = (
        P(blocks, "t"),
        P(blocks, None),
        P(blocks, None),
        P(None, "t"),
        P("t", None),
        P(blocks, "t"),
        P(blocks, None, "t"),
        P(blocks, "t", None),
        P(blocks, None, "t"),
    )
    return jax.shard_map(
        shards, mesh=split, in_specs=placed, out_specs=P(blocks, "t"), check_vma=False
    )
```

time: 341 us -> 272 us (0.80)
  waiting for transfers between devices: 140 us -> 99.6 us
  starting transfers between devices: 77.8 us -> 52.4 us
  blocking collectives: 79.3 us -> 61.2 us
  other arithmetic: 3.74 us -> 9.1 us
  local copies, waits for them, and re-layouts: 13.6 us -> 18.7 us
    all_to_all x2, waiting for transfers between devices: 124 us -> 51.2 us  [the longest x1 28.7 us: shards(): lax.all_to_all(outgoing.reshape(held, CAP, width), 'z', 0, 0, tiled=True)]
    all_to_all x0 -> x1, blocking collectives: none -> 61.2 us  [shards(): lax.all_to_all(rows.reshape(held, CAP, width), 'z', 0, 0, tiled=True)]
    unnamed x1 -> x0, blocking collectives: 59.2 us -> none
    all_gather x1, waiting for transfers between devices: 16.5 us -> 47.4 us  [shards(): full = lax.all_gather(hidden, 't', axis=0, tiled=True)]
    all_to_all x2, starting transfers between devices: 66.3 us -> 36.3 us  [the longest x1 29.4 us: shards(): lax.all_to_all(outgoing.reshape(held, CAP, width), 'z', 0, 0, tiled=True)]
    all_gather x1 -> x0, blocking collectives: 20.2 us -> none  [shards(): lax.all_gather(expert_half, 'tensor', axis=1, tiled=True)]
    ppermute x0 -> x3, starting transfers between devices: none -> 16 us  [the longest x1 8.06 us: shards(): up_other = lax.ppermute(expert_up[0], 'c', SWAP)]
    unnamed x5 -> x0, starting transfers between devices: 11.4 us -> none
  transfers between devices with their start and end apart: 8 -> 6, of which waited for: 3 -> 4; matrix products, arithmetic and copies ran while one was open for 22% -> 8% of each run, Pallas kernels for 0% -> 0%
where the time goes in v1:
time: 272 us; the launch traced here: 268 us
  waiting for transfers between devices  99.6 us (37%)
  blocking collectives  61.2 us (22%)
  starting transfers between devices  52.4 us (19%)
  local copies, waits for them, and re-layouts  18.7 us (7%)
  matrix products  13.7 us (5%)
  between operations  13.6 us (5%)
  other arithmetic  9.1 us (3%)
    all_to_all x1, blocking collectives, shards(): lax.all_to_all(rows.reshape(held, CAP, width), 'z', 0, 0, tiled=True)  61.2 us
    all_gather x1, waiting for transfers between devices, shards(): full = lax.all_gather(hidden, 't', axis=0, tiled=True)  47.4 us
    all_to_all x1, starting transfers between devices, shards(): lax.all_to_all(outgoing.reshape(held, CAP, width), 'z', 0, 0, tiled=True)  29.4 us
    all_to_all x1, waiting for transfers between devices, shards(): lax.all_to_all(outgoing.reshape(held, CAP, width), 'z', 0, 0, tiled=True)  28.7 us
    all_to_all x1, waiting for transfers between devices, shards(): lax.all_to_all(mid.reshape(parts, 2 * piece, slots + tokens), 't', 0, 0,...  22.5 us
    ppermute x1, starting transfers between devices, shards(): up_other = lax.ppermute(expert_up[0], 'c', SWAP)  8.06 us
    all_to_all x1, starting transfers between devices, shards(): lax.all_to_all(mid.reshape(parts, 2 * piece, slots + tokens), 't', 0, 0,...  6.93 us
    dot_general x2, matrix products, contract_last(): lax.dot_general(left, right, (((1,), (1,)), ((), ())), preferred_element_...  5.53 us
  transfers between devices with their start and end apart: 6, of which 4 were waited for; matrix products, arithmetic and copies ran while one was open for 8% of the time, Pallas kernels for 0%

profile of v1, /device:TPU:1, one launch (start us, length us, event | category | flops | bytes accessed | tf_op | source)
XLA Modules:
  0.0 268.2 jit_solution(2096857052480401575)
XLA Ops:
  10.4 29.4 %all-to-all-start = ((bf16[32,6,448]{2,1,0:T(8,128)(2,1)}), bf16[32,6,448]{2,1,0:T(8,128)(2,1)}, u32[]{:S(2)}, u32[]{:S(2)}) async-start(bf16[32,6,448]{2,1,0:T(8,128)(2,1)} %reshape.53), calls=%async_computation | async-start | bytes 524288 | tf_op jit(solution)/shard_map/all_to_all | solution.py:51
  39.9 2.9 %collective-permute-start = (bf16[1216,448]{0,1:T(8,128)(2,1)}, bf16[1216,448]{0,1:T(8,128)(2,1)}, u32[]{:S(2)}, u32[]{:S(2)}) collective-permute-start(bf16[1216,448]{0,1:T(8,128)(2,1)} %bitcast.31), channel_id=1, source_target_pairs={{0,16},{16,0},{1,17},{17,1},{2,18},{18,2},{3,19},{19,3},{4,20},{20... | collective-permute-start | bytes 3268616 | tf_op jit(solution)/shard_map/ppermute | solution.py:27
  42.7 1.8 copy.18
  44.5 1.2 reshape_squeeze.3
  45.8 2.9 %convolution_convert_fusion = bf16[2432,256]{1,0:T(8,128)(2,1)} fusion(bf16[2432,448]{0,1:T(8,128)(2,1)S(1)} %copy-done, bf16[256,448]{0,1:T(8,128)(2,1)} %param.9), kind=kOutput, calls=%fused_computation.1 | convolution fusion | flops 558465024 | bytes 3653632 | tf_op jit(solution)/shard_map/dot_general | solution.py:11
  48.7 1.8 copy.19
  50.4 1.2 reshape.52
  51.7 28.7 %all-to-all-done = bf16[32,6,448]{2,1,0:T(8,128)(2,1)} async-done(((bf16[32,6,448]{2,1,0:T(8,128)(2,1)}), bf16[32,6,448]{2,1,0:T(8,128)(2,1)}, u32[]{:S(2)}, u32[]{:S(2)}) %all-to-all-start) | async-done | bytes 172064 | tf_op jit(solution)/shard_map/all_to_all | solution.py:51
  81.5 2.6 fusion.4
  84.1 2.5 pad_maximum_fusion
  86.6 6.9 %all-to-all-start.1 = ((bf16[16,152,448]{2,1,0:T(8,128)(2,1)}), bf16[16,152,448]{2,1,0:T(8,128)(2,1)}, u32[]{:S(2)}, u32[]{:S(2)}) async-start(bf16[16,152,448]{2,1,0:T(8,128)(2,1)} %pad_maximum_fusion), calls=%async_computation.1 | async-start | bytes 4980736 | tf_op jit(solution)/shard_map/all_to_all | solution.py:71
  93.6 5.1 %collective-permute-start.1 = (bf16[384,76]{0,1:T(8,128)(2,1)S(1)}, bf16[384,76]{0,1:T(8,128)(2,1)S(1)}, u32[]{:S(2)}, u32[]{:S(2)}) collective-permute-start(bf16[384,76]{0,1:T(8,128)(2,1)S(1)} %bitcast.33), channel_id=1, source_target_pairs={{0,16},{16,0},{1,17},{17,1},{2,18},{18,2},{3,19},{19,3},{4,20},{20... | collective-permute-start | bytes 175112 | tf_op jit(solution)/shard_map/ppermute | solution.py:29
  100.1 22.5 %all-to-all-done.1 = bf16[16,152,448]{2,1,0:T(8,128)(2,1)} async-done(((bf16[16,152,448]{2,1,0:T(8,128)(2,1)}), bf16[16,152,448]{2,1,0:T(8,128)(2,1)}, u32[]{:S(2)}, u32[]{:S(2)}) %all-to-all-start.1) | async-done | bytes 2179104 | tf_op jit(solution)/shard_map/all_to_all | solution.py:71
  122.6 2.1 convert_reduce_fusion
  125.6 8.1 %collective-permute-start.2 = (bf16[448,1216]{1,0:T(8,128)(2,1)}, bf16[448,1216]{1,0:T(8,128)(2,1)}, u32[]{:S(2)}, u32[]{:S(2)}) collective-permute-start(bf16[448,1216]{1,0:T(8,128)(2,1)} %bitcast.12), channel_id=1, source_target_pairs={{0,16},{16,0},{1,17},{17,1},{2,18},{18,2},{3,19},{19,3},{4,20},{20... | collective-permute-start | bytes 3268616 | tf_op jit(solution)/shard_map/ppermute | solution.py:28
  133.6 2.4 copy.22
  136.0 1.4 reshape.57
  137.5 2.4 copy.23
  139.9 2.3 reshape.58
  142.2 3.5 %pad_maximum_fusion.1 = bf16[16,152,448]{2,1,0:T(8,128)(2,1)} fusion(bf16[16,76,448]{2,1,0:T(8,128)(2,1)} %reshape.58, bf16[16,76,448]{2,1,0:T(8,128)(2,1)S(1)} %reshape.57), kind=kLoop, calls=%fused_computation.7 | loop fusion | flops 4358144 | bytes 4358144 | tf_op jit(solution)/shard_map/concatenate | solution.py:56
  145.7 47.4 %all-gather.2.cloned.1.call-done = bf16[2432,448]{1,0:T(8,128)(2,1)} async-done(((bf16[152,448]{1,0:T(8,128)(2,1)}), bf16[2432,448]{1,0:T(8,128)(2,1)}) %all-gather.2.cloned.1.call-update) | async-done | bytes 2179088 | tf_op jit(solution)/shard_map/all_gather | solution.py:76
  193.1 2.8 %fusion.17 = bf16[192,448]{1,0:T(8,128)(2,1)S(1)} fusion(bf16[2432,448]{1,0:T(8,128)(2,1)} %bitcast.29, bf16[2432,448]{1,0:T(8,128)(2,1)} %all-gather.2.cloned.1.call-done), kind=kOutput, calls=%fused_computation.16 | convolution fusion | flops 418467840 | bytes 3907584 | tf_op jit(solution)/shard_map/dot_general | solution.py:78
  196.0 61.2 %all_to_all.15 = bf16[32,6,448]{2,1,0:T(8,128)(2,1)S(1)} all-to-all(bf16[32,6,448]{2,1,0:T(8,128)(2,1)S(1)} %reshape.60), channel_id=1, replica_groups=mesh['z'=32,'c'=2,'t'=16] {'z'}, dimensions={0} | all-to-all | bytes 344064 | tf_op jit(solution)/shard_map/all_to_all | solution.py:81
  257.6 3.7 %fusion.14 = bf16[256,448]{0,1:T(8,128)(2,1)} fusion(f32[256,448]{0,1:T(8,128)S(1)} %fusion.29, bf16[448,2432]{1,0:T(8,128)(2,1)} %param.13, bf16[2432,448]{1,0:T(8,128)(2,1)} %all-gather.2.cloned.1.call-done), kind=kOutput, calls=%fused_computation.15 | convolution fusion | flops 558071808 | bytes 4112384 | tf_op jit(solution)/shard_map/dot_general | solution.py:84
  (32 shorter events, 7.6 us)
Async XLA Ops:
  6.5 39.2 %copy-start = (bf16[2432,448]{0,1:T(8,128)(2,1)S(1)}, bf16[2432,448]{0,1:T(8,128)(2,1)}, u32[]{:S(2)}) copy-start(bf16[2432,448]{0,1:T(8,128)(2,1)} %param.12) | copy-start | bytes 6537220
  10.4 70.0 %all-to-all-start = ((bf16[32,6,448]{2,1,0:T(8,128)(2,1)}), bf16[32,6,448]{2,1,0:T(8,128)(2,1)}, u32[]{:S(2)}, u32[]{:S(2)}) async-start(bf16[32,6,448]{2,1,0:T(8,128)(2,1)} %reshape.53), calls=%async_computation | async-start | bytes 524288 | tf_op jit(solution)/shard_map/all_to_all | solution.py:51
  39.9 8.8 %collective-permute-start = (bf16[1216,448]{0,1:T(8,128)(2,1)}, bf16[1216,448]{0,1:T(8,128)(2,1)}, u32[]{:S(2)}, u32[]{:S(2)}) collective-permute-start(bf16[1216,448]{0,1:T(8,128)(2,1)} %bitcast.31), channel_id=1, source_target_pairs={{0,16},{16,0},{1,17},{17,1},{2,18},{18,2},{3,19},{19,3},{4,20},{20... | collective-permute-start | bytes 3268616 | tf_op jit(solution)/shard_map/ppermute | solution.py:27
  81.5 2.7 copy-start.1
  86.6 7.0 %copy-start.3 = (bf16[1,384,76]{1,2,0:T(8,128)(2,1)S(1)}, bf16[1,384,76]{1,2,0:T(8,128)(2,1)}, u32[]{:S(2)}) copy-start(bf16[1,384,76]{1,2,0:T(8,128)(2,1)} %param.17) | copy-start | bytes 175108
  86.6 36.0 %all-to-all-start.1 = ((bf16[16,152,448]{2,1,0:T(8,128)(2,1)}), bf16[16,152,448]{2,1,0:T(8,128)(2,1)}, u32[]{:S(2)}, u32[]{:S(2)}) async-start(bf16[16,152,448]{2,1,0:T(8,128)(2,1)} %pad_maximum_fusion), calls=%async_computation.1 | async-start | bytes 4980736 | tf_op jit(solution)/shard_map/all_to_all | solution.py:71
  93.6 99.5 %all-gather.2.cloned.1.call-start = ((), (), s32[]{:S(2)}) async-start(), calls=%async_computation.3 | async-start | bytes 2646016 | tf_op jit(solution)/shard_map/all_gather | solution.py:76
  93.6 6.0 %collective-permute-start.1 = (bf16[384,76]{0,1:T(8,128)(2,1)S(1)}, bf16[384,76]{0,1:T(8,128)(2,1)S(1)}, u32[]{:S(2)}, u32[]{:S(2)}) collective-permute-start(bf16[384,76]{0,1:T(8,128)(2,1)S(1)} %bitcast.33), channel_id=1, source_target_pairs={{0,16},{16,0},{1,17},{17,1},{2,18},{18,2},{3,19},{19,3},{4,20},{20... | collective-permute-start | bytes 175112 | tf_op jit(solution)/shard_map/ppermute | solution.py:29
  99.6 25.1 %copy-start.2 = (bf16[256,152]{0,1:T(8,128)(2,1)S(1)}, bf16[256,152]{0,1:T(8,128)(2,1)}, u32[]{:S(2)}) copy-start(bf16[256,152]{0,1:T(8,128)(2,1)} %param.14) | copy-start | bytes 233476
  125.6 11.9 %collective-permute-start.2 = (bf16[448,1216]{1,0:T(8,128)(2,1)}, bf16[448,1216]{1,0:T(8,128)(2,1)}, u32[]{:S(2)}, u32[]{:S(2)}) collective-permute-start(bf16[448,1216]{1,0:T(8,128)(2,1)} %bitcast.12), channel_id=1, source_target_pairs={{0,16},{16,0},{1,17},{17,1},{2,18},{18,2},{3,19},{19,3},{4,20},{20... | collective-permute-start | bytes 3268616 | tf_op jit(solution)/shard_map/ppermute | solution.py:28
Sparse Core Ops, SparseCore 0:
  125.7 67.3 all-gather.1

commit v2 on v0

v2 whole, which is shorter than its diff:
```python
import jax
import jax.numpy as jnp
from jax import lax
from jax.experimental import pallas as pl
from jax.experimental.pallas import tpu as pltpu
from jax.sharding import Mesh, PartitionSpec as P

CAP = 6
LANES = 128
F32 = jnp.float32
BF16 = jnp.bfloat16


def call(kernel, outs, *operands, flops=0):
    size = sum(v.size * v.dtype.itemsize for v in operands)
    return pl.pallas_call(
        kernel,
        out_shape=outs,
        compiler_params=pltpu.CompilerParams(vmem_limit_bytes=40 * 1024 * 1024),
        cost_estimate=pl.CostEstimate(flops=flops, bytes_accessed=size, transcendentals=0),
    )(*operands)


def dot(left, right, left_dim, right_dim):
    return lax.dot_general(
        left, right, (((left_dim,), (right_dim,)), ((), ())), preferred_element_type=F32
    )


def iota(shape, dim):
    return lax.broadcasted_iota(jnp.int32, shape, dim)


def packed(blocks, last):
    rows = last.shape[0]
    place = iota(last.shape, 0) & 7
    groups = [
        jnp.where(place >= CAP, pltpu.roll(last, CAP - 2 * j, 0), block).reshape(
            rows // 8, 8, LANES
        )
        for j, block in enumerate(blocks)
    ]
    return jnp.concatenate(groups, axis=1).astype(BF16)


def unpacked(message):
    wide = message.astype(F32)
    rows = wide.shape[0] * 8
    blocks = [wide[:, 8 * j : 8 * j + 8, :].reshape(rows, LANES) for j in range(3)]
    place = iota((rows, LANES), 0) & 7
    moved = [pltpu.roll(block, rows - CAP + 2 * j, 0) for j, block in enumerate(blocks)]
    last = jnp.where(place < 2, moved[0], jnp.where(place < 4, moved[1], moved[2]))
    last = jnp.where(iota((rows, LANES), 1) >= LANES // 2, last, 0.0)
    return [v.astype(BF16) for v in blocks + [last]]


def dispatch_kernel(routes, gates, grads_t, message, chooser):
    held = message.shape[0]
    tokens = routes.shape[1]
    ids = routes[...]
    experts = iota((held, tokens), 0)
    first, second = ids[0:1] == experts, ids[1:2] == experts
    named = jnp.where(first | second, 1.0, 0.0).astype(BF16)
    before = jnp.where(
        iota((tokens, tokens), 0) < iota((tokens, tokens), 1), 1.0, 0.0
    ).astype(BF16)
    place = experts * 8 + dot(named, before, 1, 0).astype(jnp.int32) + 1
    row = iota((held * 8, tokens), 0) + 1
    hit_first = jnp.sum(jnp.where(first, place, 0), axis=0, keepdims=True) == row
    hit_second = jnp.sum(jnp.where(second, place, 0), axis=0, keepdims=True) == row
    weight = gates[...]
    gate = jnp.sum(
        jnp.where(hit_first, weight[0:1], 0.0) + jnp.where(hit_second, weight[1:2], 0.0),
        axis=1,
        keepdims=True,
    )
    chosen = jnp.where(hit_first | hit_second, 1.0, 0.0).astype(BF16)
    chooser[...] = chosen
    width = grads_t.shape[0]
    rows = dot(chosen, grads_t[...], 1, 1)
    tail = dot(chosen, grads_t[width - LANES :, :], 1, 1) * gate
    message[...] = packed(
        [rows[:, LANES * j : LANES * (j + 1)] * gate for j in range(3)], tail
    )


def down_kernel(arrived, down_t, mid):
    cores, held = arrived.shape[0], arrived.shape[1]
    blocks = unpacked(arrived[...].reshape(cores * held, 3 * 8, LANES))
    slots, rows = cores * held * CAP, cores * held * 8
    row = iota((slots, rows), 1)
    core = jnp.where(row >= held * 8, 1, 0)
    block = ((row - core * held * 8) >> 3) * 2 + core
    pick = ((row & 7) < CAP) & (block * CAP + (row & 7) == iota((slots, rows), 0))
    pick = jnp.where(pick, 1.0, 0.0).astype(BF16)
    picked = dot(pick, jnp.concatenate(blocks, axis=1), 1, 0).astype(BF16)
    width = down_t.shape[0]
    weights = jnp.concatenate([down_t[: 3 * LANES, :], down_t[width - LANES :, :]], axis=0)
    total = dot(weights, picked, 0, 1)
    piece = mid.shape[1]
    for part in range(mid.shape[0]):
        mid[part] = total[piece * part : piece * (part + 1)].astype(BF16)


def gate_kernel(shares, act, copies):
    total = shares[0].astype(F32)
    for part in range(1, shares.shape[0]):
        total = total + shares[part].astype(F32)
    value = act[...].astype(F32)
    hidden = (total * (value / (1.0 + jnp.exp(-value)))).astype(BF16)
    for part in range(copies.shape[0]):
        copies[part] = hidden


def up_kernel(full, up, rows_t, stacked):
    piece = full.shape[1]
    for part in range(full.shape[0]):
        stacked[piece * part : piece * (part + 1), :] = full[part].astype(F32)
    rows_t[...] = dot(up[...], stacked[...].astype(BF16), 1, 0).astype(BF16)


def return_kernel(core_id, halves, message):
    held = message.shape[0]
    slots = halves.shape[2]
    core = core_id[0]
    both = (halves[0].astype(F32) + halves[1].astype(F32)).astype(BF16)
    row = iota((held * 8, slots), 0)
    slot = ((row >> 3) * 2 + core) * CAP + (row & 7)
    pick = ((row & 7) < CAP) & (slot == iota((held * 8, slots), 1))
    pick = jnp.where(pick, 1.0, 0.0).astype(BF16)
    width = both.shape[0]
    rows = dot(pick, both, 1, 1)
    message[...] = packed(
        [rows[:, LANES * j : LANES * (j + 1)] for j in range(3)],
        dot(pick, both[width - LANES :], 1, 1),
    )


def combine_kernel(returned, chooser, dense_t, out_t):
    blocks = unpacked(returned[...])
    chosen = chooser[...]
    width = out_t.shape[0]
    for j in range(3):
        low = LANES * j
        out_t[low : low + LANES, :] = (
            dense_t[low : low + LANES, :] + dot(blocks[j], chosen, 0, 0)
        ).astype(BF16)
    half = LANES // 2
    out_t[3 * LANES :, :] = (
        dense_t[3 * LANES :, :] + dot(blocks[3], chosen, 0, 0)[half:]
    ).astype(BF16)


def turn(axis, step):
    size = lax.axis_size(axis)
    return [(i, (i + step) % size) for i in range(size)]


def scattered(blocks, axis):
    size, me = lax.axis_size(axis), lax.axis_index(axis)
    total = lax.dynamic_index_in_dim(blocks, me, 0, keepdims=False).astype(F32)
    for step in range(1, size):
        block = lax.dynamic_index_in_dim(blocks, (me + step) % size, 0, keepdims=False)
        total = total + lax.ppermute(block, axis, turn(axis, step)).astype(F32)
    return total


def gathered(block, axis):
    size, me = lax.axis_size(axis), lax.axis_index(axis)
    out = jnp.zeros((size,) + block.shape, block.dtype)
    for step in range(size):
        piece = lax.ppermute(block, axis, turn(axis, step)) if step else block
        out = lax.dynamic_update_index_in_dim(out, piece, (me - step) % size, 0)
    return out


def shards(
    grads, routes, gates, dense_down, dense_up, dense_act, expert_down, expert_up, expert_act
):
    held = lax.axis_size("z")
    across, along = lax.axis_size("x"), lax.axis_size("y")
    parts = across * along
    tokens, width = grads.shape
    half = expert_down.shape[1]
    piece, share = half // parts, dense_act.shape[1]
    slots = expert_act.shape[1]
    tensor = ("x", "y")

    message, chooser = call(
        dispatch_kernel,
        (
            jax.ShapeDtypeStruct((held, 24, LANES), BF16),
            jax.ShapeDtypeStruct((held * 8, tokens), BF16),
        ),
        routes.T,
        gates.T,
        grads.T,
    )
    arrived = lax.all_to_all(message, "z", 0, 0, tiled=True)

    dense_mid = dot(dense_down, grads, 1, 1).astype(BF16)
    dense_mid = dense_mid.reshape(across, along, share, tokens)
    dense_share = scattered(scattered(dense_mid, "x").astype(BF16), "y")

    mid = call(
        down_kernel,
        jax.ShapeDtypeStruct((parts, piece, slots), BF16),
        lax.all_gather(arrived, "c", axis=0, tiled=False),
        expert_down[0].T,
    )
    shares = lax.all_to_all(mid, tensor, 0, 0, tiled=True)
    copies = call(
        gate_kernel,
        jax.ShapeDtypeStruct((parts, piece, slots), BF16),
        shares,
        expert_act[0].T,
    )
    full = lax.all_to_all(copies, tensor, 0, 0, tiled=True)
    size = full.size * 2 + expert_up.size * 2
    rows_t = pl.pallas_call(
        up_kernel,
        out_shape=jax.ShapeDtypeStruct((width, slots), BF16),
        scratch_shapes=[pltpu.VMEM((half, slots), F32)],
        compiler_params=pltpu.CompilerParams(vmem_limit_bytes=40 * 1024 * 1024),
        cost_estimate=pl.CostEstimate(flops=0, bytes_accessed=size, transcendentals=0),
    )(full, expert_up[0])
    back = pl.pallas_call(
        return_kernel,
        out_shape=jax.ShapeDtypeStruct((held, 24, LANES), BF16),
        in_specs=[
            pl.BlockSpec(memory_space=pltpu.SMEM),
            pl.BlockSpec(memory_space=pltpu.VMEM),
        ],
        compiler_params=pltpu.CompilerParams(vmem_limit_bytes=40 * 1024 * 1024),
    )(
        lax.axis_index("c").astype(jnp.int32).reshape(1),
        lax.all_gather(rows_t, "c", axis=0, tiled=False),
    )
    returned = lax.all_to_all(back, "z", 0, 0, tiled=True)

    value = dense_act.T.astype(F32)
    dense_hidden = (dense_share * jax.nn.silu(value)).astype(BF16)
    dense_full = gathered(gathered(dense_hidden, "y"), "x").reshape(parts * share, tokens)
    dense_t = dot(dense_up, dense_full, 1, 0)
    out_t = call(
        combine_kernel, jax.ShapeDtypeStruct((width, tokens), BF16), returned, chooser, dense_t
    )
    return out_t.T


def solution(mesh):
    groups, parts = mesh.devices.shape
    across = 4 if parts == 16 else 2
    split = Mesh(
        mesh.devices.reshape(groups // 2, 2, across, parts // across), ("z", "c", "x", "y")
    )
    blocks, tensor = ("z", "c"), ("x", "y")
    placed = (
        P(blocks, tensor),
        P(blocks, None),
        P(blocks, None),
        P(None, tensor),
        P(tensor, None),
        P(blocks, tensor),
        P(blocks, None, tensor),
        P(blocks, tensor, None),
        P(blocks, None, tensor),
    )
    return jax.shard_map(
        shards, mesh=split, in_specs=placed, out_specs=P(blocks, tensor), check_vma=False
    )
```

time: 341 us -> 199 us (0.58)
  blocking collectives: 79.3 us -> 8.22 us
  waiting for transfers between devices: 140 us -> 78.7 us
  between operations: 14.4 us -> 0.52 us
  starting transfers between devices: 77.8 us -> 87.3 us
  matrix products: 10.6 us -> 1.66 us
  Pallas kernels: 0 us -> 5.33 us
    all_to_all x2 -> x4, waiting for transfers between devices: 124 us -> 49.5 us  [the longest x1 35.4 us: shards(): arrived = lax.all_to_all(message, 'z', 0, 0, tiled=True)]
    unnamed x1 -> x0, blocking collectives: 59.2 us -> none
    ppermute x0 -> x12, starting transfers between devices: none -> 41.4 us  [the longest x6 21.4 us: scattered(): total = total + lax.ppermute(block, axis, turn(axis, step)).astype(F32)]
    ppermute x0 -> x12, waiting for transfers between devices: none -> 29.2 us  [the longest x6 19.1 us: scattered(): total = total + lax.ppermute(block, axis, turn(axis, step)).astype(F32)]
    all_to_all x2 -> x4, starting transfers between devices: 66.3 us -> 45.9 us  [the longest x1 29.4 us: shards(): arrived = lax.all_to_all(message, 'z', 0, 0, tiled=True)]
    all_gather x1 -> x0, waiting for transfers between devices: 16.5 us -> none  [shards(): lax.all_gather(dense_half, 'tensor', axis=1, tiled=True)]
    all_gather x1 -> x2, blocking collectives: 20.2 us -> 8.22 us  [the longest x1 4.32 us: shards(): lax.all_gather(arrived, 'c', axis=0, tiled=False)]
    unnamed x5 -> x0, starting transfers between devices: 11.4 us -> none
  transfers between devices with their start and end apart: 8 -> 16, of which waited for: 3 -> 9; matrix products, arithmetic and copies ran while one was open for 22% -> 6% of each run, Pallas kernels for 0% -> 1%
where the time goes in v2:
time: 199 us; the launch traced here: 198 us
  starting transfers between devices  87.3 us (44%)
  waiting for transfers between devices  78.7 us (40%)
  local copies, waits for them, and re-layouts  12.6 us (6%)
  blocking collectives  8.22 us (4%)
  Pallas kernels  5.33 us (3%)
  other arithmetic  3.87 us (2%)
    all_to_all x1, waiting for transfers between devices, shards(): arrived = lax.all_to_all(message, 'z', 0, 0, tiled=True)  35.4 us
    all_to_all x1, starting transfers between devices, shards(): arrived = lax.all_to_all(message, 'z', 0, 0, tiled=True)  29.4 us
    ppermute x6, starting transfers between devices, scattered(): total = total + lax.ppermute(block, axis, turn(axis, step)).astype(F32)  21.4 us
    ppermute x6, starting transfers between devices, gathered(): piece = lax.ppermute(block, axis, turn(axis, step)) if step else block  19.9 us
    ppermute x6, waiting for transfers between devices, scattered(): total = total + lax.ppermute(block, axis, turn(axis, step)).astype(F32)  19.1 us
    all_to_all x1, waiting for transfers between devices, shards(): returned = lax.all_to_all(back, 'z', 0, 0, tiled=True)  14.1 us
    ppermute x6, waiting for transfers between devices, gathered(): piece = lax.ppermute(block, axis, turn(axis, step)) if step else block  10.1 us
    all_to_all x1, starting transfers between devices, shards(): shares = lax.all_to_all(mid, tensor, 0, 0, tiled=True)  6.89 us
  transfers between devices with their start and end apart: 16, of which 9 were waited for; matrix products, arithmetic and copies ran while one was open for 6% of the time, Pallas kernels for 1%

profile of v2, /device:TPU:1, one launch (start us, length us, event | category | flops | bytes accessed | tf_op | source)
XLA Modules:
  0.0 198.2 jit_solution(9569021778333526100)
XLA Ops:
  3.6 29.4 %all-to-all-start = ((bf16[32,24,128]{2,1,0:T(8,128)(2,1)}), bf16[32,24,128]{2,1,0:T(8,128)(2,1)}, u32[]{:S(2)}, u32[]{:S(2)}) async-start(bf16[32,24,128]{2,1,0:T(8,128)(2,1)} %get-tuple-element.7), calls=%async_computation | async-start | bytes 393216 | tf_op jit(solution)/shard_map/all_to_all | solution.py:199
  33.1 35.4 %all-to-all-done = bf16[32,24,128]{2,1,0:T(8,128)(2,1)} async-done(((bf16[32,24,128]{2,1,0:T(8,128)(2,1)}), bf16[32,24,128]{2,1,0:T(8,128)(2,1)}, u32[]{:S(2)}, u32[]{:S(2)}) %all-to-all-start) | async-done | bytes 196640 | tf_op jit(solution)/shard_map/all_to_all | solution.py:199
  68.5 4.3 %all-gather = bf16[64,24,128]{2,1,0:T(8,128)(2,1)S(1)} all-gather(bf16[32,24,128]{2,1,0:T(8,128)(2,1)} %all-to-all-done), channel_id=2, replica_groups=mesh['z'=32,'c'=2,'x'=4,'y'=4] {'c'}, dimensions={0}, use_global_device_ids=true | all-gather | bytes 589824 | tf_op jit(solution)/shard_map/all_gather | solution.py:208
  75.0 6.9 %all-to-all-start.1 = ((bf16[16,76,384]{2,1,0:T(8,128)(2,1)}), bf16[16,76,384]{2,1,0:T(8,128)(2,1)S(1)}, u32[]{:S(2)}, u32[]{:S(2)}) async-start(bf16[16,76,384]{2,1,0:T(8,128)(2,1)} %copy-done.2), calls=%async_computation.1 | async-start | bytes 1966080 | tf_op jit(solution)/shard_map/all_to_all | solution.py:211
  84.8 3.4 %collective-permute-start = (bf16[4,152,256]{2,1,0:T(8,128)(2,1)}, bf16[4,152,256]{2,1,0:T(8,128)(2,1)}, u32[]{:S(2)}, u32[]{:S(2)}) collective-permute-start(bf16[4,152,256]{2,1,0:T(8,128)(2,1)} %get-tuple-element.11), channel_id=1, source_target_pairs={{0,4},{4,8},{8,12},{12,0},{1,5},{5,9},{9,13},{13,1},{2,6},{6,10},{... | collective-permute-start | bytes 933896 | tf_op jit(solution)/shard_map/ppermute | solution.py:164
  88.2 4.3 %collective-permute-start.1 = (bf16[4,152,256]{2,1,0:T(8,128)(2,1)}, bf16[4,152,256]{2,1,0:T(8,128)(2,1)}, u32[]{:S(2)}, u32[]{:S(2)}) collective-permute-start(bf16[4,152,256]{2,1,0:T(8,128)(2,1)} %get-tuple-element.13), channel_id=1, source_target_pairs={{0,8},{4,12},{8,0},{12,4},{1,9},{5,13},{9,1},{13,5},{2,10},{6,14},... | collective-permute-start | bytes 933896 | tf_op jit(solution)/shard_map/ppermute | solution.py:164
  92.5 3.1 %collective-permute-start.2 = (bf16[4,152,256]{2,1,0:T(8,128)(2,1)}, bf16[4,152,256]{2,1,0:T(8,128)(2,1)}, u32[]{:S(2)}, u32[]{:S(2)}) collective-permute-start(bf16[4,152,256]{2,1,0:T(8,128)(2,1)} %get-tuple-element.12), channel_id=1, source_target_pairs={{0,12},{4,0},{8,4},{12,8},{1,13},{5,1},{9,5},{13,9},{2,14},{6,2},{... | collective-permute-start | bytes 933896 | tf_op jit(solution)/shard_map/ppermute | solution.py:164
  95.7 6.4 %collective-permute-done = bf16[4,152,256]{2,1,0:T(8,128)(2,1)} collective-permute-done((bf16[4,152,256]{2,1,0:T(8,128)(2,1)}, bf16[4,152,256]{2,1,0:T(8,128)(2,1)}, u32[]{:S(2)}, u32[]{:S(2)}) %collective-permute-start) | collective-permute-done | bytes 311328 | tf_op jit(solution)/shard_map/ppermute | solution.py:164
  102.1 7.0 %collective-permute-done.1 = bf16[4,152,256]{2,1,0:T(8,128)(2,1)} collective-permute-done((bf16[4,152,256]{2,1,0:T(8,128)(2,1)}, bf16[4,152,256]{2,1,0:T(8,128)(2,1)}, u32[]{:S(2)}, u32[]{:S(2)}) %collective-permute-start.1) | collective-permute-done | bytes 311328 | tf_op jit(solution)/shard_map/ppermute | solution.py:164
  112.3 5.8 %all-to-all-start.2 = ((bf16[16,76,384]{2,1,0:T(8,128)(2,1)}), bf16[16,76,384]{2,1,0:T(8,128)(2,1)S(1)}, u32[]{:S(2)}, u32[]{:S(2)}) async-start(bf16[16,76,384]{2,1,0:T(8,128)(2,1)} %copy-done.1), calls=%async_computation.2 | async-start | bytes 1966080 | tf_op jit(solution)/shard_map/all_to_all | solution.py:218
  119.1 3.3 %collective-permute-start.3 = (bf16[152,256]{1,0:T(8,128)(2,1)S(1)}, bf16[152,256]{1,0:T(8,128)(2,1)}, u32[]{:S(2)}, u32[]{:S(2)}) collective-permute-start(bf16[152,256]{1,0:T(8,128)(2,1)S(1)} %get-tuple-element.14), channel_id=1, source_target_pairs={{0,1},{1,2},{2,3},{3,0},{4,5},{5,6},{6,7},{7,4},{8,9},{9,10},{10,1... | collective-permute-start | bytes 233480 | tf_op jit(solution)/shard_map/ppermute | solution.py:164
  122.4 4.3 %collective-permute-start.4 = (bf16[152,256]{1,0:T(8,128)(2,1)S(1)}, bf16[152,256]{1,0:T(8,128)(2,1)}, u32[]{:S(2)}, u32[]{:S(2)}) collective-permute-start(bf16[152,256]{1,0:T(8,128)(2,1)S(1)} %get-tuple-element.16), channel_id=1, source_target_pairs={{0,2},{1,3},{2,0},{3,1},{4,6},{5,7},{6,4},{7,5},{8,10},{9,11},{10,... | collective-permute-start | bytes 233480 | tf_op jit(solution)/shard_map/ppermute | solution.py:164
  126.7 3.1 %collective-permute-start.5 = (bf16[152,256]{1,0:T(8,128)(2,1)S(1)}, bf16[152,256]{1,0:T(8,128)(2,1)}, u32[]{:S(2)}, u32[]{:S(2)}) collective-permute-start(bf16[152,256]{1,0:T(8,128)(2,1)S(1)} %get-tuple-element.15), channel_id=1, source_target_pairs={{0,3},{1,0},{2,1},{3,2},{4,7},{5,4},{6,5},{7,6},{8,11},{9,8},{10,9... | collective-permute-start | bytes 233480 | tf_op jit(solution)/shard_map/ppermute | solution.py:164
  129.8 5.2 %collective-permute-done.3 = bf16[152,256]{1,0:T(8,128)(2,1)} collective-permute-done((bf16[152,256]{1,0:T(8,128)(2,1)S(1)}, bf16[152,256]{1,0:T(8,128)(2,1)}, u32[]{:S(2)}, u32[]{:S(2)}) %collective-permute-start.3) | collective-permute-done | bytes 77856 | tf_op jit(solution)/shard_map/ppermute | solution.py:164
  138.0 3.7 %collective-permute-start.6 = (bf16[152,256]{1,0:T(8,128)(2,1)S(1)}, bf16[152,256]{1,0:T(8,128)(2,1)S(1)}, u32[]{:S(2)}, u32[]{:S(2)}) collective-permute-start(bf16[152,256]{1,0:T(8,128)(2,1)S(1)} %get-tuple-element.10), channel_id=1, source_target_pairs={{0,1},{1,2},{2,3},{3,0},{4,5},{5,6},{6,7},{7,4},{8,9},{9,10},{10,1... | collective-permute-start | bytes 233480 | tf_op jit(solution)/shard_map/ppermute | solution.py:172
  141.8 4.2 %collective-permute-start.7 = (bf16[152,256]{1,0:T(8,128)(2,1)S(1)}, bf16[152,256]{1,0:T(8,128)(2,1)S(1)}, u32[]{:S(2)}, u32[]{:S(2)}) collective-permute-start(bf16[152,256]{1,0:T(8,128)(2,1)S(1)} %get-tuple-element.10), channel_id=1, source_target_pairs={{0,2},{1,3},{2,0},{3,1},{4,6},{5,7},{6,4},{7,5},{8,10},{9,11},{10,... | collective-permute-start | bytes 233480 | tf_op jit(solution)/shard_map/ppermute | solution.py:172
  146.0 2.6 %collective-permute-start.8 = (bf16[152,256]{1,0:T(8,128)(2,1)S(1)}, bf16[152,256]{1,0:T(8,128)(2,1)S(1)}, u32[]{:S(2)}, u32[]{:S(2)}) collective-permute-start(bf16[152,256]{1,0:T(8,128)(2,1)S(1)} %get-tuple-element.10), channel_id=1, source_target_pairs={{0,3},{1,0},{2,1},{3,2},{4,7},{5,4},{6,5},{7,6},{8,11},{9,8},{10,9... | collective-permute-start | bytes 233480 | tf_op jit(solution)/shard_map/ppermute | solution.py:172
  151.9 3.9 %all-gather.1 = bf16[896,384]{1,0:T(8,128)(2,1)S(1)} all-gather(bf16[448,384]{1,0:T(8,128)(2,1)S(1)} %shard_map.94), channel_id=3, replica_groups=mesh['z'=32,'c'=2,'x'=4,'y'=4] {'c'}, dimensions={0}, use_global_device_ids=true | all-gather | bytes 1032192 | tf_op jit(solution)/shard_map/all_gather | solution.py:237
  156.9 3.9 %all-to-all-start.3 = ((bf16[32,24,128]{2,1,0:T(8,128)(2,1)}), bf16[32,24,128]{2,1,0:T(8,128)(2,1)S(1)}, u32[]{:S(2)}, u32[]{:S(2)}) async-start(bf16[32,24,128]{2,1,0:T(8,128)(2,1)} %shard_map.95), calls=%async_computation.3 | async-start | bytes 393216 | tf_op jit(solution)/shard_map/all_to_all | solution.py:239
  163.7 4.0 %collective-permute-start.10 = (bf16[4,152,256]{2,1,0:T(8,128)(2,1)}, bf16[4,152,256]{2,1,0:T(8,128)(2,1)S(1)}, u32[]{:S(2)}, u32[]{:S(2)}) collective-permute-start(bf16[4,152,256]{2,1,0:T(8,128)(2,1)} %bitcast_dynamic-update-slice_fusion.4), channel_id=1, source_target_pairs={{0,8},{4,12},{8,0},{12,4},{1,9},{5,13},{9,1},{13,5},{2,10},{6,14},... | collective-permute-start | bytes 933896 | tf_op jit(solution)/shard_map/ppermute | solution.py:172
  167.7 3.2 %collective-permute-start.11 = (bf16[4,152,256]{2,1,0:T(8,128)(2,1)}, bf16[4,152,256]{2,1,0:T(8,128)(2,1)S(1)}, u32[]{:S(2)}, u32[]{:S(2)}) collective-permute-start(bf16[4,152,256]{2,1,0:T(8,128)(2,1)} %bitcast_dynamic-update-slice_fusion.4), channel_id=1, source_target_pairs={{0,12},{4,0},{8,4},{12,8},{1,13},{5,1},{9,5},{13,9},{2,14},{6,2},{... | collective-permute-start | bytes 933896 | tf_op jit(solution)/shard_map/ppermute | solution.py:172
  173.6 6.2 %collective-permute-done.10 = bf16[4,152,256]{2,1,0:T(8,128)(2,1)S(1)} collective-permute-done((bf16[4,152,256]{2,1,0:T(8,128)(2,1)}, bf16[4,152,256]{2,1,0:T(8,128)(2,1)S(1)}, u32[]{:S(2)}, u32[]{:S(2)}) %collective-permute-start.10) | collective-permute-done | bytes 311328 | tf_op jit(solution)/shard_map/ppermute | solution.py:172
  179.8 2.6 %collective-permute-done.11 = bf16[4,152,256]{2,1,0:T(8,128)(2,1)S(1)} collective-permute-done((bf16[4,152,256]{2,1,0:T(8,128)(2,1)}, bf16[4,152,256]{2,1,0:T(8,128)(2,1)S(1)}, u32[]{:S(2)}, u32[]{:S(2)}) %collective-permute-start.11) | collective-permute-done | bytes 311328 | tf_op jit(solution)/shard_map/ppermute | solution.py:172
  183.1 14.1 %all-to-all-done.3.returned = bf16[32,24,128]{2,1,0:T(8,128)(2,1)S(1)} async-done(((bf16[32,24,128]{2,1,0:T(8,128)(2,1)}), bf16[32,24,128]{2,1,0:T(8,128)(2,1)S(1)}, u32[]{:S(2)}, u32[]{:S(2)}) %all-to-all-start.3) | async-done | bytes 196640 | tf_op jit(solution)/shard_map/all_to_all | solution.py:239
  (55 shorter events, 27.6 us)
Async XLA Ops:
  0.0 81.9 %copy-start = (bf16[2432,448]{0,1:T(8,128)(2,1)S(1)}, bf16[2432,448]{0,1:T(8,128)(2,1)}, u32[]{:S(2)}) copy-start(bf16[2432,448]{0,1:T(8,128)(2,1)} %param.12) | copy-start | bytes 6537220
  0.0 72.8 %copy-start.3 = (bf16[1,1216,448]{1,2,0:T(8,128)(2,1)S(1)}, bf16[1,1216,448]{1,2,0:T(8,128)(2,1)}, u32[]{:S(2)}) copy-start(bf16[1,1216,448]{1,2,0:T(8,128)(2,1)} %param.15) | copy-start | bytes 3268612
  0.0 1.1 copy-start.5
  3.6 64.8 %all-to-all-start = ((bf16[32,24,128]{2,1,0:T(8,128)(2,1)}), bf16[32,24,128]{2,1,0:T(8,128)(2,1)}, u32[]{:S(2)}, u32[]{:S(2)}) async-start(bf16[32,24,128]{2,1,0:T(8,128)(2,1)} %get-tuple-element.7), calls=%async_computation | async-start | bytes 393216 | tf_op jit(solution)/shard_map/all_to_all | solution.py:199
  75.0 6.9 %copy-start.6 = (bf16[256,448]{0,1:T(8,128)(2,1)S(1)}, bf16[256,448]{0,1:T(8,128)(2,1)}, u32[]{:S(2)}) copy-start(bf16[256,448]{0,1:T(8,128)(2,1)} %param.9) | copy-start | bytes 688132
  75.0 36.2 %all-to-all-start.1 = ((bf16[16,76,384]{2,1,0:T(8,128)(2,1)}), bf16[16,76,384]{2,1,0:T(8,128)(2,1)S(1)}, u32[]{:S(2)}, u32[]{:S(2)}) async-start(bf16[16,76,384]{2,1,0:T(8,128)(2,1)} %copy-done.2), calls=%async_computation.1 | async-start | bytes 1966080 | tf_op jit(solution)/shard_map/all_to_all | solution.py:211
  82.8 1.1 copy-start.10
  84.8 26.3 %copy-start.7 = (bf16[1,384,76]{1,2,0:T(8,128)(2,1)S(1)}, bf16[1,384,76]{1,2,0:T(8,128)(2,1)}, u32[]{:S(2)}) copy-start(bf16[1,384,76]{1,2,0:T(8,128)(2,1)} %param.17) | copy-start | bytes 175108
  84.8 17.2 %collective-permute-start = (bf16[4,152,256]{2,1,0:T(8,128)(2,1)}, bf16[4,152,256]{2,1,0:T(8,128)(2,1)}, u32[]{:S(2)}, u32[]{:S(2)}) collective-permute-start(bf16[4,152,256]{2,1,0:T(8,128)(2,1)} %get-tuple-element.11), channel_id=1, source_target_pairs={{0,4},{4,8},{8,12},{12,0},{1,5},{5,9},{9,13},{13,1},{2,6},{6,10},{... | collective-permute-start | bytes 933896 | tf_op jit(solution)/shard_map/ppermute | solution.py:164
  88.2 20.8 %collective-permute-start.1 = (bf16[4,152,256]{2,1,0:T(8,128)(2,1)}, bf16[4,152,256]{2,1,0:T(8,128)(2,1)}, u32[]{:S(2)}, u32[]{:S(2)}) collective-permute-start(bf16[4,152,256]{2,1,0:T(8,128)(2,1)} %get-tuple-element.13), channel_id=1, source_target_pairs={{0,8},{4,12},{8,0},{12,4},{1,9},{5,13},{9,1},{13,5},{2,10},{6,14},... | collective-permute-start | bytes 933896 | tf_op jit(solution)/shard_map/ppermute | solution.py:164
  92.5 16.5 %collective-permute-start.2 = (bf16[4,152,256]{2,1,0:T(8,128)(2,1)}, bf16[4,152,256]{2,1,0:T(8,128)(2,1)}, u32[]{:S(2)}, u32[]{:S(2)}) collective-permute-start(bf16[4,152,256]{2,1,0:T(8,128)(2,1)} %get-tuple-element.12), channel_id=1, source_target_pairs={{0,12},{4,0},{8,4},{12,8},{1,13},{5,1},{9,5},{13,9},{2,14},{6,2},{... | collective-permute-start | bytes 933896 | tf_op jit(solution)/shard_map/ppermute | solution.py:164
  112.3 37.6 %all-to-all-start.2 = ((bf16[16,76,384]{2,1,0:T(8,128)(2,1)}), bf16[16,76,384]{2,1,0:T(8,128)(2,1)S(1)}, u32[]{:S(2)}, u32[]{:S(2)}) async-start(bf16[16,76,384]{2,1,0:T(8,128)(2,1)} %copy-done.1), calls=%async_computation.2 | async-start | bytes 1966080 | tf_op jit(solution)/shard_map/all_to_all | solution.py:218
  119.1 15.9 %collective-permute-start.3 = (bf16[152,256]{1,0:T(8,128)(2,1)S(1)}, bf16[152,256]{1,0:T(8,128)(2,1)}, u32[]{:S(2)}, u32[]{:S(2)}) collective-permute-start(bf16[152,256]{1,0:T(8,128)(2,1)S(1)} %get-tuple-element.14), channel_id=1, source_target_pairs={{0,1},{1,2},{2,3},{3,0},{4,5},{5,6},{6,7},{7,4},{8,9},{9,10},{10,1... | collective-permute-start | bytes 233480 | tf_op jit(solution)/shard_map/ppermute | solution.py:164
  122.4 12.7 %collective-permute-start.4 = (bf16[152,256]{1,0:T(8,128)(2,1)S(1)}, bf16[152,256]{1,0:T(8,128)(2,1)}, u32[]{:S(2)}, u32[]{:S(2)}) collective-permute-start(bf16[152,256]{1,0:T(8,128)(2,1)S(1)} %get-tuple-element.16), channel_id=1, source_target_pairs={{0,2},{1,3},{2,0},{3,1},{4,6},{5,7},{6,4},{7,5},{8,10},{9,11},{10,... | collective-permute-start | bytes 233480 | tf_op jit(solution)/shard_map/ppermute | solution.py:164
  126.7 8.9 %collective-permute-start.5 = (bf16[152,256]{1,0:T(8,128)(2,1)S(1)}, bf16[152,256]{1,0:T(8,128)(2,1)}, u32[]{:S(2)}, u32[]{:S(2)}) collective-permute-start(bf16[152,256]{1,0:T(8,128)(2,1)S(1)} %get-tuple-element.15), channel_id=1, source_target_pairs={{0,3},{1,0},{2,1},{3,2},{4,7},{5,4},{6,5},{7,6},{8,11},{9,8},{10,9... | collective-permute-start | bytes 233480 | tf_op jit(solution)/shard_map/ppermute | solution.py:164
  138.0 10.6 %collective-permute-start.6 = (bf16[152,256]{1,0:T(8,128)(2,1)S(1)}, bf16[152,256]{1,0:T(8,128)(2,1)S(1)}, u32[]{:S(2)}, u32[]{:S(2)}) collective-permute-start(bf16[152,256]{1,0:T(8,128)(2,1)S(1)} %get-tuple-element.10), channel_id=1, source_target_pairs={{0,1},{1,2},{2,3},{3,0},{4,5},{5,6},{6,7},{7,4},{8,9},{9,10},{10,1... | collective-permute-start | bytes 233480 | tf_op jit(solution)/shard_map/ppermute | solution.py:172
  141.8 7.5 %collective-permute-start.7 = (bf16[152,256]{1,0:T(8,128)(2,1)S(1)}, bf16[152,256]{1,0:T(8,128)(2,1)S(1)}, u32[]{:S(2)}, u32[]{:S(2)}) collective-permute-start(bf16[152,256]{1,0:T(8,128)(2,1)S(1)} %get-tuple-element.10), channel_id=1, source_target_pairs={{0,2},{1,3},{2,0},{3,1},{4,6},{5,7},{6,4},{7,5},{8,10},{9,11},{10,... | collective-permute-start | bytes 233480 | tf_op jit(solution)/shard_map/ppermute | solution.py:172
  146.0 14.8 %collective-permute-start.8 = (bf16[152,256]{1,0:T(8,128)(2,1)S(1)}, bf16[152,256]{1,0:T(8,128)(2,1)S(1)}, u32[]{:S(2)}, u32[]{:S(2)}) collective-permute-start(bf16[152,256]{1,0:T(8,128)(2,1)S(1)} %get-tuple-element.10), channel_id=1, source_target_pairs={{0,3},{1,0},{2,1},{3,2},{4,7},{5,4},{6,5},{7,6},{8,11},{9,8},{10,9... | collective-permute-start | bytes 233480 | tf_op jit(solution)/shard_map/ppermute | solution.py:172
  149.9 1.3 copy-start.4
  156.9 40.3 %all-to-all-start.3 = ((bf16[32,24,128]{2,1,0:T(8,128)(2,1)}), bf16[32,24,128]{2,1,0:T(8,128)(2,1)S(1)}, u32[]{:S(2)}, u32[]{:S(2)}) async-start(bf16[32,24,128]{2,1,0:T(8,128)(2,1)} %shard_map.95), calls=%async_computation.3 | async-start | bytes 393216 | tf_op jit(solution)/shard_map/all_to_all | solution.py:239
  161.4 12.1 %collective-permute-start.9 = (bf16[4,152,256]{2,1,0:T(8,128)(2,1)}, bf16[4,152,256]{2,1,0:T(8,128)(2,1)S(1)}, u32[]{:S(2)}, u32[]{:S(2)}) collective-permute-start(bf16[4,152,256]{2,1,0:T(8,128)(2,1)} %bitcast_dynamic-update-slice_fusion.4), channel_id=1, source_target_pairs={{0,4},{4,8},{8,12},{12,0},{1,5},{5,9},{9,13},{13,1},{2,6},{6,10},{... | collective-permute-start | bytes 933896 | tf_op jit(solution)/shard_map/ppermute | solution.py:172
  163.7 16.0 %collective-permute-start.10 = (bf16[4,152,256]{2,1,0:T(8,128)(2,1)}, bf16[4,152,256]{2,1,0:T(8,128)(2,1)S(1)}, u32[]{:S(2)}, u32[]{:S(2)}) collective-permute-start(bf16[4,152,256]{2,1,0:T(8,128)(2,1)} %bitcast_dynamic-update-slice_fusion.4), channel_id=1, source_target_pairs={{0,8},{4,12},{8,0},{12,4},{1,9},{5,13},{9,1},{13,5},{2,10},{6,14},... | collective-permute-start | bytes 933896 | tf_op jit(solution)/shard_map/ppermute | solution.py:172
  167.7 14.6 %collective-permute-start.11 = (bf16[4,152,256]{2,1,0:T(8,128)(2,1)}, bf16[4,152,256]{2,1,0:T(8,128)(2,1)S(1)}, u32[]{:S(2)}, u32[]{:S(2)}) collective-permute-start(bf16[4,152,256]{2,1,0:T(8,128)(2,1)} %bitcast_dynamic-update-slice_fusion.4), channel_id=1, source_target_pairs={{0,12},{4,0},{8,4},{12,8},{1,13},{5,1},{9,5},{13,9},{2,14},{6,2},{... | collective-permute-start | bytes 933896 | tf_op jit(solution)/shard_map/ppermute | solution.py:172
  171.1 11.3 %copy-start.11 = (bf16[448,2432]{1,0:T(8,128)(2,1)S(1)}, bf16[448,2432]{1,0:T(8,128)(2,1)}, u32[]{:S(2)}) copy-start(bf16[448,2432]{1,0:T(8,128)(2,1)} %param.13) | copy-start | bytes 6537220
  (4 other events, 3.3 us)

commit v3 on v2

--- a/solution.py
+++ b/solution.py
@@ -7,17 +7,18 @@
 
 CAP = 6
 LANES = 128
+ROOM = 60
 F32 = jnp.float32
 BF16 = jnp.bfloat16
 
 
-def call(kernel, outs, *operands, flops=0):
+def call(kernel, outs, *operands, room=40):
     size = sum(v.size * v.dtype.itemsize for v in operands)
     return pl.pallas_call(
         kernel,
         out_shape=outs,
-        compiler_params=pltpu.CompilerParams(vmem_limit_bytes=40 * 1024 * 1024),
-        cost_estimate=pl.CostEstimate(flops=flops, bytes_accessed=size, transcendentals=0),
+        compiler_params=pltpu.CompilerParams(vmem_limit_bytes=room * 1024 * 1024),
+        cost_estimate=pl.CostEstimate(flops=0, bytes_accessed=size, transcendentals=0),
     )(*operands)
 
 
@@ -195,27 +196,37 @@
         routes.T,
         gates.T,
         grads.T,
-    )
+        room=ROOM,
+    )
+    message, dense_rows = lax.optimization_barrier((message, grads.T))
     arrived = lax.all_to_all(message, "z", 0, 0, tiled=True)
-
-    dense_mid = dot(dense_down, grads, 1, 1).astype(BF16)
+    dense_mid = dot(dense_down, dense_rows, 1, 0).astype(BF16)
     dense_mid = dense_mid.reshape(across, along, share, tokens)
-    dense_share = scattered(scattered(dense_mid, "x").astype(BF16), "y")
+    dense_sum = scattered(dense_mid, "x").astype(BF16)
+    arrived, dense_sum = lax.optimization_barrier((arrived, dense_sum))
 
     mid = call(
         down_kernel,
         jax.ShapeDtypeStruct((parts, piece, slots), BF16),
         lax.all_gather(arrived, "c", axis=0, tiled=False),
         expert_down[0].T,
-    )
+        room=ROOM,
+    )
+    mid, dense_sum = lax.optimization_barrier((mid, dense_sum))
     shares = lax.all_to_all(mid, tensor, 0, 0, tiled=True)
+    dense_share = scattered(dense_sum, "y")
+    shares, dense_share = lax.optimization_barrier((shares, dense_share))
     copies = call(
         gate_kernel,
         jax.ShapeDtypeStruct((parts, piece, slots), BF16),
         shares,
         expert_act[0].T,
     )
+    copies, dense_share = lax.optimization_barrier((copies, dense_share))
     full = lax.all_to_all(copies, tensor, 0, 0, tiled=True)
+    dense_hidden = (dense_share * jax.nn.silu(dense_act.T.astype(F32))).astype(BF16)
+    dense_column = gathered(dense_hidden, "y")
+    full, dense_column = lax.optimization_barrier((full, dense_column))
     size = full.size * 2 + expert_up.size * 2
     rows_t = pl.pallas_call(
         up_kernel,
@@ -236,11 +247,9 @@
         lax.axis_index("c").astype(jnp.int32).reshape(1),
         lax.all_gather(rows_t, "c", axis=0, tiled=False),
     )
+    back, dense_column = lax.optimization_barrier((back, dense_column))
     returned = lax.all_to_all(back, "z", 0, 0, tiled=True)
-
-    value = dense_act.T.astype(F32)
-    dense_hidden = (dense_share * jax.nn.silu(value)).astype(BF16)
-    dense_full = gathered(gathered(dense_hidden, "y"), "x").reshape(parts * share, tokens)
+    dense_full = gathered(dense_column, "x").reshape(parts * share, tokens)
     dense_t = dot(dense_up, dense_full, 1, 0)
     out_t = call(
         combine_kernel, jax.ShapeDtypeStruct((width, tokens), BF16), returned, chooser, dense_t

time: 199 us -> 185 us (0.930)
  waiting for transfers between devices: 78.7 us -> 58.9 us
  local copies, waits for them, and re-layouts: 12.6 us -> 6.74 us
  starting transfers between devices: 87.3 us -> 92.1 us
  Pallas kernels: 5.33 us -> 8.83 us
    all_to_all x1, waiting for transfers between devices: 35.4 us -> 4.85 us  [shards(): arrived = lax.all_to_all(message, 'z', 0, 0, tiled=True)]
    all_to_all x1, starting transfers between devices: 3.86 us -> 12.1 us  [shards(): returned = lax.all_to_all(back, 'z', 0, 0, tiled=True)]
    ppermute x6, waiting for transfers between devices: 10.1 us -> 16 us  [gathered(): piece = lax.ppermute(block, axis, turn(axis, step)) if step else block]
    ppermute x6, waiting for transfers between devices: 19.1 us -> 23.8 us  [scattered(): total = total + lax.ppermute(block, axis, turn(axis, step)).astype(F32)]
    unnamed x24 -> x14, local copies, waits for them, and re-layouts: 6.73 us -> 2.26 us
    pallas_call x4, Pallas kernels: 3.49 us -> 6.99 us  [call(): pl.pallas_call(kernel, out_shape=outs, compiler_params=pltpu.CompilerPara...]
    dynamic_update_slice x7, local copies, waits for them, and re-layouts: 3.14 us -> 0.13 us  [gathered(): out = lax.dynamic_update_index_in_dim(out, piece, (me - step) % size, 0)]
    ppermute x6, starting transfers between devices: 21.4 us -> 18.7 us  [scattered(): total = total + lax.ppermute(block, axis, turn(axis, step)).astype(F32)]
  transfers between devices with their start and end apart: 16 -> 16, of which waited for: 9 -> 12; matrix products, arithmetic and copies ran while one was open for 6% -> 6% of each run, Pallas kernels for 1% -> 0%
where the time goes in v3:
time: 185 us; the launch traced here: 184 us
  starting transfers between devices  92.1 us (50%)
  waiting for transfers between devices  58.9 us (32%)
  blocking collectives  9.54 us (5%)
  Pallas kernels  8.83 us (5%)
  local copies, waits for them, and re-layouts  6.74 us (4%)
  other arithmetic  4.39 us (2%)
  matrix products  2.56 us (1%)
    all_to_all x1, starting transfers between devices, shards(): arrived = lax.all_to_all(message, 'z', 0, 0, tiled=True)  29.4 us
    ppermute x6, waiting for transfers between devices, scattered(): total = total + lax.ppermute(block, axis, turn(axis, step)).astype(F32)  23.8 us
    ppermute x6, starting transfers between devices, gathered(): piece = lax.ppermute(block, axis, turn(axis, step)) if step else block  20.7 us
    ppermute x6, starting transfers between devices, scattered(): total = total + lax.ppermute(block, axis, turn(axis, step)).astype(F32)  18.7 us
    ppermute x6, waiting for transfers between devices, gathered(): piece = lax.ppermute(block, axis, turn(axis, step)) if step else block  16 us
    all_to_all x1, waiting for transfers between devices, shards(): returned = lax.all_to_all(back, 'z', 0, 0, tiled=True)  14.2 us
    all_to_all x1, starting transfers between devices, shards(): returned = lax.all_to_all(back, 'z', 0, 0, tiled=True)  12.1 us
    pallas_call x4, Pallas kernels, call(): pl.pallas_call(kernel, out_shape=outs, compiler_params=pltpu.CompilerPara...  6.99 us
  transfers between devices with their start and end apart: 16, of which 12 were waited for; matrix products, arithmetic and copies ran while one was open for 6% of the time, Pallas kernels for 0%

profile of v3, /device:TPU:1, one launch (start us, length us, event | category | flops | bytes accessed | tf_op | source)
XLA Modules:
  0.0 183.6 jit_solution(18130791136846195006)
XLA Ops:
  2.3 29.4 %all-to-all-start = ((bf16[32,24,128]{2,1,0:T(8,128)(2,1)}), bf16[32,24,128]{2,1,0:T(8,128)(2,1)}, u32[]{:S(2)}, u32[]{:S(2)}) async-start(bf16[32,24,128]{2,1,0:T(8,128)(2,1)} %get-tuple-element.22), calls=%async_computation | async-start | bytes 393216 | tf_op jit(solution)/shard_map/all_to_all | solution.py:202
  37.1 4.4 %collective-permute-start.2 = (bf16[4,152,256]{2,1,0:T(8,128)(2,1)}, bf16[4,152,256]{2,1,0:T(8,128)(2,1)S(1)}, u32[]{:S(2)}, u32[]{:S(2)}) collective-permute-start(bf16[4,152,256]{2,1,0:T(8,128)(2,1)} %get-tuple-element.40), channel_id=1, source_target_pairs={{0,12},{4,0},{8,4},{12,8},{1,13},{5,1},{9,5},{13,9},{2,14},{6,2},{... | collective-permute-start | bytes 933896 | tf_op jit(solution)/shard_map/ppermute | solution.py:165
  43.9 2.5 %collective-permute-start = (bf16[4,152,256]{2,1,0:T(8,128)(2,1)S(1)}, bf16[4,152,256]{2,1,0:T(8,128)(2,1)S(1)}, u32[]{:S(2)}, u32[]{:S(2)}) collective-permute-start(bf16[4,152,256]{2,1,0:T(8,128)(2,1)S(1)} %get-tuple-element.39), channel_id=1, source_target_pairs={{0,4},{4,8},{8,12},{12,0},{1,5},{5,9},{9,13},{13,1},{2,6},{6,10},{... | collective-permute-start | bytes 933896 | tf_op jit(solution)/shard_map/ppermute | solution.py:165
  48.3 4.6 %collective-permute-done.1 = bf16[4,152,256]{2,1,0:T(8,128)(2,1)S(1)} collective-permute-done((bf16[4,152,256]{2,1,0:T(8,128)(2,1)}, bf16[4,152,256]{2,1,0:T(8,128)(2,1)S(1)}, u32[]{:S(2)}, u32[]{:S(2)}) %collective-permute-start.1) | collective-permute-done | bytes 311328 | tf_op jit(solution)/shard_map/ppermute | solution.py:165
  52.8 8.3 %collective-permute-done = bf16[4,152,256]{2,1,0:T(8,128)(2,1)S(1)} collective-permute-done((bf16[4,152,256]{2,1,0:T(8,128)(2,1)S(1)}, bf16[4,152,256]{2,1,0:T(8,128)(2,1)S(1)}, u32[]{:S(2)}, u32[]{:S(2)}) %collective-permute-start) | collective-permute-done | bytes 311328 | tf_op jit(solution)/shard_map/ppermute | solution.py:165
  62.3 4.9 %all-to-all-done = bf16[32,24,128]{2,1,0:T(8,128)(2,1)} async-done(((bf16[32,24,128]{2,1,0:T(8,128)(2,1)}), bf16[32,24,128]{2,1,0:T(8,128)(2,1)}, u32[]{:S(2)}, u32[]{:S(2)}) %all-to-all-start) | async-done | bytes 196640 | tf_op jit(solution)/shard_map/all_to_all | solution.py:202
  67.1 6.7 %all-gather = bf16[64,24,128]{2,1,0:T(8,128)(2,1)} all-gather(bf16[32,24,128]{2,1,0:T(8,128)(2,1)} %all-to-all-done), channel_id=2, replica_groups=mesh['z'=32,'c'=2,'x'=4,'y'=4] {'c'}, dimensions={0}, use_global_device_ids=true | all-gather | bytes 589824 | tf_op jit(solution)/shard_map/all_gather | solution.py:211
  73.8 3.6 %shard_map.92 = bf16[16,76,384]{2,1,0:T(8,128)(2,1)} custom-call(bf16[2,32,24,128]{3,2,1,0:T(8,128)(2,1)} %bitcast.79, bf16[448,1216]{1,0:T(8,128)(2,1)} %bitcast.81), custom_call_target="tpu_custom_call" | custom-call | bytes 1482752 | tf_op jit(solution)/shard_map/pallas_call | solution.py:17
  77.3 6.9 %all-to-all-start.1 = ((bf16[16,76,384]{2,1,0:T(8,128)(2,1)}), bf16[16,76,384]{2,1,0:T(8,128)(2,1)S(1)}, u32[]{:S(2)}, u32[]{:S(2)}) async-start(bf16[16,76,384]{2,1,0:T(8,128)(2,1)} %shard_map.92), calls=%async_computation.1 | async-start | bytes 1966080 | tf_op jit(solution)/shard_map/all_to_all | solution.py:216
  85.0 4.4 %collective-permute-start.5 = (bf16[152,256]{1,0:T(8,128)(2,1)}, bf16[152,256]{1,0:T(8,128)(2,1)}, u32[]{:S(2)}, u32[]{:S(2)}) collective-permute-start(bf16[152,256]{1,0:T(8,128)(2,1)} %get-tuple-element.43), channel_id=1, source_target_pairs={{0,3},{1,0},{2,1},{3,2},{4,7},{5,4},{6,5},{7,6},{8,11},{9,8},{10,9... | collective-permute-start | bytes 233480 | tf_op jit(solution)/shard_map/ppermute | solution.py:165
  94.4 4.3 %collective-permute-done.5 = bf16[152,256]{1,0:T(8,128)(2,1)} collective-permute-done((bf16[152,256]{1,0:T(8,128)(2,1)}, bf16[152,256]{1,0:T(8,128)(2,1)}, u32[]{:S(2)}, u32[]{:S(2)}) %collective-permute-start.5) | collective-permute-done | bytes 77856 | tf_op jit(solution)/shard_map/ppermute | solution.py:165
  98.7 4.8 %collective-permute-done.3 = bf16[152,256]{1,0:T(8,128)(2,1)} collective-permute-done((bf16[152,256]{1,0:T(8,128)(2,1)}, bf16[152,256]{1,0:T(8,128)(2,1)}, u32[]{:S(2)}, u32[]{:S(2)}) %collective-permute-start.3) | collective-permute-done | bytes 77856 | tf_op jit(solution)/shard_map/ppermute | solution.py:165
  106.3 4.3 %all-to-all-start.2 = ((bf16[16,76,384]{2,1,0:T(8,128)(2,1)}), bf16[16,76,384]{2,1,0:T(8,128)(2,1)S(1)}, u32[]{:S(2)}, u32[]{:S(2)}) async-start(bf16[16,76,384]{2,1,0:T(8,128)(2,1)} %copy-done.1), calls=%async_computation.2 | async-start | bytes 1966080 | tf_op jit(solution)/shard_map/all_to_all | solution.py:226
  112.3 3.3 %collective-permute-start.6 = (bf16[152,256]{1,0:T(8,128)(2,1)}, bf16[152,256]{1,0:T(8,128)(2,1)S(1)}, u32[]{:S(2)}, u32[]{:S(2)}) collective-permute-start(bf16[152,256]{1,0:T(8,128)(2,1)} %get-tuple-element.38), channel_id=1, source_target_pairs={{0,1},{1,2},{2,3},{3,0},{4,5},{5,6},{6,7},{7,4},{8,9},{9,10},{10,1... | collective-permute-start | bytes 233480 | tf_op jit(solution)/shard_map/ppermute | solution.py:173
  115.7 4.3 %collective-permute-start.7 = (bf16[152,256]{1,0:T(8,128)(2,1)}, bf16[152,256]{1,0:T(8,128)(2,1)S(1)}, u32[]{:S(2)}, u32[]{:S(2)}) collective-permute-start(bf16[152,256]{1,0:T(8,128)(2,1)} %get-tuple-element.38), channel_id=1, source_target_pairs={{0,2},{1,3},{2,0},{3,1},{4,6},{5,7},{6,4},{7,5},{8,10},{9,11},{10,... | collective-permute-start | bytes 233480 | tf_op jit(solution)/shard_map/ppermute | solution.py:173
  120.0 3.1 %collective-permute-start.8 = (bf16[152,256]{1,0:T(8,128)(2,1)}, bf16[152,256]{1,0:T(8,128)(2,1)S(1)}, u32[]{:S(2)}, u32[]{:S(2)}) collective-permute-start(bf16[152,256]{1,0:T(8,128)(2,1)} %get-tuple-element.38), channel_id=1, source_target_pairs={{0,3},{1,0},{2,1},{3,2},{4,7},{5,4},{6,5},{7,6},{8,11},{9,8},{10,9... | collective-permute-start | bytes 233480 | tf_op jit(solution)/shard_map/ppermute | solution.py:173
  123.1 3.8 %collective-permute-done.6 = bf16[152,256]{1,0:T(8,128)(2,1)S(1)} collective-permute-done((bf16[152,256]{1,0:T(8,128)(2,1)}, bf16[152,256]{1,0:T(8,128)(2,1)S(1)}, u32[]{:S(2)}, u32[]{:S(2)}) %collective-permute-start.6) | collective-permute-done | bytes 77856 | tf_op jit(solution)/shard_map/ppermute | solution.py:173
  130.9 2.9 %all-gather.1 = bf16[896,384]{1,0:T(8,128)(2,1)S(1)} all-gather(bf16[448,384]{1,0:T(8,128)(2,1)S(1)} %shard_map.94), channel_id=3, replica_groups=mesh['z'=32,'c'=2,'x'=4,'y'=4] {'c'}, dimensions={0}, use_global_device_ids=true | all-gather | bytes 1032192 | tf_op jit(solution)/shard_map/all_gather | solution.py:248
  134.8 12.1 %all-to-all-start.3 = ((bf16[32,24,128]{2,1,0:T(8,128)(2,1)}), bf16[32,24,128]{2,1,0:T(8,128)(2,1)S(1)}, u32[]{:S(2)}, u32[]{:S(2)}) async-start(bf16[32,24,128]{2,1,0:T(8,128)(2,1)} %shard_map.95), calls=%async_computation.3 | async-start | bytes 393216 | tf_op jit(solution)/shard_map/all_to_all | solution.py:251
  146.9 2.7 %collective-permute-start.9 = (bf16[4,152,256]{2,1,0:T(8,128)(2,1)S(1)}, bf16[4,152,256]{2,1,0:T(8,128)(2,1)S(1)}, u32[]{:S(2)}, u32[]{:S(2)}) collective-permute-start(bf16[4,152,256]{2,1,0:T(8,128)(2,1)S(1)} %bitcast_dynamic-update-slice_fusion.4), channel_id=1, source_target_pairs={{0,4},{4,8},{8,12},{12,0},{1,5},{5,9},{9,13},{13,1},{2,6},{6,10},{... | collective-permute-start | bytes 933896 | tf_op jit(solution)/shard_map/ppermute | solution.py:173
  149.7 4.3 %collective-permute-start.10 = (bf16[4,152,256]{2,1,0:T(8,128)(2,1)S(1)}, bf16[4,152,256]{2,1,0:T(8,128)(2,1)S(1)}, u32[]{:S(2)}, u32[]{:S(2)}) collective-permute-start(bf16[4,152,256]{2,1,0:T(8,128)(2,1)S(1)} %bitcast_dynamic-update-slice_fusion.4), channel_id=1, source_target_pairs={{0,8},{4,12},{8,0},{12,4},{1,9},{5,13},{9,1},{13,5},{2,10},{6,14},... | collective-permute-start | bytes 933896 | tf_op jit(solution)/shard_map/ppermute | solution.py:173
  154.0 3.0 %collective-permute-start.11 = (bf16[4,152,256]{2,1,0:T(8,128)(2,1)S(1)}, bf16[4,152,256]{2,1,0:T(8,128)(2,1)S(1)}, u32[]{:S(2)}, u32[]{:S(2)}) collective-permute-start(bf16[4,152,256]{2,1,0:T(8,128)(2,1)S(1)} %bitcast_dynamic-update-slice_fusion.4), channel_id=1, source_target_pairs={{0,12},{4,0},{8,4},{12,8},{1,13},{5,1},{9,5},{13,9},{2,14},{6,2},{... | collective-permute-start | bytes 933896 | tf_op jit(solution)/shard_map/ppermute | solution.py:173
  158.3 7.1 %collective-permute-done.10 = bf16[4,152,256]{2,1,0:T(8,128)(2,1)S(1)} collective-permute-done((bf16[4,152,256]{2,1,0:T(8,128)(2,1)S(1)}, bf16[4,152,256]{2,1,0:T(8,128)(2,1)S(1)}, u32[]{:S(2)}, u32[]{:S(2)}) %collective-permute-start.10) | collective-permute-done | bytes 311328 | tf_op jit(solution)/shard_map/ppermute | solution.py:173
  168.3 14.2 %all-to-all-done.3.returned = bf16[32,24,128]{2,1,0:T(8,128)(2,1)S(1)} async-done(((bf16[32,24,128]{2,1,0:T(8,128)(2,1)}), bf16[32,24,128]{2,1,0:T(8,128)(2,1)S(1)}, u32[]{:S(2)}, u32[]{:S(2)}) %all-to-all-start.3) | async-done | bytes 196640 | tf_op jit(solution)/shard_map/all_to_all | solution.py:251
  (47 shorter events, 33.3 us)
Async XLA Ops:
  0.0 31.7 %copy-start = (bf16[2432,448]{0,1:T(8,128)(2,1)S(1)}, bf16[2432,448]{0,1:T(8,128)(2,1)}, u32[]{:S(2)}) copy-start(bf16[2432,448]{0,1:T(8,128)(2,1)} %param.12) | copy-start | bytes 6537220
  2.3 64.8 %all-to-all-start = ((bf16[32,24,128]{2,1,0:T(8,128)(2,1)}), bf16[32,24,128]{2,1,0:T(8,128)(2,1)}, u32[]{:S(2)}, u32[]{:S(2)}) async-start(bf16[32,24,128]{2,1,0:T(8,128)(2,1)} %get-tuple-element.22), calls=%async_computation | async-start | bytes 393216 | tf_op jit(solution)/shard_map/all_to_all | solution.py:202
  37.1 11.2 %collective-permute-start.2 = (bf16[4,152,256]{2,1,0:T(8,128)(2,1)}, bf16[4,152,256]{2,1,0:T(8,128)(2,1)S(1)}, u32[]{:S(2)}, u32[]{:S(2)}) collective-permute-start(bf16[4,152,256]{2,1,0:T(8,128)(2,1)} %get-tuple-element.40), channel_id=1, source_target_pairs={{0,12},{4,0},{8,4},{12,8},{1,13},{5,1},{9,5},{13,9},{2,14},{6,2},{... | collective-permute-start | bytes 933896 | tf_op jit(solution)/shard_map/ppermute | solution.py:165
  41.5 11.4 %collective-permute-start.1 = (bf16[4,152,256]{2,1,0:T(8,128)(2,1)}, bf16[4,152,256]{2,1,0:T(8,128)(2,1)S(1)}, u32[]{:S(2)}, u32[]{:S(2)}) collective-permute-start(bf16[4,152,256]{2,1,0:T(8,128)(2,1)} %get-tuple-element.41), channel_id=1, source_target_pairs={{0,8},{4,12},{8,0},{12,4},{1,9},{5,13},{9,1},{13,5},{2,10},{6,14},... | collective-permute-start | bytes 933896 | tf_op jit(solution)/shard_map/ppermute | solution.py:165
  43.9 17.2 %collective-permute-start = (bf16[4,152,256]{2,1,0:T(8,128)(2,1)S(1)}, bf16[4,152,256]{2,1,0:T(8,128)(2,1)S(1)}, u32[]{:S(2)}, u32[]{:S(2)}) collective-permute-start(bf16[4,152,256]{2,1,0:T(8,128)(2,1)S(1)} %get-tuple-element.39), channel_id=1, source_target_pairs={{0,4},{4,8},{8,12},{12,0},{1,5},{5,9},{9,13},{13,1},{2,6},{6,10},{... | collective-permute-start | bytes 933896 | tf_op jit(solution)/shard_map/ppermute | solution.py:165
  77.3 27.8 %copy-start.4 = (bf16[1,384,76]{1,2,0:T(8,128)(2,1)S(1)}, bf16[1,384,76]{1,2,0:T(8,128)(2,1)}, u32[]{:S(2)}) copy-start(bf16[1,384,76]{1,2,0:T(8,128)(2,1)} %param.17) | copy-start | bytes 175108
  77.3 27.8 %all-to-all-start.1 = ((bf16[16,76,384]{2,1,0:T(8,128)(2,1)}), bf16[16,76,384]{2,1,0:T(8,128)(2,1)S(1)}, u32[]{:S(2)}, u32[]{:S(2)}) async-start(bf16[16,76,384]{2,1,0:T(8,128)(2,1)} %shard_map.92), calls=%async_computation.1 | async-start | bytes 1966080 | tf_op jit(solution)/shard_map/all_to_all | solution.py:216
  85.0 13.7 %collective-permute-start.5 = (bf16[152,256]{1,0:T(8,128)(2,1)}, bf16[152,256]{1,0:T(8,128)(2,1)}, u32[]{:S(2)}, u32[]{:S(2)}) collective-permute-start(bf16[152,256]{1,0:T(8,128)(2,1)} %get-tuple-element.43), channel_id=1, source_target_pairs={{0,3},{1,0},{2,1},{3,2},{4,7},{5,4},{6,5},{7,6},{8,11},{9,8},{10,9... | collective-permute-start | bytes 233480 | tf_op jit(solution)/shard_map/ppermute | solution.py:165
  89.4 9.3 %collective-permute-start.4 = (bf16[152,256]{1,0:T(8,128)(2,1)}, bf16[152,256]{1,0:T(8,128)(2,1)}, u32[]{:S(2)}, u32[]{:S(2)}) collective-permute-start(bf16[152,256]{1,0:T(8,128)(2,1)} %get-tuple-element.44), channel_id=1, source_target_pairs={{0,2},{1,3},{2,0},{3,1},{4,6},{5,7},{6,4},{7,5},{8,10},{9,11},{10,... | collective-permute-start | bytes 233480 | tf_op jit(solution)/shard_map/ppermute | solution.py:165
  91.9 11.6 %collective-permute-start.3 = (bf16[152,256]{1,0:T(8,128)(2,1)}, bf16[152,256]{1,0:T(8,128)(2,1)}, u32[]{:S(2)}, u32[]{:S(2)}) collective-permute-start(bf16[152,256]{1,0:T(8,128)(2,1)} %get-tuple-element.42), channel_id=1, source_target_pairs={{0,1},{1,2},{2,3},{3,0},{4,5},{5,6},{6,7},{7,4},{8,9},{9,10},{10,1... | collective-permute-start | bytes 233480 | tf_op jit(solution)/shard_map/ppermute | solution.py:165
  105.4 1.0 copy-start.1
  106.3 4.4 %copy-start.5 = (bf16[256,152]{0,1:T(8,128)(2,1)S(1)}, bf16[256,152]{0,1:T(8,128)(2,1)}, u32[]{:S(2)}) copy-start(bf16[256,152]{0,1:T(8,128)(2,1)} %param.14) | copy-start | bytes 233476
  106.3 22.5 %all-to-all-start.2 = ((bf16[16,76,384]{2,1,0:T(8,128)(2,1)}), bf16[16,76,384]{2,1,0:T(8,128)(2,1)S(1)}, u32[]{:S(2)}, u32[]{:S(2)}) async-start(bf16[16,76,384]{2,1,0:T(8,128)(2,1)} %copy-done.1), calls=%async_computation.2 | async-start | bytes 1966080 | tf_op jit(solution)/shard_map/all_to_all | solution.py:226
  112.3 14.5 %collective-permute-start.6 = (bf16[152,256]{1,0:T(8,128)(2,1)}, bf16[152,256]{1,0:T(8,128)(2,1)S(1)}, u32[]{:S(2)}, u32[]{:S(2)}) collective-permute-start(bf16[152,256]{1,0:T(8,128)(2,1)} %get-tuple-element.38), channel_id=1, source_target_pairs={{0,1},{1,2},{2,3},{3,0},{4,5},{5,6},{6,7},{7,4},{8,9},{9,10},{10,1... | collective-permute-start | bytes 233480 | tf_op jit(solution)/shard_map/ppermute | solution.py:173
  115.7 13.1 %collective-permute-start.7 = (bf16[152,256]{1,0:T(8,128)(2,1)}, bf16[152,256]{1,0:T(8,128)(2,1)S(1)}, u32[]{:S(2)}, u32[]{:S(2)}) collective-permute-start(bf16[152,256]{1,0:T(8,128)(2,1)} %get-tuple-element.38), channel_id=1, source_target_pairs={{0,2},{1,3},{2,0},{3,1},{4,6},{5,7},{6,4},{7,5},{8,10},{9,11},{10,... | collective-permute-start | bytes 233480 | tf_op jit(solution)/shard_map/ppermute | solution.py:173
  120.0 8.8 %collective-permute-start.8 = (bf16[152,256]{1,0:T(8,128)(2,1)}, bf16[152,256]{1,0:T(8,128)(2,1)S(1)}, u32[]{:S(2)}, u32[]{:S(2)}) collective-permute-start(bf16[152,256]{1,0:T(8,128)(2,1)} %get-tuple-element.38), channel_id=1, source_target_pairs={{0,3},{1,0},{2,1},{3,2},{4,7},{5,4},{6,5},{7,6},{8,11},{9,8},{10,9... | collective-permute-start | bytes 233480 | tf_op jit(solution)/shard_map/ppermute | solution.py:173
  128.8 1.3 copy-start.2
  134.8 47.8 %all-to-all-start.3 = ((bf16[32,24,128]{2,1,0:T(8,128)(2,1)}), bf16[32,24,128]{2,1,0:T(8,128)(2,1)S(1)}, u32[]{:S(2)}, u32[]{:S(2)}) async-start(bf16[32,24,128]{2,1,0:T(8,128)(2,1)} %shard_map.95), calls=%async_computation.3 | async-start | bytes 393216 | tf_op jit(solution)/shard_map/all_to_all | solution.py:251
  146.9 11.4 %collective-permute-start.9 = (bf16[4,152,256]{2,1,0:T(8,128)(2,1)S(1)}, bf16[4,152,256]{2,1,0:T(8,128)(2,1)S(1)}, u32[]{:S(2)}, u32[]{:S(2)}) collective-permute-start(bf16[4,152,256]{2,1,0:T(8,128)(2,1)S(1)} %bitcast_dynamic-update-slice_fusion.4), channel_id=1, source_target_pairs={{0,4},{4,8},{8,12},{12,0},{1,5},{5,9},{9,13},{13,1},{2,6},{6,10},{... | collective-permute-start | bytes 933896 | tf_op jit(solution)/shard_map/ppermute | solution.py:173
  149.7 15.8 %collective-permute-start.10 = (bf16[4,152,256]{2,1,0:T(8,128)(2,1)S(1)}, bf16[4,152,256]{2,1,0:T(8,128)(2,1)S(1)}, u32[]{:S(2)}, u32[]{:S(2)}) collective-permute-start(bf16[4,152,256]{2,1,0:T(8,128)(2,1)S(1)} %bitcast_dynamic-update-slice_fusion.4), channel_id=1, source_target_pairs={{0,8},{4,12},{8,0},{12,4},{1,9},{5,13},{9,1},{13,5},{2,10},{6,14},... | collective-permute-start | bytes 933896 | tf_op jit(solution)/shard_map/ppermute | solution.py:173
  154.0 13.5 %collective-permute-start.11 = (bf16[4,152,256]{2,1,0:T(8,128)(2,1)S(1)}, bf16[4,152,256]{2,1,0:T(8,128)(2,1)S(1)}, u32[]{:S(2)}, u32[]{:S(2)}) collective-permute-start(bf16[4,152,256]{2,1,0:T(8,128)(2,1)S(1)} %bitcast_dynamic-update-slice_fusion.4), channel_id=1, source_target_pairs={{0,12},{4,0},{8,4},{12,8},{1,13},{5,1},{9,5},{13,9},{2,14},{6,2},{... | collective-permute-start | bytes 933896 | tf_op jit(solution)/shard_map/ppermute | solution.py:173
  157.1 10.4 %copy-start.6 = (bf16[448,2432]{1,0:T(8,128)(2,1)S(1)}, bf16[448,2432]{1,0:T(8,128)(2,1)}, u32[]{:S(2)}) copy-start(bf16[448,2432]{1,0:T(8,128)(2,1)} %param.13) | copy-start | bytes 6537220
  167.6 15.0 %copy-start.3 = (bf16[256,256]{1,0:T(8,128)(2,1)S(1)}, bf16[256,256]{1,0:T(8,128)(2,1)}, u32[]{:S(2)}) copy-start(bf16[256,256]{1,0:T(8,128)(2,1)} %get-tuple-element.35.chooser) | copy-start | bytes 393220

commit v4 on v2

--- a/solution.py
+++ b/solution.py
@@ -7,17 +7,22 @@
 
 CAP = 6
 LANES = 128
+ROOM = 60
 F32 = jnp.float32
 BF16 = jnp.bfloat16
 
 
-def call(kernel, outs, *operands, flops=0):
+def call(kernel, outs, *operands, room=20, scratch=(), spaces=None, out_space=pltpu.VMEM):
     size = sum(v.size * v.dtype.itemsize for v in operands)
+    spaces = spaces or [pltpu.VMEM] * len(operands)
     return pl.pallas_call(
         kernel,
         out_shape=outs,
-        compiler_params=pltpu.CompilerParams(vmem_limit_bytes=40 * 1024 * 1024),
-        cost_estimate=pl.CostEstimate(flops=flops, bytes_accessed=size, transcendentals=0),
+        in_specs=[pl.BlockSpec(memory_space=space) for space in spaces],
+        out_specs=jax.tree.map(lambda _: pl.BlockSpec(memory_space=out_space), outs),
+        scratch_shapes=list(scratch),
+        compiler_params=pltpu.CompilerParams(vmem_limit_bytes=room * 1024 * 1024),
+        cost_estimate=pl.CostEstimate(flops=0, bytes_accessed=size, transcendentals=0),
     )(*operands)
 
 
@@ -84,7 +89,7 @@
     )
 
 
-def down_kernel(arrived, down_t, mid):
+def down_kernel(arrived, down_t, mid, held_out, sems):
     cores, held = arrived.shape[0], arrived.shape[1]
     blocks = unpacked(arrived[...].reshape(cores * held, 3 * 8, LANES))
     slots, rows = cores * held * CAP, cores * held * 8
@@ -98,18 +103,35 @@
     weights = jnp.concatenate([down_t[: 3 * LANES, :], down_t[width - LANES :, :]], axis=0)
     total = dot(weights, picked, 0, 1)
     piece = mid.shape[1]
+    copies = []
     for part in range(mid.shape[0]):
-        mid[part] = total[piece * part : piece * (part + 1)].astype(BF16)
-
-
-def gate_kernel(shares, act, copies):
+        held_out[part] = total[piece * part : piece * (part + 1)].astype(BF16)
+        copies.append(pltpu.make_async_copy(held_out.at[part], mid.at[part], sems.at[part]))
+        copies[part].start()
+    for copy in copies:
+        copy.wait()
+
+
+def gate_kernel(shares, act, copies, held_out, sems):
     total = shares[0].astype(F32)
     for part in range(1, shares.shape[0]):
         total = total + shares[part].astype(F32)
     value = act[...].astype(F32)
-    hidden = (total * (value / (1.0 + jnp.exp(-value)))).astype(BF16)
-    for part in range(copies.shape[0]):
-        copies[part] = hidden
+    held_out[...] = (total * (value / (1.0 + jnp.exp(-value)))).astype(BF16)
+    sent = [
+        pltpu.make_async_copy(held_out, copies.at[part], sems.at[part])
+        for part in range(copies.shape[0])
+    ]
+    for copy in sent:
+        copy.start()
+    for copy in sent:
+        copy.wait()
+
+
+def hold_kernel(weights, held_in, sem):
+    copy = pltpu.make_async_copy(weights, held_in, sem)
+    copy.start()
+    copy.wait()
 
 
 def up_kernel(full, up, rows_t, stacked):
@@ -151,27 +173,66 @@
     ).astype(BF16)
 
 
-def turn(axis, step):
-    size = lax.axis_size(axis)
-    return [(i, (i + step) % size) for i in range(size)]
-
-
-def scattered(blocks, axis):
-    size, me = lax.axis_size(axis), lax.axis_index(axis)
-    total = lax.dynamic_index_in_dim(blocks, me, 0, keepdims=False).astype(F32)
-    for step in range(1, size):
-        block = lax.dynamic_index_in_dim(blocks, (me + step) % size, 0, keepdims=False)
-        total = total + lax.ppermute(block, axis, turn(axis, step)).astype(F32)
-    return total
-
-
-def gathered(block, axis):
-    size, me = lax.axis_size(axis), lax.axis_index(axis)
-    out = jnp.zeros((size,) + block.shape, block.dtype)
+def wrapped(value, size):
+    value = jnp.where(value >= size, value - size, value)
+    return jnp.where(value < 0, value + size, value)
+
+
+def dense_down_kernel(place, down_t, grads_t, *rest):
+    slabs, blocks = rest[:-1], rest[-1]
+    size = len(slabs)
+    blocks[...] = dot(down_t[...], grads_t[...], 0, 0).reshape(blocks.shape)
     for step in range(size):
-        piece = lax.ppermute(block, axis, turn(axis, step)) if step else block
-        out = lax.dynamic_update_index_in_dim(out, piece, (me - step) % size, 0)
-    return out
+        first = wrapped(place[0] + step, size) * place[2]
+        for second in range(size):
+            slabs[step][second] = blocks[first + second * place[3]].astype(BF16)
+
+
+def dense_sum_kernel(place, *rest):
+    size = len(rest) // 2
+    slabs, sums = rest[:size], rest[size:]
+    for step in range(size):
+        second = wrapped(place[1] + step, size)
+        total = slabs[0][second].astype(F32)
+        for slab in slabs[1:]:
+            total = total + slab[second].astype(F32)
+        sums[step][...] = total.astype(sums[step].dtype)
+
+
+def dense_gate_kernel(*rest):
+    pieces, act, hidden = rest[:-2], rest[-2], rest[-1]
+    total = pieces[0][...].astype(F32)
+    for piece in pieces[1:]:
+        total = total + piece[...].astype(F32)
+    value = act[...].astype(F32)
+    hidden[...] = (total * (value / (1.0 + jnp.exp(-value)))).astype(BF16)
+
+
+def dense_up_kernel(place, *rest):
+    slabs, up, out_t, blocks = rest[:-3], rest[-3], rest[-2], rest[-1]
+    size = len(slabs)
+    for back in range(size):
+        first = wrapped(place[0] - back, size) * place[2]
+        for step in range(size):
+            second = wrapped(place[1] - step, size) * place[3]
+            blocks[first + second] = slabs[back][step].astype(F32)
+    full = blocks[...].reshape(up.shape[1], blocks.shape[2]).astype(BF16)
+    out_t[...] = dot(up[...], full, 1, 0)
+
+
+def moved(value, stage, step, size):
+    pairs = []
+    for core in range(2):
+        for x in range(size):
+            for y in range(size):
+                if core == stage:
+                    target = ((x + step) % size, y)
+                else:
+                    target = (x, (y + step) % size)
+                pairs.append(
+                    ((core * size + x) * size + y, (core * size + target[0]) * size + target[1])
+                )
+    return lax.ppermute(value, ("c", "x", "y"), pairs)
 
 
 def shards(
@@ -195,53 +256,105 @@
         routes.T,
         gates.T,
         grads.T,
-    )
+        room=ROOM,
+    )
+    core, x, y = lax.axis_index("c"), lax.axis_index("x"), lax.axis_index("y")
+    place = jnp.stack(
+        [
+            jnp.where(core == 0, x, y),
+            jnp.where(core == 0, y, x),
+            jnp.where(core == 0, along, 1),
+            jnp.where(core == 0, 1, along),
+        ]
+    ).astype(jnp.int32)
+    smem, vmem = pltpu.SMEM, pltpu.VMEM
+    slab = jax.ShapeDtypeStruct((along, share, tokens), BF16)
+    piece_f32 = jax.ShapeDtypeStruct((share, tokens), F32)
+    piece_bf16 = jax.ShapeDtypeStruct((share, tokens), BF16)
+    blocks = pltpu.VMEM((parts, share, tokens), F32)
+    steps = range(1, along)
+
+    message, dense_rows = lax.optimization_barrier((message, grads.T))
     arrived = lax.all_to_all(message, "z", 0, 0, tiled=True)
-
-    dense_mid = dot(dense_down, grads, 1, 1).astype(BF16)
-    dense_mid = dense_mid.reshape(across, along, share, tokens)
-    dense_share = scattered(scattered(dense_mid, "x").astype(BF16), "y")
-
+    slabs = call(
+        dense_down_kernel,
+        (slab,) * along,
+        place,
+        dense_down.T,
+        dense_rows,
+        scratch=[blocks],
+        spaces=[smem, vmem, vmem],
+    )
+    sums = call(
+        dense_sum_kernel,
+        (piece_f32,) + (piece_bf16,) * (along - 1),
+        place,
+        slabs[0],
+        *[moved(slabs[step], 0, step, along) for step in steps],
+        spaces=[smem] + [vmem] * along,
+    )
+    arrived, sums = lax.optimization_barrier((arrived, sums))
+
+    parts_out = jax.ShapeDtypeStruct((parts, piece, slots), BF16)
     mid = call(
         down_kernel,
-        jax.ShapeDtypeStruct((parts, piece, slots), BF16),
+        parts_out,
         lax.all_gather(arrived, "c", axis=0, tiled=False),
         expert_down[0].T,
-    )
+        scratch=[pltpu.VMEM((parts, piece, slots), BF16), pltpu.SemaphoreType.DMA((parts,))],
+        out_space=pltpu.HBM,
+    )
+    mid, sums, up = lax.optimization_barrier((mid, sums, expert_up[0]))
     shares = lax.all_to_all(mid, tensor, 0, 0, tiled=True)
+    pieces = [sums[0]] + [moved(sums[step], 1, step, along) for step in steps]
+    up = call(
+        hold_kernel,
+        jax.ShapeDtypeStruct((width, half), BF16),
+        up,
+        scratch=[pltpu.SemaphoreType.DMA],
+        spaces=[pltpu.HBM],
+    )
+    shares, pieces, up = lax.optimization_barrier((shares, pieces, up))
     copies = call(
         gate_kernel,
-        jax.ShapeDtypeStruct((parts, piece, slots), BF16),
+        parts_out,
         shares,
         expert_act[0].T,
-    )
+        scratch=[pltpu.VMEM((piece, slots), BF16), pltpu.SemaphoreType.DMA((parts,))],
+        out_space=pltpu.HBM,
+    )
+    copies, pieces = lax.optimization_barrier((copies, pieces))
     full = lax.all_to_all(copies, tensor, 0, 0, tiled=True)
-    size = full.size * 2 + expert_up.size * 2
-    rows_t = pl.pallas_call(
+    hidden = call(dense_gate_kernel, piece_bf16, *pieces, dense_act.T)
+    columns = [hidden] + [moved(hidden, 1, step, along) for step in steps]
+    full, columns = lax.optimization_barrier((full, columns))
+    rows_t = call(
         up_kernel,
-        out_shape=jax.ShapeDtypeStruct((width, slots), BF16),
-        scratch_shapes=[pltpu.VMEM((half, slots), F32)],
-        compiler_params=pltpu.CompilerParams(vmem_limit_bytes=40 * 1024 * 1024),
-        cost_estimate=pl.CostEstimate(flops=0, bytes_accessed=size, transcendentals=0),
-    )(full, expert_up[0])
-    back = pl.pallas_call(
+        jax.ShapeDtypeStruct((width, slots), BF16),
+        full,
+        up,
+        scratch=[pltpu.VMEM((half, slots), F32)],
+    )
+    back = call(
         return_kernel,
-        out_shape=jax.ShapeDtypeStruct((held, 24, LANES), BF16),
-        in_specs=[
-            pl.BlockSpec(memory_space=pltpu.SMEM),
-            pl.BlockSpec(memory_space=pltpu.VMEM),
-        ],
-        compiler_params=pltpu.CompilerParams(vmem_limit_bytes=40 * 1024 * 1024),
-    )(
-        lax.axis_index("c").astype(jnp.int32).reshape(1),
+        jax.ShapeDtypeStruct((held, 24, LANES), BF16),
+        core.astype(jnp.int32).reshape(1),
         lax.all_gather(rows_t, "c", axis=0, tiled=False),
-    )
+        spaces=[smem, vmem],
+    )
+    back, columns = lax.optimization_barrier((back, columns))
     returned = lax.all_to_all(back, "z", 0, 0, tiled=True)
-
-    value = dense_act.T.astype(F32)
-    dense_hidden = (dense_share * jax.nn.silu(value)).astype(BF16)
-    dense_full = gathered(gathered(dense_hidden, "y"), "x").reshape(parts * share, tokens)
-    dense_t = dot(dense_up, dense_full, 1, 0)
+    column = jnp.stack(columns)
+    dense_t = call(
+        dense_up_kernel,
+        jax.ShapeDtypeStruct((width, tokens), F32),
+        place,
+        column,
+        *[moved(column, 0, step, along) for step in steps],
+        dense_up,
+        scratch=[blocks],
+        spaces=[smem] + [vmem] * (along + 1),
+    )
     out_t = call(
         combine_kernel, jax.ShapeDtypeStruct((width, tokens), BF16), returned, chooser, dense_t
     )

time: 199 us -> 171 us (0.86)
  waiting for transfers between devices: 78.7 us -> 57.3 us
  local copies, waits for them, and re-layouts: 12.6 us -> 4.69 us
  Pallas kernels: 5.33 us -> 12.8 us
  other arithmetic: 3.87 us -> 0.12 us
    all_to_all x1, waiting for transfers between devices: 35.4 us -> 14.1 us  [shards(): arrived = lax.all_to_all(message, 'z', 0, 0, tiled=True)]
    pallas_call x6 -> x11, Pallas kernels: 5.33 us -> 12.8 us  [call(): pl.pallas_call(kernel, out_shape=outs, in_specs=[pl.BlockSpec(memory_spac...]
    ppermute x12, waiting for transfers between devices: 29.2 us -> 24.4 us  [moved(): return lax.ppermute(value, ('c', 'x', 'y'), pairs)]
    all_to_all x1, waiting for transfers between devices: 14.1 us -> 18.8 us  [shards(): returned = lax.all_to_all(back, 'z', 0, 0, tiled=True)]
    dynamic_update_slice x7 -> x0, local copies, waits for them, and re-layouts: 3.14 us -> none  [gathered(): out = lax.dynamic_update_index_in_dim(out, piece, (me - step) % size, 0)]
    ppermute x12, starting transfers between devices: 41.4 us -> 38.3 us  [moved(): return lax.ppermute(value, ('c', 'x', 'y'), pairs)]
    all_to_all x1, starting transfers between devices: 3.86 us -> 6.73 us  [shards(): returned = lax.all_to_all(back, 'z', 0, 0, tiled=True)]
    convert_element_type x1 -> x0, other arithmetic: 2.13 us -> none  [shards(): dense_share = scattered(scattered(dense_mid, 'x').astype(BF16), 'y')]
  transfers between devices with their start and end apart: 16 -> 16, of which waited for: 9 -> 12; matrix products, arithmetic and copies ran while one was open for 6% -> 0% of each run, Pallas kernels for 1% -> 3%
where the time goes in v4:
time: 171 us; the launch traced here: 170 us
  starting transfers between devices  85.5 us (50%)
  waiting for transfers between devices  57.3 us (34%)
  Pallas kernels  12.8 us (7%)
  blocking collectives  9.62 us (6%)
  local copies, waits for them, and re-layouts  4.69 us (3%)
    ppermute x12, starting transfers between devices, moved(): return lax.ppermute(value, ('c', 'x', 'y'), pairs)  38.3 us
    all_to_all x1, starting transfers between devices, shards(): arrived = lax.all_to_all(message, 'z', 0, 0, tiled=True)  29.3 us
    ppermute x12, waiting for transfers between devices, moved(): return lax.ppermute(value, ('c', 'x', 'y'), pairs)  24.4 us
    all_to_all x1, waiting for transfers between devices, shards(): returned = lax.all_to_all(back, 'z', 0, 0, tiled=True)  18.8 us
    all_to_all x1, waiting for transfers between devices, shards(): arrived = lax.all_to_all(message, 'z', 0, 0, tiled=True)  14.1 us
    pallas_call x11, Pallas kernels, call(): pl.pallas_call(kernel, out_shape=outs, in_specs=[pl.BlockSpec(memory_spac...  12.8 us
    all_to_all x1, starting transfers between devices, shards(): shares = lax.all_to_all(mid, tensor, 0, 0, tiled=True)  6.9 us
    all_to_all x1, starting transfers between devices, shards(): returned = lax.all_to_all(back, 'z', 0, 0, tiled=True)  6.73 us
  transfers between devices with their start and end apart: 16, of which 12 were waited for; matrix products, arithmetic and copies ran while one was open for 0% of the time, Pallas kernels for 3%

profile of v4, /device:TPU:1, one launch (start us, length us, event | category | flops | bytes accessed | tf_op | source)
XLA Modules:
  0.0 170.4 jit_solution(14074113165508688880)
XLA Ops:
  2.1 29.3 %all-to-all-start = ((bf16[32,24,128]{2,1,0:T(8,128)(2,1)}), bf16[32,24,128]{2,1,0:T(8,128)(2,1)S(1)}, u32[]{:S(2)}, u32[]{:S(2)}) async-start(bf16[32,24,128]{2,1,0:T(8,128)(2,1)} %get-tuple-element.50), calls=%async_computation | async-start | bytes 393216 | tf_op jit(solution)/shard_map/all_to_all | solution.py:278
  35.6 3.3 %collective-permute-start = (bf16[4,152,256]{2,1,0:T(8,128)(2,1)S(1)}, bf16[4,152,256]{2,1,0:T(8,128)(2,1)S(1)}, u32[]{:S(2)}, u32[]{:S(2)}) collective-permute-start(bf16[4,152,256]{2,1,0:T(8,128)(2,1)S(1)} %get-tuple-element.53), channel_id=1, source_target_pairs={{0,4},{1,5},{2,6},{3,7},{4,8},{5,9},{6,10},{7,11},{8,12},{9,13},{1... | collective-permute-start | bytes 933896 | tf_op jit(solution)/shard_map/ppermute | solution.py:235
  39.0 4.5 %collective-permute-start.1 = (bf16[4,152,256]{2,1,0:T(8,128)(2,1)S(1)}, bf16[4,152,256]{2,1,0:T(8,128)(2,1)S(1)}, u32[]{:S(2)}, u32[]{:S(2)}) collective-permute-start(bf16[4,152,256]{2,1,0:T(8,128)(2,1)S(1)} %get-tuple-element.54), channel_id=1, source_target_pairs={{0,8},{1,9},{2,10},{3,11},{4,12},{5,13},{6,14},{7,15},{8,0},{9,1},... | collective-permute-start | bytes 933896 | tf_op jit(solution)/shard_map/ppermute | solution.py:235
  43.5 3.0 %collective-permute-start.2 = (bf16[4,152,256]{2,1,0:T(8,128)(2,1)S(1)}, bf16[4,152,256]{2,1,0:T(8,128)(2,1)S(1)}, u32[]{:S(2)}, u32[]{:S(2)}) collective-permute-start(bf16[4,152,256]{2,1,0:T(8,128)(2,1)S(1)} %get-tuple-element.55), channel_id=1, source_target_pairs={{0,12},{1,13},{2,14},{3,15},{4,0},{5,1},{6,2},{7,3},{8,4},{9,5},{1... | collective-permute-start | bytes 933896 | tf_op jit(solution)/shard_map/ppermute | solution.py:235
  46.5 3.0 %collective-permute-done.1.rest_2_ = bf16[4,152,256]{2,1,0:T(8,128)(2,1)S(1)} collective-permute-done((bf16[4,152,256]{2,1,0:T(8,128)(2,1)S(1)}, bf16[4,152,256]{2,1,0:T(8,128)(2,1)S(1)}, u32[]{:S(2)}, u32[]{:S(2)}) %collective-permute-start.1) | collective-permute-done | bytes 311328 | tf_op jit(solution)/shard_map/ppermute | solution.py:235
  52.7 14.1 %all-to-all-done = bf16[32,24,128]{2,1,0:T(8,128)(2,1)S(1)} async-done(((bf16[32,24,128]{2,1,0:T(8,128)(2,1)}), bf16[32,24,128]{2,1,0:T(8,128)(2,1)S(1)}, u32[]{:S(2)}, u32[]{:S(2)}) %all-to-all-start) | async-done | bytes 196640 | tf_op jit(solution)/shard_map/all_to_all | solution.py:278
  66.9 4.1 %all-gather = bf16[64,24,128]{2,1,0:T(8,128)(2,1)S(1)} all-gather(bf16[32,24,128]{2,1,0:T(8,128)(2,1)S(1)} %all-to-all-done), channel_id=2, replica_groups=mesh['z'=32,'c'=2,'x'=4,'y'=4] {'c'}, dimensions={0}, use_global_device_ids=true | all-gather | bytes 589824 | tf_op jit(solution)/shard_map/all_gather | solution.py:302
  73.0 6.9 %all-to-all-start.1 = ((bf16[16,76,384]{2,1,0:T(8,128)(2,1)}), bf16[16,76,384]{2,1,0:T(8,128)(2,1)S(1)}, u32[]{:S(2)}, u32[]{:S(2)}) async-start(bf16[16,76,384]{2,1,0:T(8,128)(2,1)} %shard_map.94), calls=%async_computation.1 | async-start | bytes 1966080 | tf_op jit(solution)/shard_map/all_to_all | solution.py:308
  79.9 3.3 %collective-permute-start.3 = (bf16[152,256]{1,0:T(8,128)(2,1)}, bf16[152,256]{1,0:T(8,128)(2,1)S(1)}, u32[]{:S(2)}, u32[]{:S(2)}) collective-permute-start(bf16[152,256]{1,0:T(8,128)(2,1)} %get-tuple-element.67), channel_id=1, source_target_pairs={{0,1},{1,2},{2,3},{3,0},{4,5},{5,6},{6,7},{7,4},{8,9},{9,10},{10,1... | collective-permute-start | bytes 233480 | tf_op jit(solution)/shard_map/ppermute | solution.py:235
  83.2 4.3 %collective-permute-start.4 = (bf16[152,256]{1,0:T(8,128)(2,1)}, bf16[152,256]{1,0:T(8,128)(2,1)S(1)}, u32[]{:S(2)}, u32[]{:S(2)}) collective-permute-start(bf16[152,256]{1,0:T(8,128)(2,1)} %get-tuple-element.68), channel_id=1, source_target_pairs={{0,2},{1,3},{2,0},{3,1},{4,6},{5,7},{6,4},{7,5},{8,10},{9,11},{10,... | collective-permute-start | bytes 233480 | tf_op jit(solution)/shard_map/ppermute | solution.py:235
  87.5 3.1 %collective-permute-start.5 = (bf16[152,256]{1,0:T(8,128)(2,1)}, bf16[152,256]{1,0:T(8,128)(2,1)S(1)}, u32[]{:S(2)}, u32[]{:S(2)}) collective-permute-start(bf16[152,256]{1,0:T(8,128)(2,1)} %copy-done.12), channel_id=1, source_target_pairs={{0,3},{1,0},{2,1},{3,2},{4,7},{5,4},{6,5},{7,6},{8,11},{9,8},{10,9... | collective-permute-start | bytes 233480 | tf_op jit(solution)/shard_map/ppermute | solution.py:235
  90.8 3.3 %collective-permute-done.3.rest_1_ = bf16[152,256]{1,0:T(8,128)(2,1)S(1)} collective-permute-done((bf16[152,256]{1,0:T(8,128)(2,1)}, bf16[152,256]{1,0:T(8,128)(2,1)S(1)}, u32[]{:S(2)}, u32[]{:S(2)}) %collective-permute-start.3) | collective-permute-done | bytes 77856 | tf_op jit(solution)/shard_map/ppermute | solution.py:235
  99.8 4.2 %all-to-all-start.2 = ((bf16[16,76,384]{2,1,0:T(8,128)(2,1)}), bf16[16,76,384]{2,1,0:T(8,128)(2,1)S(1)}, u32[]{:S(2)}, u32[]{:S(2)}) async-start(bf16[16,76,384]{2,1,0:T(8,128)(2,1)} %shard_map.96), calls=%async_computation.2 | async-start | bytes 1966080 | tf_op jit(solution)/shard_map/all_to_all | solution.py:327
  104.2 4.5 %collective-permute-start.8 = (bf16[152,256]{1,0:T(8,128)(2,1)S(1)}, bf16[152,256]{1,0:T(8,128)(2,1)S(1)}, u32[]{:S(2)}, u32[]{:S(2)}) collective-permute-start(bf16[152,256]{1,0:T(8,128)(2,1)S(1)} %shard_map.97), channel_id=1, source_target_pairs={{0,3},{1,0},{2,1},{3,2},{4,7},{5,4},{6,5},{7,6},{8,11},{9,8},{10,9... | collective-permute-start | bytes 233480 | tf_op jit(solution)/shard_map/ppermute | solution.py:235
  108.7 2.5 %collective-permute-start.7 = (bf16[152,256]{1,0:T(8,128)(2,1)S(1)}, bf16[152,256]{1,0:T(8,128)(2,1)S(1)}, u32[]{:S(2)}, u32[]{:S(2)}) collective-permute-start(bf16[152,256]{1,0:T(8,128)(2,1)S(1)} %shard_map.97), channel_id=1, source_target_pairs={{0,2},{1,3},{2,0},{3,1},{4,6},{5,7},{6,4},{7,5},{8,10},{9,11},{10,... | collective-permute-start | bytes 233480 | tf_op jit(solution)/shard_map/ppermute | solution.py:235
  111.2 2.5 %collective-permute-start.6 = (bf16[152,256]{1,0:T(8,128)(2,1)S(1)}, bf16[152,256]{1,0:T(8,128)(2,1)S(1)}, u32[]{:S(2)}, u32[]{:S(2)}) collective-permute-start(bf16[152,256]{1,0:T(8,128)(2,1)S(1)} %shard_map.97), channel_id=1, source_target_pairs={{0,1},{1,2},{2,3},{3,0},{4,5},{5,6},{6,7},{7,4},{8,9},{9,10},{10,1... | collective-permute-start | bytes 233480 | tf_op jit(solution)/shard_map/ppermute | solution.py:235
  113.7 3.7 %collective-permute-done.8 = bf16[152,256]{1,0:T(8,128)(2,1)S(1)} collective-permute-done((bf16[152,256]{1,0:T(8,128)(2,1)S(1)}, bf16[152,256]{1,0:T(8,128)(2,1)S(1)}, u32[]{:S(2)}, u32[]{:S(2)}) %collective-permute-start.8) | collective-permute-done | bytes 77856 | tf_op jit(solution)/shard_map/ppermute | solution.py:235
  120.4 5.5 %all-gather.1 = bf16[896,384]{1,0:T(8,128)(2,1)S(1)} all-gather(bf16[448,384]{1,0:T(8,128)(2,1)S(1)} %shard_map.98), channel_id=3, replica_groups=mesh['z'=32,'c'=2,'x'=4,'y'=4] {'c'}, dimensions={0}, use_global_device_ids=true | all-gather | bytes 1032192 | tf_op jit(solution)/shard_map/all_gather | solution.py:342
  127.0 6.7 %all-to-all-start.3 = ((bf16[32,24,128]{2,1,0:T(8,128)(2,1)}), bf16[32,24,128]{2,1,0:T(8,128)(2,1)S(1)}, u32[]{:S(2)}, u32[]{:S(2)}) async-start(bf16[32,24,128]{2,1,0:T(8,128)(2,1)} %shard_map.99), calls=%async_computation.3 | async-start | bytes 393216 | tf_op jit(solution)/shard_map/all_to_all | solution.py:346
  133.8 2.6 %collective-permute-start.11 = (bf16[4,152,256]{2,1,0:T(8,128)(2,1)S(1)}, bf16[4,152,256]{2,1,0:T(8,128)(2,1)S(1)}, u32[]{:S(2)}, u32[]{:S(2)}) collective-permute-start(bf16[4,152,256]{2,1,0:T(8,128)(2,1)S(1)} %pad_maximum_fusion.rest_0_), channel_id=1, source_target_pairs={{0,12},{1,13},{2,14},{3,15},{4,0},{5,1},{6,2},{7,3},{8,4},{9,5},{1... | collective-permute-start | bytes 933896 | tf_op jit(solution)/shard_map/ppermute | solution.py:235
  136.4 2.9 %collective-permute-start.10 = (bf16[4,152,256]{2,1,0:T(8,128)(2,1)S(1)}, bf16[4,152,256]{2,1,0:T(8,128)(2,1)S(1)}, u32[]{:S(2)}, u32[]{:S(2)}) collective-permute-start(bf16[4,152,256]{2,1,0:T(8,128)(2,1)S(1)} %pad_maximum_fusion.rest_0_), channel_id=1, source_target_pairs={{0,8},{1,9},{2,10},{3,11},{4,12},{5,13},{6,14},{7,15},{8,0},{9,1},... | collective-permute-start | bytes 933896 | tf_op jit(solution)/shard_map/ppermute | solution.py:235
  141.9 3.9 %collective-permute-done.10.rest_2_ = bf16[4,152,256]{2,1,0:T(8,128)(2,1)S(1)} collective-permute-done((bf16[4,152,256]{2,1,0:T(8,128)(2,1)S(1)}, bf16[4,152,256]{2,1,0:T(8,128)(2,1)S(1)}, u32[]{:S(2)}, u32[]{:S(2)}) %collective-permute-start.10) | collective-permute-done | bytes 311328 | tf_op jit(solution)/shard_map/ppermute | solution.py:235
  145.8 3.3 %collective-permute-done.9.rest_1_ = bf16[4,152,256]{2,1,0:T(8,128)(2,1)S(1)} collective-permute-done((bf16[4,152,256]{2,1,0:T(8,128)(2,1)S(1)}, bf16[4,152,256]{2,1,0:T(8,128)(2,1)S(1)}, u32[]{:S(2)}, u32[]{:S(2)}) %collective-permute-start.9) | collective-permute-done | bytes 311328 | tf_op jit(solution)/shard_map/ppermute | solution.py:235
  150.6 18.8 %all-to-all-done.3.returned = bf16[32,24,128]{2,1,0:T(8,128)(2,1)S(1)} async-done(((bf16[32,24,128]{2,1,0:T(8,128)(2,1)}), bf16[32,24,128]{2,1,0:T(8,128)(2,1)S(1)}, u32[]{:S(2)}, u32[]{:S(2)}) %all-to-all-start.3) | async-done | bytes 196640 | tf_op jit(solution)/shard_map/all_to_all | solution.py:346
  (49 shorter events, 26.8 us)
Async XLA Ops:
  2.1 64.7 %all-to-all-start = ((bf16[32,24,128]{2,1,0:T(8,128)(2,1)}), bf16[32,24,128]{2,1,0:T(8,128)(2,1)S(1)}, u32[]{:S(2)}, u32[]{:S(2)}) async-start(bf16[32,24,128]{2,1,0:T(8,128)(2,1)} %get-tuple-element.50), calls=%async_computation | async-start | bytes 393216 | tf_op jit(solution)/shard_map/all_to_all | solution.py:278
  35.6 35.4 %copy-start.2 = (bf16[1,1216,448]{1,2,0:T(8,128)(2,1)S(1)}, bf16[1,1216,448]{1,2,0:T(8,128)(2,1)}, u32[]{:S(2)}) copy-start(bf16[1,1216,448]{1,2,0:T(8,128)(2,1)} %param.15) | copy-start | bytes 3268612
  35.6 10.9 %collective-permute-start = (bf16[4,152,256]{2,1,0:T(8,128)(2,1)S(1)}, bf16[4,152,256]{2,1,0:T(8,128)(2,1)S(1)}, u32[]{:S(2)}, u32[]{:S(2)}) collective-permute-start(bf16[4,152,256]{2,1,0:T(8,128)(2,1)S(1)} %get-tuple-element.53), channel_id=1, source_target_pairs={{0,4},{1,5},{2,6},{3,7},{4,8},{5,9},{6,10},{7,11},{8,12},{9,13},{1... | collective-permute-start | bytes 933896 | tf_op jit(solution)/shard_map/ppermute | solution.py:235
  39.0 10.5 %collective-permute-start.1 = (bf16[4,152,256]{2,1,0:T(8,128)(2,1)S(1)}, bf16[4,152,256]{2,1,0:T(8,128)(2,1)S(1)}, u32[]{:S(2)}, u32[]{:S(2)}) collective-permute-start(bf16[4,152,256]{2,1,0:T(8,128)(2,1)S(1)} %get-tuple-element.54), channel_id=1, source_target_pairs={{0,8},{1,9},{2,10},{3,11},{4,12},{5,13},{6,14},{7,15},{8,0},{9,1},... | collective-permute-start | bytes 933896 | tf_op jit(solution)/shard_map/ppermute | solution.py:235
  43.5 7.9 %collective-permute-start.2 = (bf16[4,152,256]{2,1,0:T(8,128)(2,1)S(1)}, bf16[4,152,256]{2,1,0:T(8,128)(2,1)S(1)}, u32[]{:S(2)}, u32[]{:S(2)}) collective-permute-start(bf16[4,152,256]{2,1,0:T(8,128)(2,1)S(1)} %get-tuple-element.55), channel_id=1, source_target_pairs={{0,12},{1,13},{2,14},{3,15},{4,0},{5,1},{6,2},{7,3},{8,4},{9,5},{1... | collective-permute-start | bytes 933896 | tf_op jit(solution)/shard_map/ppermute | solution.py:235
  52.7 20.2 %copy-start.12 = (bf16[152,256]{1,0:T(8,128)(2,1)}, bf16[152,256]{1,0:T(8,128)(2,1)S(1)}, u32[]{:S(2)}) copy-start(bf16[152,256]{1,0:T(8,128)(2,1)S(1)} %get-tuple-element.69) | copy-start | bytes 233476
  73.0 17.6 %copy-start.3 = (bf16[1,448,1216]{2,1,0:T(8,128)(2,1)S(1)}, bf16[1,448,1216]{2,1,0:T(8,128)(2,1)}, u32[]{:S(2)}) copy-start(bf16[1,448,1216]{2,1,0:T(8,128)(2,1)} %param.16) | copy-start | bytes 3268612
  73.0 24.7 %all-to-all-start.1 = ((bf16[16,76,384]{2,1,0:T(8,128)(2,1)}), bf16[16,76,384]{2,1,0:T(8,128)(2,1)S(1)}, u32[]{:S(2)}, u32[]{:S(2)}) async-start(bf16[16,76,384]{2,1,0:T(8,128)(2,1)} %shard_map.94), calls=%async_computation.1 | async-start | bytes 1966080 | tf_op jit(solution)/shard_map/all_to_all | solution.py:308
  79.9 14.2 %collective-permute-start.3 = (bf16[152,256]{1,0:T(8,128)(2,1)}, bf16[152,256]{1,0:T(8,128)(2,1)S(1)}, u32[]{:S(2)}, u32[]{:S(2)}) collective-permute-start(bf16[152,256]{1,0:T(8,128)(2,1)} %get-tuple-element.67), channel_id=1, source_target_pairs={{0,1},{1,2},{2,3},{3,0},{4,5},{5,6},{6,7},{7,4},{8,9},{9,10},{10,1... | collective-permute-start | bytes 233480 | tf_op jit(solution)/shard_map/ppermute | solution.py:235
  83.2 13.2 %collective-permute-start.4 = (bf16[152,256]{1,0:T(8,128)(2,1)}, bf16[152,256]{1,0:T(8,128)(2,1)S(1)}, u32[]{:S(2)}, u32[]{:S(2)}) collective-permute-start(bf16[152,256]{1,0:T(8,128)(2,1)} %get-tuple-element.68), channel_id=1, source_target_pairs={{0,2},{1,3},{2,0},{3,1},{4,6},{5,7},{6,4},{7,5},{8,10},{9,11},{10,... | collective-permute-start | bytes 233480 | tf_op jit(solution)/shard_map/ppermute | solution.py:235
  87.5 9.6 %collective-permute-start.5 = (bf16[152,256]{1,0:T(8,128)(2,1)}, bf16[152,256]{1,0:T(8,128)(2,1)S(1)}, u32[]{:S(2)}, u32[]{:S(2)}) collective-permute-start(bf16[152,256]{1,0:T(8,128)(2,1)} %copy-done.12), channel_id=1, source_target_pairs={{0,3},{1,0},{2,1},{3,2},{4,7},{5,4},{6,5},{7,6},{8,11},{9,8},{10,9... | collective-permute-start | bytes 233480 | tf_op jit(solution)/shard_map/ppermute | solution.py:235
  99.8 4.3 %copy-start.6 = (bf16[256,152]{0,1:T(8,128)(2,1)S(1)}, bf16[256,152]{0,1:T(8,128)(2,1)}, u32[]{:S(2)}) copy-start(bf16[256,152]{0,1:T(8,128)(2,1)} %param.14) | copy-start | bytes 233476
  99.8 4.3 %copy-start.8 = (bf16[152,256]{1,0:T(8,128)(2,1)S(1)}, bf16[152,256]{1,0:T(8,128)(2,1)}, u32[]{:S(2)}) copy-start(bf16[152,256]{1,0:T(8,128)(2,1)} %copy-done.7) | copy-start | bytes 233476
  99.8 4.3 %copy-start.10 = (bf16[152,256]{1,0:T(8,128)(2,1)S(1)}, bf16[152,256]{1,0:T(8,128)(2,1)}, u32[]{:S(2)}) copy-start(bf16[152,256]{1,0:T(8,128)(2,1)} %copy-done.9) | copy-start | bytes 233476
  99.8 19.8 %all-to-all-start.2 = ((bf16[16,76,384]{2,1,0:T(8,128)(2,1)}), bf16[16,76,384]{2,1,0:T(8,128)(2,1)S(1)}, u32[]{:S(2)}, u32[]{:S(2)}) async-start(bf16[16,76,384]{2,1,0:T(8,128)(2,1)} %shard_map.96), calls=%async_computation.2 | async-start | bytes 1966080 | tf_op jit(solution)/shard_map/all_to_all | solution.py:327
  104.2 13.2 %collective-permute-start.8 = (bf16[152,256]{1,0:T(8,128)(2,1)S(1)}, bf16[152,256]{1,0:T(8,128)(2,1)S(1)}, u32[]{:S(2)}, u32[]{:S(2)}) collective-permute-start(bf16[152,256]{1,0:T(8,128)(2,1)S(1)} %shard_map.97), channel_id=1, source_target_pairs={{0,3},{1,0},{2,1},{3,2},{4,7},{5,4},{6,5},{7,6},{8,11},{9,8},{10,9... | collective-permute-start | bytes 233480 | tf_op jit(solution)/shard_map/ppermute | solution.py:235
  108.7 9.9 %collective-permute-start.7 = (bf16[152,256]{1,0:T(8,128)(2,1)S(1)}, bf16[152,256]{1,0:T(8,128)(2,1)S(1)}, u32[]{:S(2)}, u32[]{:S(2)}) collective-permute-start(bf16[152,256]{1,0:T(8,128)(2,1)S(1)} %shard_map.97), channel_id=1, source_target_pairs={{0,2},{1,3},{2,0},{3,1},{4,6},{5,7},{6,4},{7,5},{8,10},{9,11},{10,... | collective-permute-start | bytes 233480 | tf_op jit(solution)/shard_map/ppermute | solution.py:235
  111.2 8.4 %collective-permute-start.6 = (bf16[152,256]{1,0:T(8,128)(2,1)S(1)}, bf16[152,256]{1,0:T(8,128)(2,1)S(1)}, u32[]{:S(2)}, u32[]{:S(2)}) collective-permute-start(bf16[152,256]{1,0:T(8,128)(2,1)S(1)} %shard_map.97), channel_id=1, source_target_pairs={{0,1},{1,2},{2,3},{3,0},{4,5},{5,6},{6,7},{7,4},{8,9},{9,10},{10,1... | collective-permute-start | bytes 233480 | tf_op jit(solution)/shard_map/ppermute | solution.py:235
  120.4 28.8 %copy-start.1 = (bf16[448,2432]{1,0:T(8,128)(2,1)S(1)}, bf16[448,2432]{1,0:T(8,128)(2,1)}, u32[]{:S(2)}) copy-start(bf16[448,2432]{1,0:T(8,128)(2,1)} %rest_4_.1) | copy-start | bytes 6537220
  127.0 42.4 %all-to-all-start.3 = ((bf16[32,24,128]{2,1,0:T(8,128)(2,1)}), bf16[32,24,128]{2,1,0:T(8,128)(2,1)S(1)}, u32[]{:S(2)}, u32[]{:S(2)}) async-start(bf16[32,24,128]{2,1,0:T(8,128)(2,1)} %shard_map.99), calls=%async_computation.3 | async-start | bytes 393216 | tf_op jit(solution)/shard_map/all_to_all | solution.py:346
  133.8 35.6 %copy-start.5 = (bf16[256,256]{1,0:T(8,128)(2,1)S(1)}, bf16[256,256]{1,0:T(8,128)(2,1)}, u32[]{:S(2)}) copy-start(bf16[256,256]{1,0:T(8,128)(2,1)} %get-tuple-element.88.chooser) | copy-start | bytes 393220
  133.8 8.1 %collective-permute-start.11 = (bf16[4,152,256]{2,1,0:T(8,128)(2,1)S(1)}, bf16[4,152,256]{2,1,0:T(8,128)(2,1)S(1)}, u32[]{:S(2)}, u32[]{:S(2)}) collective-permute-start(bf16[4,152,256]{2,1,0:T(8,128)(2,1)S(1)} %pad_maximum_fusion.rest_0_), channel_id=1, source_target_pairs={{0,12},{1,13},{2,14},{3,15},{4,0},{5,1},{6,2},{7,3},{8,4},{9,5},{1... | collective-permute-start | bytes 933896 | tf_op jit(solution)/shard_map/ppermute | solution.py:235
  136.4 9.4 %collective-permute-start.10 = (bf16[4,152,256]{2,1,0:T(8,128)(2,1)S(1)}, bf16[4,152,256]{2,1,0:T(8,128)(2,1)S(1)}, u32[]{:S(2)}, u32[]{:S(2)}) collective-permute-start(bf16[4,152,256]{2,1,0:T(8,128)(2,1)S(1)} %pad_maximum_fusion.rest_0_), channel_id=1, source_target_pairs={{0,8},{1,9},{2,10},{3,11},{4,12},{5,13},{6,14},{7,15},{8,0},{9,1},... | collective-permute-start | bytes 933896 | tf_op jit(solution)/shard_map/ppermute | solution.py:235
  139.3 9.9 %collective-permute-start.9 = (bf16[4,152,256]{2,1,0:T(8,128)(2,1)S(1)}, bf16[4,152,256]{2,1,0:T(8,128)(2,1)S(1)}, u32[]{:S(2)}, u32[]{:S(2)}) collective-permute-start(bf16[4,152,256]{2,1,0:T(8,128)(2,1)S(1)} %pad_maximum_fusion.rest_0_), channel_id=1, source_target_pairs={{0,4},{1,5},{2,6},{3,7},{4,8},{5,9},{6,10},{7,11},{8,12},{9,13},{1... | collective-permute-start | bytes 933896 | tf_op jit(solution)/shard_map/ppermute | solution.py:235
  (5 other events, 4.7 us)

commit v5 on v4

--- a/solution.py
+++ b/solution.py
@@ -306,14 +306,15 @@
     )
     mid, sums, up = lax.optimization_barrier((mid, sums, expert_up[0]))
     shares = lax.all_to_all(mid, tensor, 0, 0, tiled=True)
-    pieces = [sums[0]] + [moved(sums[step], 1, step, along) for step in steps]
     up = call(
         hold_kernel,
         jax.ShapeDtypeStruct((width, half), BF16),
         up,
         scratch=[pltpu.SemaphoreType.DMA],
         spaces=[pltpu.HBM],
-    )
+        room=2,
+    )
+    pieces = [sums[0]] + [moved(sums[step], 1, step, along) for step in steps]
     shares, pieces, up = lax.optimization_barrier((shares, pieces, up))
     copies = call(
         gate_kernel,
@@ -325,9 +326,7 @@
     )
     copies, pieces = lax.optimization_barrier((copies, pieces))
     full = lax.all_to_all(copies, tensor, 0, 0, tiled=True)
-    hidden = call(dense_gate_kernel, piece_bf16, *pieces, dense_act.T)
-    columns = [hidden] + [moved(hidden, 1, step, along) for step in steps]
-    full, columns = lax.optimization_barrier((full, columns))
+    full, pieces = lax.optimization_barrier((full, pieces))
     rows_t = call(
         up_kernel,
         jax.ShapeDtypeStruct((width, slots), BF16),
@@ -342,8 +341,10 @@
         lax.all_gather(rows_t, "c", axis=0, tiled=False),
         spaces=[smem, vmem],
     )
-    back, columns = lax.optimization_barrier((back, columns))
+    back, pieces = lax.optimization_barrier((back, pieces))
     returned = lax.all_to_all(back, "z", 0, 0, tiled=True)
+    hidden = call(dense_gate_kernel, piece_bf16, *pieces, dense_act.T)
+    columns = [hidden] + [moved(hidden, 1, step, along) for step in steps]
     column = jnp.stack(columns)
     dense_t = call(
         dense_up_kernel,

time: 171 us -> 170 us (level)
  blocking collectives: 9.62 us -> 27.4 us
  waiting for transfers between devices: 57.3 us -> 43.2 us
  starting transfers between devices: 85.5 us -> 79.9 us
    all_to_all x0 -> x1, blocking collectives: none -> 18.1 us  [shards(): full = lax.all_to_all(copies, tensor, 0, 0, tiled=True)]
    all_to_all x1, waiting for transfers between devices: 18.8 us -> 6.66 us  [shards(): returned = lax.all_to_all(back, 'z', 0, 0, tiled=True)]
    all_to_all x1 -> x0, starting transfers between devices: 4.23 us -> none  [shards(): full = lax.all_to_all(copies, tensor, 0, 0, tiled=True)]
    ppermute x12, waiting for transfers between devices: 24.4 us -> 22.4 us  [moved(): return lax.ppermute(value, ('c', 'x', 'y'), pairs)]
  transfers between devices with their start and end apart: 16 -> 15, of which waited for: 12 -> 10; matrix products, arithmetic and copies ran while one was open for 0% -> 0% of each run, Pallas kernels for 3% -> 3%
where the time goes in v5:
time: 170 us; the launch traced here: 169 us
  starting transfers between devices  79.9 us (47%)
  waiting for transfers between devices  43.2 us (25%)
  blocking collectives  27.4 us (16%)
  Pallas kernels  13.1 us (8%)
  local copies, waits for them, and re-layouts  4.68 us (3%)
    ppermute x12, starting transfers between devices, moved(): return lax.ppermute(value, ('c', 'x', 'y'), pairs)  37 us
    all_to_all x1, starting transfers between devices, shards(): arrived = lax.all_to_all(message, 'z', 0, 0, tiled=True)  29.3 us
    ppermute x12, waiting for transfers between devices, moved(): return lax.ppermute(value, ('c', 'x', 'y'), pairs)  22.4 us
    all_to_all x1, blocking collectives, shards(): full = lax.all_to_all(copies, tensor, 0, 0, tiled=True)  18.1 us
    all_to_all x1, waiting for transfers between devices, shards(): arrived = lax.all_to_all(message, 'z', 0, 0, tiled=True)  14.1 us
    pallas_call x11, Pallas kernels, call(): pl.pallas_call(kernel, out_shape=outs, in_specs=[pl.BlockSpec(memory_spac...  13.1 us
    all_to_all x1, starting transfers between devices, shards(): shares = lax.all_to_all(mid, tensor, 0, 0, tiled=True)  6.9 us
    all_to_all x1, starting transfers between devices, shards(): returned = lax.all_to_all(back, 'z', 0, 0, tiled=True)  6.72 us
  transfers between devices with their start and end apart: 15, of which 10 were waited for; matrix products, arithmetic and copies ran while one was open for 0% of the time, Pallas kernels for 3%

profile of v5, /device:TPU:1, one launch (start us, length us, event | category | flops | bytes accessed | tf_op | source)
XLA Modules:
  0.0 168.7 jit_solution(7913654657375554040)
XLA Ops:
  2.1 29.3 %all-to-all-start = ((bf16[32,24,128]{2,1,0:T(8,128)(2,1)}), bf16[32,24,128]{2,1,0:T(8,128)(2,1)S(1)}, u32[]{:S(2)}, u32[]{:S(2)}) async-start(bf16[32,24,128]{2,1,0:T(8,128)(2,1)} %get-tuple-element.50), calls=%async_computation | async-start | bytes 393216 | tf_op jit(solution)/shard_map/all_to_all | solution.py:278
  35.6 3.3 %collective-permute-start = (bf16[4,152,256]{2,1,0:T(8,128)(2,1)S(1)}, bf16[4,152,256]{2,1,0:T(8,128)(2,1)S(1)}, u32[]{:S(2)}, u32[]{:S(2)}) collective-permute-start(bf16[4,152,256]{2,1,0:T(8,128)(2,1)S(1)} %get-tuple-element.53), channel_id=1, source_target_pairs={{0,4},{1,5},{2,6},{3,7},{4,8},{5,9},{6,10},{7,11},{8,12},{9,13},{1... | collective-permute-start | bytes 933896 | tf_op jit(solution)/shard_map/ppermute | solution.py:235
  39.0 4.5 %collective-permute-start.1 = (bf16[4,152,256]{2,1,0:T(8,128)(2,1)S(1)}, bf16[4,152,256]{2,1,0:T(8,128)(2,1)S(1)}, u32[]{:S(2)}, u32[]{:S(2)}) collective-permute-start(bf16[4,152,256]{2,1,0:T(8,128)(2,1)S(1)} %get-tuple-element.54), channel_id=1, source_target_pairs={{0,8},{1,9},{2,10},{3,11},{4,12},{5,13},{6,14},{7,15},{8,0},{9,1},... | collective-permute-start | bytes 933896 | tf_op jit(solution)/shard_map/ppermute | solution.py:235
  43.5 3.0 %collective-permute-start.2 = (bf16[4,152,256]{2,1,0:T(8,128)(2,1)S(1)}, bf16[4,152,256]{2,1,0:T(8,128)(2,1)S(1)}, u32[]{:S(2)}, u32[]{:S(2)}) collective-permute-start(bf16[4,152,256]{2,1,0:T(8,128)(2,1)S(1)} %get-tuple-element.55), channel_id=1, source_target_pairs={{0,12},{1,13},{2,14},{3,15},{4,0},{5,1},{6,2},{7,3},{8,4},{9,5},{1... | collective-permute-start | bytes 933896 | tf_op jit(solution)/shard_map/ppermute | solution.py:235
  46.5 3.0 %collective-permute-done.1.rest_2_ = bf16[4,152,256]{2,1,0:T(8,128)(2,1)S(1)} collective-permute-done((bf16[4,152,256]{2,1,0:T(8,128)(2,1)S(1)}, bf16[4,152,256]{2,1,0:T(8,128)(2,1)S(1)}, u32[]{:S(2)}, u32[]{:S(2)}) %collective-permute-start.1) | collective-permute-done | bytes 311328 | tf_op jit(solution)/shard_map/ppermute | solution.py:235
  52.7 14.1 %all-to-all-done = bf16[32,24,128]{2,1,0:T(8,128)(2,1)S(1)} async-done(((bf16[32,24,128]{2,1,0:T(8,128)(2,1)}), bf16[32,24,128]{2,1,0:T(8,128)(2,1)S(1)}, u32[]{:S(2)}, u32[]{:S(2)}) %all-to-all-start) | async-done | bytes 196640 | tf_op jit(solution)/shard_map/all_to_all | solution.py:278
  66.9 4.1 %all-gather = bf16[64,24,128]{2,1,0:T(8,128)(2,1)S(1)} all-gather(bf16[32,24,128]{2,1,0:T(8,128)(2,1)S(1)} %all-to-all-done), channel_id=2, replica_groups=mesh['z'=32,'c'=2,'x'=4,'y'=4] {'c'}, dimensions={0}, use_global_device_ids=true | all-gather | bytes 589824 | tf_op jit(solution)/shard_map/all_gather | solution.py:302
  73.0 6.9 %all-to-all-start.1 = ((bf16[16,76,384]{2,1,0:T(8,128)(2,1)}), bf16[16,76,384]{2,1,0:T(8,128)(2,1)S(1)}, u32[]{:S(2)}, u32[]{:S(2)}) async-start(bf16[16,76,384]{2,1,0:T(8,128)(2,1)} %shard_map.94), calls=%async_computation.1 | async-start | bytes 1966080 | tf_op jit(solution)/shard_map/all_to_all | solution.py:308
  79.9 3.3 %collective-permute-start.3 = (bf16[152,256]{1,0:T(8,128)(2,1)}, bf16[152,256]{1,0:T(8,128)(2,1)S(1)}, u32[]{:S(2)}, u32[]{:S(2)}) collective-permute-start(bf16[152,256]{1,0:T(8,128)(2,1)} %get-tuple-element.67), channel_id=1, source_target_pairs={{0,1},{1,2},{2,3},{3,0},{4,5},{5,6},{6,7},{7,4},{8,9},{9,10},{10,1... | collective-permute-start | bytes 233480 | tf_op jit(solution)/shard_map/ppermute | solution.py:235
  83.2 4.3 %collective-permute-start.4 = (bf16[152,256]{1,0:T(8,128)(2,1)}, bf16[152,256]{1,0:T(8,128)(2,1)S(1)}, u32[]{:S(2)}, u32[]{:S(2)}) collective-permute-start(bf16[152,256]{1,0:T(8,128)(2,1)} %get-tuple-element.68), channel_id=1, source_target_pairs={{0,2},{1,3},{2,0},{3,1},{4,6},{5,7},{6,4},{7,5},{8,10},{9,11},{10,... | collective-permute-start | bytes 233480 | tf_op jit(solution)/shard_map/ppermute | solution.py:235
  87.5 3.1 %collective-permute-start.5 = (bf16[152,256]{1,0:T(8,128)(2,1)}, bf16[152,256]{1,0:T(8,128)(2,1)S(1)}, u32[]{:S(2)}, u32[]{:S(2)}) collective-permute-start(bf16[152,256]{1,0:T(8,128)(2,1)} %copy-done.12), channel_id=1, source_target_pairs={{0,3},{1,0},{2,1},{3,2},{4,7},{5,4},{6,5},{7,6},{8,11},{9,8},{10,9... | collective-permute-start | bytes 233480 | tf_op jit(solution)/shard_map/ppermute | solution.py:235
  90.8 3.3 %collective-permute-done.3.rest_1_ = bf16[152,256]{1,0:T(8,128)(2,1)S(1)} collective-permute-done((bf16[152,256]{1,0:T(8,128)(2,1)}, bf16[152,256]{1,0:T(8,128)(2,1)S(1)}, u32[]{:S(2)}, u32[]{:S(2)}) %collective-permute-start.3) | collective-permute-done | bytes 77856 | tf_op jit(solution)/shard_map/ppermute | solution.py:235
  94.1 2.3 %collective-permute-done.4.rest_2_ = bf16[152,256]{1,0:T(8,128)(2,1)S(1)} collective-permute-done((bf16[152,256]{1,0:T(8,128)(2,1)}, bf16[152,256]{1,0:T(8,128)(2,1)S(1)}, u32[]{:S(2)}, u32[]{:S(2)}) %collective-permute-start.4) | collective-permute-done | bytes 77856 | tf_op jit(solution)/shard_map/ppermute | solution.py:235
  100.1 18.1 %all_to_all.20.full = bf16[16,76,384]{2,1,0:T(8,128)(2,1)S(1)} all-to-all(bf16[16,76,384]{2,1,0:T(8,128)(2,1)S(1)} %shard_map.96), channel_id=1, replica_groups=mesh['z'=32,'c'=2,'x'=4,'y'=4] {'x','y'}, dimensions={0} | all-to-all | bytes 1867776 | tf_op jit(solution)/shard_map/all_to_all | solution.py:328
  119.0 5.2 %all-gather.1 = bf16[896,384]{1,0:T(8,128)(2,1)S(1)} all-gather(bf16[448,384]{1,0:T(8,128)(2,1)S(1)} %shard_map.97), channel_id=3, replica_groups=mesh['z'=32,'c'=2,'x'=4,'y'=4] {'c'}, dimensions={0}, use_global_device_ids=true | all-gather | bytes 1032192 | tf_op jit(solution)/shard_map/all_gather | solution.py:341
  125.3 6.7 %all-to-all-start.3 = ((bf16[32,24,128]{2,1,0:T(8,128)(2,1)}), bf16[32,24,128]{2,1,0:T(8,128)(2,1)S(1)}, u32[]{:S(2)}, u32[]{:S(2)}) async-start(bf16[32,24,128]{2,1,0:T(8,128)(2,1)} %shard_map.98), calls=%async_computation.3 | async-start | bytes 393216 | tf_op jit(solution)/shard_map/all_to_all | solution.py:345
  132.2 2.8 %collective-permute-start.8 = (bf16[152,256]{1,0:T(8,128)(2,1)S(1)}, bf16[152,256]{1,0:T(8,128)(2,1)S(1)}, u32[]{:S(2)}, u32[]{:S(2)}) collective-permute-start(bf16[152,256]{1,0:T(8,128)(2,1)S(1)} %shard_map.99), channel_id=1, source_target_pairs={{0,3},{1,0},{2,1},{3,2},{4,7},{5,4},{6,5},{7,6},{8,11},{9,8},{10,9... | collective-permute-start | bytes 233480 | tf_op jit(solution)/shard_map/ppermute | solution.py:235
  135.0 2.3 %collective-permute-start.7 = (bf16[152,256]{1,0:T(8,128)(2,1)S(1)}, bf16[152,256]{1,0:T(8,128)(2,1)S(1)}, u32[]{:S(2)}, u32[]{:S(2)}) collective-permute-start(bf16[152,256]{1,0:T(8,128)(2,1)S(1)} %shard_map.99), channel_id=1, source_target_pairs={{0,2},{1,3},{2,0},{3,1},{4,6},{5,7},{6,4},{7,5},{8,10},{9,11},{10,... | collective-permute-start | bytes 233480 | tf_op jit(solution)/shard_map/ppermute | solution.py:235
  139.6 2.3 %collective-permute-done.7 = bf16[152,256]{1,0:T(8,128)(2,1)S(1)} collective-permute-done((bf16[152,256]{1,0:T(8,128)(2,1)S(1)}, bf16[152,256]{1,0:T(8,128)(2,1)S(1)}, u32[]{:S(2)}, u32[]{:S(2)}) %collective-permute-start.7) | collective-permute-done | bytes 77856 | tf_op jit(solution)/shard_map/ppermute | solution.py:235
  144.0 2.8 %collective-permute-start.11 = (bf16[4,152,256]{2,1,0:T(8,128)(2,1)S(1)}, bf16[4,152,256]{2,1,0:T(8,128)(2,1)S(1)}, u32[]{:S(2)}, u32[]{:S(2)}) collective-permute-start(bf16[4,152,256]{2,1,0:T(8,128)(2,1)S(1)} %pad_maximum_fusion.rest_0_), channel_id=1, source_target_pairs={{0,12},{1,13},{2,14},{3,15},{4,0},{5,1},{6,2},{7,3},{8,4},{9,5},{1... | collective-permute-start | bytes 933896 | tf_op jit(solution)/shard_map/ppermute | solution.py:235
  146.8 3.1 %collective-permute-start.10 = (bf16[4,152,256]{2,1,0:T(8,128)(2,1)S(1)}, bf16[4,152,256]{2,1,0:T(8,128)(2,1)S(1)}, u32[]{:S(2)}, u32[]{:S(2)}) collective-permute-start(bf16[4,152,256]{2,1,0:T(8,128)(2,1)S(1)} %pad_maximum_fusion.rest_0_), channel_id=1, source_target_pairs={{0,8},{1,9},{2,10},{3,11},{4,12},{5,13},{6,14},{7,15},{8,0},{9,1},... | collective-permute-start | bytes 933896 | tf_op jit(solution)/shard_map/ppermute | solution.py:235
  152.1 4.1 %collective-permute-done.10.rest_2_ = bf16[4,152,256]{2,1,0:T(8,128)(2,1)S(1)} collective-permute-done((bf16[4,152,256]{2,1,0:T(8,128)(2,1)S(1)}, bf16[4,152,256]{2,1,0:T(8,128)(2,1)S(1)}, u32[]{:S(2)}, u32[]{:S(2)}) %collective-permute-start.10) | collective-permute-done | bytes 311328 | tf_op jit(solution)/shard_map/ppermute | solution.py:235
  156.2 3.3 %collective-permute-done.9.rest_1_ = bf16[4,152,256]{2,1,0:T(8,128)(2,1)S(1)} collective-permute-done((bf16[4,152,256]{2,1,0:T(8,128)(2,1)S(1)}, bf16[4,152,256]{2,1,0:T(8,128)(2,1)S(1)}, u32[]{:S(2)}, u32[]{:S(2)}) %collective-permute-start.9) | collective-permute-done | bytes 311328 | tf_op jit(solution)/shard_map/ppermute | solution.py:235
  161.1 6.7 %all-to-all-done.3.returned = bf16[32,24,128]{2,1,0:T(8,128)(2,1)S(1)} async-done(((bf16[32,24,128]{2,1,0:T(8,128)(2,1)}), bf16[32,24,128]{2,1,0:T(8,128)(2,1)S(1)}, u32[]{:S(2)}, u32[]{:S(2)}) %all-to-all-start.3) | async-done | bytes 196640 | tf_op jit(solution)/shard_map/all_to_all | solution.py:345
  (48 shorter events, 26.4 us)
Async XLA Ops:
  2.1 64.7 %all-to-all-start = ((bf16[32,24,128]{2,1,0:T(8,128)(2,1)}), bf16[32,24,128]{2,1,0:T(8,128)(2,1)S(1)}, u32[]{:S(2)}, u32[]{:S(2)}) async-start(bf16[32,24,128]{2,1,0:T(8,128)(2,1)} %get-tuple-element.50), calls=%async_computation | async-start | bytes 393216 | tf_op jit(solution)/shard_map/all_to_all | solution.py:278
  31.5 1.6 copy-start
  35.6 35.4 %copy-start.2 = (bf16[1,1216,448]{1,2,0:T(8,128)(2,1)S(1)}, bf16[1,1216,448]{1,2,0:T(8,128)(2,1)}, u32[]{:S(2)}) copy-start(bf16[1,1216,448]{1,2,0:T(8,128)(2,1)} %param.15) | copy-start | bytes 3268612
  35.6 10.9 %collective-permute-start = (bf16[4,152,256]{2,1,0:T(8,128)(2,1)S(1)}, bf16[4,152,256]{2,1,0:T(8,128)(2,1)S(1)}, u32[]{:S(2)}, u32[]{:S(2)}) collective-permute-start(bf16[4,152,256]{2,1,0:T(8,128)(2,1)S(1)} %get-tuple-element.53), channel_id=1, source_target_pairs={{0,4},{1,5},{2,6},{3,7},{4,8},{5,9},{6,10},{7,11},{8,12},{9,13},{1... | collective-permute-start | bytes 933896 | tf_op jit(solution)/shard_map/ppermute | solution.py:235
  39.0 10.5 %collective-permute-start.1 = (bf16[4,152,256]{2,1,0:T(8,128)(2,1)S(1)}, bf16[4,152,256]{2,1,0:T(8,128)(2,1)S(1)}, u32[]{:S(2)}, u32[]{:S(2)}) collective-permute-start(bf16[4,152,256]{2,1,0:T(8,128)(2,1)S(1)} %get-tuple-element.54), channel_id=1, source_target_pairs={{0,8},{1,9},{2,10},{3,11},{4,12},{5,13},{6,14},{7,15},{8,0},{9,1},... | collective-permute-start | bytes 933896 | tf_op jit(solution)/shard_map/ppermute | solution.py:235
  43.5 7.9 %collective-permute-start.2 = (bf16[4,152,256]{2,1,0:T(8,128)(2,1)S(1)}, bf16[4,152,256]{2,1,0:T(8,128)(2,1)S(1)}, u32[]{:S(2)}, u32[]{:S(2)}) collective-permute-start(bf16[4,152,256]{2,1,0:T(8,128)(2,1)S(1)} %get-tuple-element.55), channel_id=1, source_target_pairs={{0,12},{1,13},{2,14},{3,15},{4,0},{5,1},{6,2},{7,3},{8,4},{9,5},{1... | collective-permute-start | bytes 933896 | tf_op jit(solution)/shard_map/ppermute | solution.py:235
  52.7 20.2 %copy-start.12 = (bf16[152,256]{1,0:T(8,128)(2,1)}, bf16[152,256]{1,0:T(8,128)(2,1)S(1)}, u32[]{:S(2)}) copy-start(bf16[152,256]{1,0:T(8,128)(2,1)S(1)} %get-tuple-element.69) | copy-start | bytes 233476
  73.0 17.6 %copy-start.3 = (bf16[1,448,1216]{2,1,0:T(8,128)(2,1)S(1)}, bf16[1,448,1216]{2,1,0:T(8,128)(2,1)}, u32[]{:S(2)}) copy-start(bf16[1,448,1216]{2,1,0:T(8,128)(2,1)} %param.16) | copy-start | bytes 3268612
  73.0 24.7 %all-to-all-start.1 = ((bf16[16,76,384]{2,1,0:T(8,128)(2,1)}), bf16[16,76,384]{2,1,0:T(8,128)(2,1)S(1)}, u32[]{:S(2)}, u32[]{:S(2)}) async-start(bf16[16,76,384]{2,1,0:T(8,128)(2,1)} %shard_map.94), calls=%async_computation.1 | async-start | bytes 1966080 | tf_op jit(solution)/shard_map/all_to_all | solution.py:308
  79.9 14.2 %collective-permute-start.3 = (bf16[152,256]{1,0:T(8,128)(2,1)}, bf16[152,256]{1,0:T(8,128)(2,1)S(1)}, u32[]{:S(2)}, u32[]{:S(2)}) collective-permute-start(bf16[152,256]{1,0:T(8,128)(2,1)} %get-tuple-element.67), channel_id=1, source_target_pairs={{0,1},{1,2},{2,3},{3,0},{4,5},{5,6},{6,7},{7,4},{8,9},{9,10},{10,1... | collective-permute-start | bytes 233480 | tf_op jit(solution)/shard_map/ppermute | solution.py:235
  83.2 13.2 %collective-permute-start.4 = (bf16[152,256]{1,0:T(8,128)(2,1)}, bf16[152,256]{1,0:T(8,128)(2,1)S(1)}, u32[]{:S(2)}, u32[]{:S(2)}) collective-permute-start(bf16[152,256]{1,0:T(8,128)(2,1)} %get-tuple-element.68), channel_id=1, source_target_pairs={{0,2},{1,3},{2,0},{3,1},{4,6},{5,7},{6,4},{7,5},{8,10},{9,11},{10,... | collective-permute-start | bytes 233480 | tf_op jit(solution)/shard_map/ppermute | solution.py:235
  87.5 9.6 %collective-permute-start.5 = (bf16[152,256]{1,0:T(8,128)(2,1)}, bf16[152,256]{1,0:T(8,128)(2,1)S(1)}, u32[]{:S(2)}, u32[]{:S(2)}) collective-permute-start(bf16[152,256]{1,0:T(8,128)(2,1)} %copy-done.12), channel_id=1, source_target_pairs={{0,3},{1,0},{2,1},{3,2},{4,7},{5,4},{6,5},{7,6},{8,11},{9,8},{10,9... | collective-permute-start | bytes 233480 | tf_op jit(solution)/shard_map/ppermute | solution.py:235
  119.0 13.1 %copy-start.6 = (bf16[256,152]{0,1:T(8,128)(2,1)S(1)}, bf16[256,152]{0,1:T(8,128)(2,1)}, u32[]{:S(2)}) copy-start(bf16[256,152]{0,1:T(8,128)(2,1)} %param.14) | copy-start | bytes 233476
  119.0 13.1 %copy-start.8 = (bf16[152,256]{1,0:T(8,128)(2,1)S(1)}, bf16[152,256]{1,0:T(8,128)(2,1)}, u32[]{:S(2)}) copy-start(bf16[152,256]{1,0:T(8,128)(2,1)} %copy-done.7) | copy-start | bytes 233476
  119.0 13.1 %copy-start.10 = (bf16[152,256]{1,0:T(8,128)(2,1)S(1)}, bf16[152,256]{1,0:T(8,128)(2,1)}, u32[]{:S(2)}) copy-start(bf16[152,256]{1,0:T(8,128)(2,1)} %copy-done.9) | copy-start | bytes 233476
  124.2 35.3 %copy-start.1 = (bf16[448,2432]{1,0:T(8,128)(2,1)S(1)}, bf16[448,2432]{1,0:T(8,128)(2,1)}, u32[]{:S(2)}) copy-start(bf16[448,2432]{1,0:T(8,128)(2,1)} %rest_4_.1) | copy-start | bytes 6537220
  125.3 42.4 %all-to-all-start.3 = ((bf16[32,24,128]{2,1,0:T(8,128)(2,1)}), bf16[32,24,128]{2,1,0:T(8,128)(2,1)S(1)}, u32[]{:S(2)}, u32[]{:S(2)}) async-start(bf16[32,24,128]{2,1,0:T(8,128)(2,1)} %shard_map.98), calls=%async_computation.3 | async-start | bytes 393216 | tf_op jit(solution)/shard_map/all_to_all | solution.py:345
  132.2 7.4 %collective-permute-start.8 = (bf16[152,256]{1,0:T(8,128)(2,1)S(1)}, bf16[152,256]{1,0:T(8,128)(2,1)S(1)}, u32[]{:S(2)}, u32[]{:S(2)}) collective-permute-start(bf16[152,256]{1,0:T(8,128)(2,1)S(1)} %shard_map.99), channel_id=1, source_target_pairs={{0,3},{1,0},{2,1},{3,2},{4,7},{5,4},{6,5},{7,6},{8,11},{9,8},{10,9... | collective-permute-start | bytes 233480 | tf_op jit(solution)/shard_map/ppermute | solution.py:235
  135.0 6.9 %collective-permute-start.7 = (bf16[152,256]{1,0:T(8,128)(2,1)S(1)}, bf16[152,256]{1,0:T(8,128)(2,1)S(1)}, u32[]{:S(2)}, u32[]{:S(2)}) collective-permute-start(bf16[152,256]{1,0:T(8,128)(2,1)S(1)} %shard_map.99), channel_id=1, source_target_pairs={{0,2},{1,3},{2,0},{3,1},{4,6},{5,7},{6,4},{7,5},{8,10},{9,11},{10,... | collective-permute-start | bytes 233480 | tf_op jit(solution)/shard_map/ppermute | solution.py:235
  137.3 6.6 %collective-permute-start.6 = (bf16[152,256]{1,0:T(8,128)(2,1)S(1)}, bf16[152,256]{1,0:T(8,128)(2,1)S(1)}, u32[]{:S(2)}, u32[]{:S(2)}) collective-permute-start(bf16[152,256]{1,0:T(8,128)(2,1)S(1)} %shard_map.99), channel_id=1, source_target_pairs={{0,1},{1,2},{2,3},{3,0},{4,5},{5,6},{6,7},{7,4},{8,9},{9,10},{10,1... | collective-permute-start | bytes 233480 | tf_op jit(solution)/shard_map/ppermute | solution.py:235
  144.0 23.8 %copy-start.5 = (bf16[256,256]{1,0:T(8,128)(2,1)S(1)}, bf16[256,256]{1,0:T(8,128)(2,1)}, u32[]{:S(2)}) copy-start(bf16[256,256]{1,0:T(8,128)(2,1)} %get-tuple-element.88.chooser) | copy-start | bytes 393220
  144.0 8.1 %collective-permute-start.11 = (bf16[4,152,256]{2,1,0:T(8,128)(2,1)S(1)}, bf16[4,152,256]{2,1,0:T(8,128)(2,1)S(1)}, u32[]{:S(2)}, u32[]{:S(2)}) collective-permute-start(bf16[4,152,256]{2,1,0:T(8,128)(2,1)S(1)} %pad_maximum_fusion.rest_0_), channel_id=1, source_target_pairs={{0,12},{1,13},{2,14},{3,15},{4,0},{5,1},{6,2},{7,3},{8,4},{9,5},{1... | collective-permute-start | bytes 933896 | tf_op jit(solution)/shard_map/ppermute | solution.py:235
  146.8 9.4 %collective-permute-start.10 = (bf16[4,152,256]{2,1,0:T(8,128)(2,1)S(1)}, bf16[4,152,256]{2,1,0:T(8,128)(2,1)S(1)}, u32[]{:S(2)}, u32[]{:S(2)}) collective-permute-start(bf16[4,152,256]{2,1,0:T(8,128)(2,1)S(1)} %pad_maximum_fusion.rest_0_), channel_id=1, source_target_pairs={{0,8},{1,9},{2,10},{3,11},{4,12},{5,13},{6,14},{7,15},{8,0},{9,1},... | collective-permute-start | bytes 933896 | tf_op jit(solution)/shard_map/ppermute | solution.py:235
  149.9 9.6 %collective-permute-start.9 = (bf16[4,152,256]{2,1,0:T(8,128)(2,1)S(1)}, bf16[4,152,256]{2,1,0:T(8,128)(2,1)S(1)}, u32[]{:S(2)}, u32[]{:S(2)}) collective-permute-start(bf16[4,152,256]{2,1,0:T(8,128)(2,1)S(1)} %pad_maximum_fusion.rest_0_), channel_id=1, source_target_pairs={{0,4},{1,5},{2,6},{3,7},{4,8},{5,9},{6,10},{7,11},{8,12},{9,13},{1... | collective-permute-start | bytes 933896 | tf_op jit(solution)/shard_map/ppermute | solution.py:235
  (4 other events, 3.0 us)

commit v6 on v5

--- a/solution.py
+++ b/solution.py
@@ -304,8 +304,20 @@
         scratch=[pltpu.VMEM((parts, piece, slots), BF16), pltpu.SemaphoreType.DMA((parts,))],
         out_space=pltpu.HBM,
     )
-    mid, sums, up = lax.optimization_barrier((mid, sums, expert_up[0]))
+    mid, sums = lax.optimization_barrier((mid, sums))
     shares = lax.all_to_all(mid, tensor, 0, 0, tiled=True)
+    pieces = [sums[0]] + [moved(sums[step], 1, step, along) for step in steps]
+    shares, pieces = lax.optimization_barrier((shares, pieces))
+    copies = call(
+        gate_kernel,
+        parts_out,
+        shares,
+        expert_act[0].T,
+        scratch=[pltpu.VMEM((piece, slots), BF16), pltpu.SemaphoreType.DMA((parts,))],
+        out_space=pltpu.HBM,
+    )
+    copies, pieces, up = lax.optimization_barrier((copies, pieces, expert_up[0]))
+    full = lax.all_to_all(copies, tensor, 0, 0, tiled=True)
     up = call(
         hold_kernel,
         jax.ShapeDtypeStruct((width, half), BF16),
@@ -314,19 +326,7 @@
         spaces=[pltpu.HBM],
         room=2,
     )
-    pieces = [sums[0]] + [moved(sums[step], 1, step, along) for step in steps]
-    shares, pieces, up = lax.optimization_barrier((shares, pieces, up))
-    copies = call(
-        gate_kernel,
-        parts_out,
-        shares,
-        expert_act[0].T,
-        scratch=[pltpu.VMEM((piece, slots), BF16), pltpu.SemaphoreType.DMA((parts,))],
-        out_space=pltpu.HBM,
-    )
-    copies, pieces = lax.optimization_barrier((copies, pieces))
-    full = lax.all_to_all(copies, tensor, 0, 0, tiled=True)
-    full, pieces = lax.optimization_barrier((full, pieces))
+    full, pieces, up = lax.optimization_barrier((full, pieces, up))
     rows_t = call(
         up_kernel,
         jax.ShapeDtypeStruct((width, slots), BF16),

time: 170 us -> 168 us (0.988)
  blocking collectives: 27.4 us -> 9.1 us
  waiting for transfers between devices: 43.2 us -> 58.3 us
  starting transfers between devices: 79.9 us -> 84.2 us
  local copies, waits for them, and re-layouts: 4.68 us -> 2.6 us
    all_to_all x1 -> x0, blocking collectives: 18.1 us -> none  [shards(): full = lax.all_to_all(copies, tensor, 0, 0, tiled=True)]
    all_to_all x0 -> x1, waiting for transfers between devices: none -> 14.4 us  [shards(): full = lax.all_to_all(copies, tensor, 0, 0, tiled=True)]
    all_to_all x0 -> x1, starting transfers between devices: none -> 4.85 us  [shards(): full = lax.all_to_all(copies, tensor, 0, 0, tiled=True)]
    unnamed x26 -> x24, local copies, waits for them, and re-layouts: 4.68 us -> 2.6 us
  transfers between devices with their start and end apart: 15 -> 16, of which waited for: 10 -> 11; matrix products, arithmetic and copies ran while one was open for 0% -> 0% of each run, Pallas kernels for 3% -> 2%
where the time goes in v6:
time: 168 us; the launch traced here: 167 us
  starting transfers between devices  84.2 us (50%)
  waiting for transfers between devices  58.3 us (35%)
  Pallas kernels  12.2 us (7%)
  blocking collectives  9.1 us (5%)
  local copies, waits for them, and re-layouts  2.6 us (2%)
    ppermute x12, starting transfers between devices, moved(): return lax.ppermute(value, ('c', 'x', 'y'), pairs)  37 us
    all_to_all x1, starting transfers between devices, shards(): arrived = lax.all_to_all(message, 'z', 0, 0, tiled=True)  29.3 us
    ppermute x12, waiting for transfers between devices, moved(): return lax.ppermute(value, ('c', 'x', 'y'), pairs)  23 us
    all_to_all x1, waiting for transfers between devices, shards(): arrived = lax.all_to_all(message, 'z', 0, 0, tiled=True)  14.7 us
    all_to_all x1, waiting for transfers between devices, shards(): full = lax.all_to_all(copies, tensor, 0, 0, tiled=True)  14.4 us
    pallas_call x11, Pallas kernels, call(): pl.pallas_call(kernel, out_shape=outs, in_specs=[pl.BlockSpec(memory_spac...  12.2 us
    all_to_all x1, starting transfers between devices, shards(): shares = lax.all_to_all(mid, tensor, 0, 0, tiled=True)  6.9 us
    all_to_all x1, waiting for transfers between devices, shards(): returned = lax.all_to_all(back, 'z', 0, 0, tiled=True)  6.24 us
  transfers between devices with their start and end apart: 16, of which 11 were waited for; matrix products, arithmetic and copies ran while one was open for 0% of the time, Pallas kernels for 2%

profile of v6, /device:TPU:1, one launch (start us, length us, event | category | flops | bytes accessed | tf_op | source)
XLA Modules:
  0.0 166.9 jit_solution(1107349280152061188)
XLA Ops:
  2.1 29.3 %all-to-all-start = ((bf16[32,24,128]{2,1,0:T(8,128)(2,1)}), bf16[32,24,128]{2,1,0:T(8,128)(2,1)S(1)}, u32[]{:S(2)}, u32[]{:S(2)}) async-start(bf16[32,24,128]{2,1,0:T(8,128)(2,1)} %get-tuple-element.50), calls=%async_computation | async-start | bytes 393216 | tf_op jit(solution)/shard_map/all_to_all | solution.py:278
  35.6 3.3 %collective-permute-start = (bf16[4,152,256]{2,1,0:T(8,128)(2,1)S(1)}, bf16[4,152,256]{2,1,0:T(8,128)(2,1)S(1)}, u32[]{:S(2)}, u32[]{:S(2)}) collective-permute-start(bf16[4,152,256]{2,1,0:T(8,128)(2,1)S(1)} %get-tuple-element.53), channel_id=1, source_target_pairs={{0,4},{1,5},{2,6},{3,7},{4,8},{5,9},{6,10},{7,11},{8,12},{9,13},{1... | collective-permute-start | bytes 933896 | tf_op jit(solution)/shard_map/ppermute | solution.py:235
  39.0 4.5 %collective-permute-start.1 = (bf16[4,152,256]{2,1,0:T(8,128)(2,1)S(1)}, bf16[4,152,256]{2,1,0:T(8,128)(2,1)S(1)}, u32[]{:S(2)}, u32[]{:S(2)}) collective-permute-start(bf16[4,152,256]{2,1,0:T(8,128)(2,1)S(1)} %get-tuple-element.54), channel_id=1, source_target_pairs={{0,8},{1,9},{2,10},{3,11},{4,12},{5,13},{6,14},{7,15},{8,0},{9,1},... | collective-permute-start | bytes 933896 | tf_op jit(solution)/shard_map/ppermute | solution.py:235
  43.5 3.0 %collective-permute-start.2 = (bf16[4,152,256]{2,1,0:T(8,128)(2,1)S(1)}, bf16[4,152,256]{2,1,0:T(8,128)(2,1)S(1)}, u32[]{:S(2)}, u32[]{:S(2)}) collective-permute-start(bf16[4,152,256]{2,1,0:T(8,128)(2,1)S(1)} %get-tuple-element.55), channel_id=1, source_target_pairs={{0,12},{1,13},{2,14},{3,15},{4,0},{5,1},{6,2},{7,3},{8,4},{9,5},{1... | collective-permute-start | bytes 933896 | tf_op jit(solution)/shard_map/ppermute | solution.py:235
  46.5 3.0 %collective-permute-done.1.rest_2_ = bf16[4,152,256]{2,1,0:T(8,128)(2,1)S(1)} collective-permute-done((bf16[4,152,256]{2,1,0:T(8,128)(2,1)S(1)}, bf16[4,152,256]{2,1,0:T(8,128)(2,1)S(1)}, u32[]{:S(2)}, u32[]{:S(2)}) %collective-permute-start.1) | collective-permute-done | bytes 311328 | tf_op jit(solution)/shard_map/ppermute | solution.py:235
  52.1 14.7 %all-to-all-done = bf16[32,24,128]{2,1,0:T(8,128)(2,1)S(1)} async-done(((bf16[32,24,128]{2,1,0:T(8,128)(2,1)}), bf16[32,24,128]{2,1,0:T(8,128)(2,1)S(1)}, u32[]{:S(2)}, u32[]{:S(2)}) %all-to-all-start) | async-done | bytes 196640 | tf_op jit(solution)/shard_map/all_to_all | solution.py:278
  66.9 4.1 %all-gather = bf16[64,24,128]{2,1,0:T(8,128)(2,1)S(1)} all-gather(bf16[32,24,128]{2,1,0:T(8,128)(2,1)S(1)} %all-to-all-done), channel_id=2, replica_groups=mesh['z'=32,'c'=2,'x'=4,'y'=4] {'c'}, dimensions={0}, use_global_device_ids=true | all-gather | bytes 589824 | tf_op jit(solution)/shard_map/all_gather | solution.py:302
  73.0 6.9 %all-to-all-start.1 = ((bf16[16,76,384]{2,1,0:T(8,128)(2,1)}), bf16[16,76,384]{2,1,0:T(8,128)(2,1)S(1)}, u32[]{:S(2)}, u32[]{:S(2)}) async-start(bf16[16,76,384]{2,1,0:T(8,128)(2,1)} %shard_map.94), calls=%async_computation.1 | async-start | bytes 1966080 | tf_op jit(solution)/shard_map/all_to_all | solution.py:308
  79.9 3.3 %collective-permute-start.3 = (bf16[152,256]{1,0:T(8,128)(2,1)S(1)}, bf16[152,256]{1,0:T(8,128)(2,1)S(1)}, u32[]{:S(2)}, u32[]{:S(2)}) collective-permute-start(bf16[152,256]{1,0:T(8,128)(2,1)S(1)} %get-tuple-element.67), channel_id=1, source_target_pairs={{0,1},{1,2},{2,3},{3,0},{4,5},{5,6},{6,7},{7,4},{8,9},{9,10},{10,1... | collective-permute-start | bytes 233480 | tf_op jit(solution)/shard_map/ppermute | solution.py:235
  83.2 4.3 %collective-permute-start.4 = (bf16[152,256]{1,0:T(8,128)(2,1)S(1)}, bf16[152,256]{1,0:T(8,128)(2,1)S(1)}, u32[]{:S(2)}, u32[]{:S(2)}) collective-permute-start(bf16[152,256]{1,0:T(8,128)(2,1)S(1)} %get-tuple-element.68), channel_id=1, source_target_pairs={{0,2},{1,3},{2,0},{3,1},{4,6},{5,7},{6,4},{7,5},{8,10},{9,11},{10,... | collective-permute-start | bytes 233480 | tf_op jit(solution)/shard_map/ppermute | solution.py:235
  87.5 3.1 %collective-permute-start.5 = (bf16[152,256]{1,0:T(8,128)(2,1)S(1)}, bf16[152,256]{1,0:T(8,128)(2,1)S(1)}, u32[]{:S(2)}, u32[]{:S(2)}) collective-permute-start(bf16[152,256]{1,0:T(8,128)(2,1)S(1)} %get-tuple-element.69), channel_id=1, source_target_pairs={{0,3},{1,0},{2,1},{3,2},{4,7},{5,4},{6,5},{7,6},{8,11},{9,8},{10,9... | collective-permute-start | bytes 233480 | tf_op jit(solution)/shard_map/ppermute | solution.py:235
  90.6 3.5 %collective-permute-done.3.rest_1_ = bf16[152,256]{1,0:T(8,128)(2,1)S(1)} collective-permute-done((bf16[152,256]{1,0:T(8,128)(2,1)S(1)}, bf16[152,256]{1,0:T(8,128)(2,1)S(1)}, u32[]{:S(2)}, u32[]{:S(2)}) %collective-permute-start.3) | collective-permute-done | bytes 77856 | tf_op jit(solution)/shard_map/ppermute | solution.py:235
  97.7 4.9 %all-to-all-start.2 = ((bf16[16,76,384]{2,1,0:T(8,128)(2,1)}), bf16[16,76,384]{2,1,0:T(8,128)(2,1)S(1)}, u32[]{:S(2)}, u32[]{:S(2)}) async-start(bf16[16,76,384]{2,1,0:T(8,128)(2,1)} %shard_map.95), calls=%async_computation.2 | async-start | bytes 1966080 | tf_op jit(solution)/shard_map/all_to_all | solution.py:320
  102.8 14.4 %all-to-all-done.2.full = bf16[16,76,384]{2,1,0:T(8,128)(2,1)S(1)} async-done(((bf16[16,76,384]{2,1,0:T(8,128)(2,1)}), bf16[16,76,384]{2,1,0:T(8,128)(2,1)S(1)}, u32[]{:S(2)}, u32[]{:S(2)}) %all-to-all-start.2) | async-done | bytes 933920 | tf_op jit(solution)/shard_map/all_to_all | solution.py:320
  118.0 5.0 %all-gather.1 = bf16[896,384]{1,0:T(8,128)(2,1)S(1)} all-gather(bf16[448,384]{1,0:T(8,128)(2,1)S(1)} %shard_map.97), channel_id=3, replica_groups=mesh['z'=32,'c'=2,'x'=4,'y'=4] {'c'}, dimensions={0}, use_global_device_ids=true | all-gather | bytes 1032192 | tf_op jit(solution)/shard_map/all_gather | solution.py:341
  124.1 6.2 %all-to-all-start.3 = ((bf16[32,24,128]{2,1,0:T(8,128)(2,1)}), bf16[32,24,128]{2,1,0:T(8,128)(2,1)S(1)}, u32[]{:S(2)}, u32[]{:S(2)}) async-start(bf16[32,24,128]{2,1,0:T(8,128)(2,1)} %shard_map.98), calls=%async_computation.3 | async-start | bytes 393216 | tf_op jit(solution)/shard_map/all_to_all | solution.py:345
  130.4 2.7 %collective-permute-start.8 = (bf16[152,256]{1,0:T(8,128)(2,1)S(1)}, bf16[152,256]{1,0:T(8,128)(2,1)S(1)}, u32[]{:S(2)}, u32[]{:S(2)}) collective-permute-start(bf16[152,256]{1,0:T(8,128)(2,1)S(1)} %shard_map.99), channel_id=1, source_target_pairs={{0,3},{1,0},{2,1},{3,2},{4,7},{5,4},{6,5},{7,6},{8,11},{9,8},{10,9... | collective-permute-start | bytes 233480 | tf_op jit(solution)/shard_map/ppermute | solution.py:235
  133.0 2.6 %collective-permute-start.7 = (bf16[152,256]{1,0:T(8,128)(2,1)S(1)}, bf16[152,256]{1,0:T(8,128)(2,1)S(1)}, u32[]{:S(2)}, u32[]{:S(2)}) collective-permute-start(bf16[152,256]{1,0:T(8,128)(2,1)S(1)} %shard_map.99), channel_id=1, source_target_pairs={{0,2},{1,3},{2,0},{3,1},{4,6},{5,7},{6,4},{7,5},{8,10},{9,11},{10,... | collective-permute-start | bytes 233480 | tf_op jit(solution)/shard_map/ppermute | solution.py:235
  140.0 2.4 %collective-permute-done.6 = bf16[152,256]{1,0:T(8,128)(2,1)S(1)} collective-permute-done((bf16[152,256]{1,0:T(8,128)(2,1)S(1)}, bf16[152,256]{1,0:T(8,128)(2,1)S(1)}, u32[]{:S(2)}, u32[]{:S(2)}) %collective-permute-start.6) | collective-permute-done | bytes 77856 | tf_op jit(solution)/shard_map/ppermute | solution.py:235
  142.4 3.0 %collective-permute-start.11 = (bf16[4,152,256]{2,1,0:T(8,128)(2,1)S(1)}, bf16[4,152,256]{2,1,0:T(8,128)(2,1)S(1)}, u32[]{:S(2)}, u32[]{:S(2)}) collective-permute-start(bf16[4,152,256]{2,1,0:T(8,128)(2,1)S(1)} %pad_maximum_fusion.rest_0_), channel_id=1, source_target_pairs={{0,12},{1,13},{2,14},{3,15},{4,0},{5,1},{6,2},{7,3},{8,4},{9,5},{1... | collective-permute-start | bytes 933896 | tf_op jit(solution)/shard_map/ppermute | solution.py:235
  145.4 3.0 %collective-permute-start.10 = (bf16[4,152,256]{2,1,0:T(8,128)(2,1)S(1)}, bf16[4,152,256]{2,1,0:T(8,128)(2,1)S(1)}, u32[]{:S(2)}, u32[]{:S(2)}) collective-permute-start(bf16[4,152,256]{2,1,0:T(8,128)(2,1)S(1)} %pad_maximum_fusion.rest_0_), channel_id=1, source_target_pairs={{0,8},{1,9},{2,10},{3,11},{4,12},{5,13},{6,14},{7,15},{8,0},{9,1},... | collective-permute-start | bytes 933896 | tf_op jit(solution)/shard_map/ppermute | solution.py:235
  150.7 4.1 %collective-permute-done.10.rest_2_ = bf16[4,152,256]{2,1,0:T(8,128)(2,1)S(1)} collective-permute-done((bf16[4,152,256]{2,1,0:T(8,128)(2,1)S(1)}, bf16[4,152,256]{2,1,0:T(8,128)(2,1)S(1)}, u32[]{:S(2)}, u32[]{:S(2)}) %collective-permute-start.10) | collective-permute-done | bytes 311328 | tf_op jit(solution)/shard_map/ppermute | solution.py:235
  154.8 3.3 %collective-permute-done.9.rest_1_ = bf16[4,152,256]{2,1,0:T(8,128)(2,1)S(1)} collective-permute-done((bf16[4,152,256]{2,1,0:T(8,128)(2,1)S(1)}, bf16[4,152,256]{2,1,0:T(8,128)(2,1)S(1)}, u32[]{:S(2)}, u32[]{:S(2)}) %collective-permute-start.9) | collective-permute-done | bytes 311328 | tf_op jit(solution)/shard_map/ppermute | solution.py:235
  159.7 6.2 %all-to-all-done.3.returned = bf16[32,24,128]{2,1,0:T(8,128)(2,1)S(1)} async-done(((bf16[32,24,128]{2,1,0:T(8,128)(2,1)}), bf16[32,24,128]{2,1,0:T(8,128)(2,1)S(1)}, u32[]{:S(2)}, u32[]{:S(2)}) %all-to-all-start.3) | async-done | bytes 196640 | tf_op jit(solution)/shard_map/all_to_all | solution.py:345
  (47 shorter events, 25.8 us)
Async XLA Ops:
  2.1 64.7 %all-to-all-start = ((bf16[32,24,128]{2,1,0:T(8,128)(2,1)}), bf16[32,24,128]{2,1,0:T(8,128)(2,1)S(1)}, u32[]{:S(2)}, u32[]{:S(2)}) async-start(bf16[32,24,128]{2,1,0:T(8,128)(2,1)} %get-tuple-element.50), calls=%async_computation | async-start | bytes 393216 | tf_op jit(solution)/shard_map/all_to_all | solution.py:278
  35.6 35.4 %copy-start.2 = (bf16[1,1216,448]{1,2,0:T(8,128)(2,1)S(1)}, bf16[1,1216,448]{1,2,0:T(8,128)(2,1)}, u32[]{:S(2)}) copy-start(bf16[1,1216,448]{1,2,0:T(8,128)(2,1)} %param.15) | copy-start | bytes 3268612
  35.6 10.9 %collective-permute-start = (bf16[4,152,256]{2,1,0:T(8,128)(2,1)S(1)}, bf16[4,152,256]{2,1,0:T(8,128)(2,1)S(1)}, u32[]{:S(2)}, u32[]{:S(2)}) collective-permute-start(bf16[4,152,256]{2,1,0:T(8,128)(2,1)S(1)} %get-tuple-element.53), channel_id=1, source_target_pairs={{0,4},{1,5},{2,6},{3,7},{4,8},{5,9},{6,10},{7,11},{8,12},{9,13},{1... | collective-permute-start | bytes 933896 | tf_op jit(solution)/shard_map/ppermute | solution.py:235
  39.0 10.5 %collective-permute-start.1 = (bf16[4,152,256]{2,1,0:T(8,128)(2,1)S(1)}, bf16[4,152,256]{2,1,0:T(8,128)(2,1)S(1)}, u32[]{:S(2)}, u32[]{:S(2)}) collective-permute-start(bf16[4,152,256]{2,1,0:T(8,128)(2,1)S(1)} %get-tuple-element.54), channel_id=1, source_target_pairs={{0,8},{1,9},{2,10},{3,11},{4,12},{5,13},{6,14},{7,15},{8,0},{9,1},... | collective-permute-start | bytes 933896 | tf_op jit(solution)/shard_map/ppermute | solution.py:235
  43.5 7.9 %collective-permute-start.2 = (bf16[4,152,256]{2,1,0:T(8,128)(2,1)S(1)}, bf16[4,152,256]{2,1,0:T(8,128)(2,1)S(1)}, u32[]{:S(2)}, u32[]{:S(2)}) collective-permute-start(bf16[4,152,256]{2,1,0:T(8,128)(2,1)S(1)} %get-tuple-element.55), channel_id=1, source_target_pairs={{0,12},{1,13},{2,14},{3,15},{4,0},{5,1},{6,2},{7,3},{8,4},{9,5},{1... | collective-permute-start | bytes 933896 | tf_op jit(solution)/shard_map/ppermute | solution.py:235
  73.0 23.5 %copy-start.11 = (bf16[1,384,76]{1,2,0:T(8,128)(2,1)S(1)}, bf16[1,384,76]{1,2,0:T(8,128)(2,1)}, u32[]{:S(2)}) copy-start(bf16[1,384,76]{1,2,0:T(8,128)(2,1)} %param.17) | copy-start | bytes 175108
  73.0 23.4 %all-to-all-start.1 = ((bf16[16,76,384]{2,1,0:T(8,128)(2,1)}), bf16[16,76,384]{2,1,0:T(8,128)(2,1)S(1)}, u32[]{:S(2)}, u32[]{:S(2)}) async-start(bf16[16,76,384]{2,1,0:T(8,128)(2,1)} %shard_map.94), calls=%async_computation.1 | async-start | bytes 1966080 | tf_op jit(solution)/shard_map/all_to_all | solution.py:308
  79.9 14.2 %collective-permute-start.3 = (bf16[152,256]{1,0:T(8,128)(2,1)S(1)}, bf16[152,256]{1,0:T(8,128)(2,1)S(1)}, u32[]{:S(2)}, u32[]{:S(2)}) collective-permute-start(bf16[152,256]{1,0:T(8,128)(2,1)S(1)} %get-tuple-element.67), channel_id=1, source_target_pairs={{0,1},{1,2},{2,3},{3,0},{4,5},{5,6},{6,7},{7,4},{8,9},{9,10},{10,1... | collective-permute-start | bytes 233480 | tf_op jit(solution)/shard_map/ppermute | solution.py:235
  83.2 13.2 %collective-permute-start.4 = (bf16[152,256]{1,0:T(8,128)(2,1)S(1)}, bf16[152,256]{1,0:T(8,128)(2,1)S(1)}, u32[]{:S(2)}, u32[]{:S(2)}) collective-permute-start(bf16[152,256]{1,0:T(8,128)(2,1)S(1)} %get-tuple-element.68), channel_id=1, source_target_pairs={{0,2},{1,3},{2,0},{3,1},{4,6},{5,7},{6,4},{7,5},{8,10},{9,11},{10,... | collective-permute-start | bytes 233480 | tf_op jit(solution)/shard_map/ppermute | solution.py:235
  87.5 8.9 %collective-permute-start.5 = (bf16[152,256]{1,0:T(8,128)(2,1)S(1)}, bf16[152,256]{1,0:T(8,128)(2,1)S(1)}, u32[]{:S(2)}, u32[]{:S(2)}) collective-permute-start(bf16[152,256]{1,0:T(8,128)(2,1)S(1)} %get-tuple-element.69), channel_id=1, source_target_pairs={{0,3},{1,0},{2,1},{3,2},{4,7},{5,4},{6,5},{7,6},{8,11},{9,8},{10,9... | collective-permute-start | bytes 233480 | tf_op jit(solution)/shard_map/ppermute | solution.py:235
  97.7 4.9 %copy-start.3 = (bf16[1,448,1216]{2,1,0:T(8,128)(2,1)S(1)}, bf16[1,448,1216]{2,1,0:T(8,128)(2,1)}, u32[]{:S(2)}) copy-start(bf16[1,448,1216]{2,1,0:T(8,128)(2,1)} %param.16) | copy-start | bytes 3268612
  97.7 19.4 %all-to-all-start.2 = ((bf16[16,76,384]{2,1,0:T(8,128)(2,1)}), bf16[16,76,384]{2,1,0:T(8,128)(2,1)S(1)}, u32[]{:S(2)}, u32[]{:S(2)}) async-start(bf16[16,76,384]{2,1,0:T(8,128)(2,1)} %shard_map.95), calls=%async_computation.2 | async-start | bytes 1966080 | tf_op jit(solution)/shard_map/all_to_all | solution.py:320
  117.9 12.3 %copy-start.6 = (bf16[256,152]{0,1:T(8,128)(2,1)S(1)}, bf16[256,152]{0,1:T(8,128)(2,1)}, u32[]{:S(2)}) copy-start(bf16[256,152]{0,1:T(8,128)(2,1)} %param.14) | copy-start | bytes 233476
  118.0 12.3 %copy-start.8 = (bf16[152,256]{1,0:T(8,128)(2,1)S(1)}, bf16[152,256]{1,0:T(8,128)(2,1)}, u32[]{:S(2)}) copy-start(bf16[152,256]{1,0:T(8,128)(2,1)} %copy-done.7) | copy-start | bytes 233476
  118.0 12.3 %copy-start.10 = (bf16[152,256]{1,0:T(8,128)(2,1)S(1)}, bf16[152,256]{1,0:T(8,128)(2,1)}, u32[]{:S(2)}) copy-start(bf16[152,256]{1,0:T(8,128)(2,1)} %copy-done.9) | copy-start | bytes 233476
  123.0 35.2 %copy-start.1 = (bf16[448,2432]{1,0:T(8,128)(2,1)S(1)}, bf16[448,2432]{1,0:T(8,128)(2,1)}, u32[]{:S(2)}) copy-start(bf16[448,2432]{1,0:T(8,128)(2,1)} %rest_4_.1) | copy-start | bytes 6537220
  124.1 41.8 %all-to-all-start.3 = ((bf16[32,24,128]{2,1,0:T(8,128)(2,1)}), bf16[32,24,128]{2,1,0:T(8,128)(2,1)S(1)}, u32[]{:S(2)}, u32[]{:S(2)}) async-start(bf16[32,24,128]{2,1,0:T(8,128)(2,1)} %shard_map.98), calls=%async_computation.3 | async-start | bytes 393216 | tf_op jit(solution)/shard_map/all_to_all | solution.py:345
  130.4 7.3 %collective-permute-start.8 = (bf16[152,256]{1,0:T(8,128)(2,1)S(1)}, bf16[152,256]{1,0:T(8,128)(2,1)S(1)}, u32[]{:S(2)}, u32[]{:S(2)}) collective-permute-start(bf16[152,256]{1,0:T(8,128)(2,1)S(1)} %shard_map.99), channel_id=1, source_target_pairs={{0,3},{1,0},{2,1},{3,2},{4,7},{5,4},{6,5},{7,6},{8,11},{9,8},{10,9... | collective-permute-start | bytes 233480 | tf_op jit(solution)/shard_map/ppermute | solution.py:235
  133.0 6.9 %collective-permute-start.7 = (bf16[152,256]{1,0:T(8,128)(2,1)S(1)}, bf16[152,256]{1,0:T(8,128)(2,1)S(1)}, u32[]{:S(2)}, u32[]{:S(2)}) collective-permute-start(bf16[152,256]{1,0:T(8,128)(2,1)S(1)} %shard_map.99), channel_id=1, source_target_pairs={{0,2},{1,3},{2,0},{3,1},{4,6},{5,7},{6,4},{7,5},{8,10},{9,11},{10,... | collective-permute-start | bytes 233480 | tf_op jit(solution)/shard_map/ppermute | solution.py:235
  135.7 6.6 %collective-permute-start.6 = (bf16[152,256]{1,0:T(8,128)(2,1)S(1)}, bf16[152,256]{1,0:T(8,128)(2,1)S(1)}, u32[]{:S(2)}, u32[]{:S(2)}) collective-permute-start(bf16[152,256]{1,0:T(8,128)(2,1)S(1)} %shard_map.99), channel_id=1, source_target_pairs={{0,1},{1,2},{2,3},{3,0},{4,5},{5,6},{6,7},{7,4},{8,9},{9,10},{10,1... | collective-permute-start | bytes 233480 | tf_op jit(solution)/shard_map/ppermute | solution.py:235
  142.4 23.5 %copy-start.5 = (bf16[256,256]{1,0:T(8,128)(2,1)S(1)}, bf16[256,256]{1,0:T(8,128)(2,1)}, u32[]{:S(2)}) copy-start(bf16[256,256]{1,0:T(8,128)(2,1)} %get-tuple-element.88.chooser) | copy-start | bytes 393220
  142.4 8.3 %collective-permute-start.11 = (bf16[4,152,256]{2,1,0:T(8,128)(2,1)S(1)}, bf16[4,152,256]{2,1,0:T(8,128)(2,1)S(1)}, u32[]{:S(2)}, u32[]{:S(2)}) collective-permute-start(bf16[4,152,256]{2,1,0:T(8,128)(2,1)S(1)} %pad_maximum_fusion.rest_0_), channel_id=1, source_target_pairs={{0,12},{1,13},{2,14},{3,15},{4,0},{5,1},{6,2},{7,3},{8,4},{9,5},{1... | collective-permute-start | bytes 933896 | tf_op jit(solution)/shard_map/ppermute | solution.py:235
  145.4 9.4 %collective-permute-start.10 = (bf16[4,152,256]{2,1,0:T(8,128)(2,1)S(1)}, bf16[4,152,256]{2,1,0:T(8,128)(2,1)S(1)}, u32[]{:S(2)}, u32[]{:S(2)}) collective-permute-start(bf16[4,152,256]{2,1,0:T(8,128)(2,1)S(1)} %pad_maximum_fusion.rest_0_), channel_id=1, source_target_pairs={{0,8},{1,9},{2,10},{3,11},{4,12},{5,13},{6,14},{7,15},{8,0},{9,1},... | collective-permute-start | bytes 933896 | tf_op jit(solution)/shard_map/ppermute | solution.py:235
  148.4 9.8 %collective-permute-start.9 = (bf16[4,152,256]{2,1,0:T(8,128)(2,1)S(1)}, bf16[4,152,256]{2,1,0:T(8,128)(2,1)S(1)}, u32[]{:S(2)}, u32[]{:S(2)}) collective-permute-start(bf16[4,152,256]{2,1,0:T(8,128)(2,1)S(1)} %pad_maximum_fusion.rest_0_), channel_id=1, source_target_pairs={{0,4},{1,5},{2,6},{3,7},{4,8},{5,9},{6,10},{7,11},{8,12},{9,13},{1... | collective-permute-start | bytes 933896 | tf_op jit(solution)/shard_map/ppermute | solution.py:235
  (4 other events, 5.2 us)

commit v7 on v6

--- a/solution.py
+++ b/solution.py
@@ -285,27 +285,28 @@
         scratch=[blocks],
         spaces=[smem, vmem, vmem],
     )
+    slabs = [slabs[0]] + [moved(slabs[step], 0, step, along) for step in steps]
+    arrived = lax.all_gather(arrived, "c", axis=0, tiled=False)
+    arrived, slabs = lax.optimization_barrier((arrived, slabs))
+
+    parts_out = jax.ShapeDtypeStruct((parts, piece, slots), BF16)
+    mid = call(
+        down_kernel,
+        parts_out,
+        arrived,
+        expert_down[0].T,
+        scratch=[pltpu.VMEM((parts, piece, slots), BF16), pltpu.SemaphoreType.DMA((parts,))],
+        out_space=pltpu.HBM,
+    )
+    mid, slabs = lax.optimization_barrier((mid, slabs))
+    shares = lax.all_to_all(mid, tensor, 0, 0, tiled=True)
     sums = call(
         dense_sum_kernel,
         (piece_f32,) + (piece_bf16,) * (along - 1),
         place,
-        slabs[0],
-        *[moved(slabs[step], 0, step, along) for step in steps],
+        *slabs,
         spaces=[smem] + [vmem] * along,
     )
-    arrived, sums = lax.optimization_barrier((arrived, sums))
-
-    parts_out = jax.ShapeDtypeStruct((parts, piece, slots), BF16)
-    mid = call(
-        down_kernel,
-        parts_out,
-        lax.all_gather(arrived, "c", axis=0, tiled=False),
-        expert_down[0].T,
-        scratch=[pltpu.VMEM((parts, piece, slots), BF16), pltpu.SemaphoreType.DMA((parts,))],
-        out_space=pltpu.HBM,
-    )
-    mid, sums = lax.optimization_barrier((mid, sums))
-    shares = lax.all_to_all(mid, tensor, 0, 0, tiled=True)
     pieces = [sums[0]] + [moved(sums[step], 1, step, along) for step in steps]
     shares, pieces = lax.optimization_barrier((shares, pieces))
     copies = call(

time: 168 us -> 167 us (level)
  starting transfers between devices: 84.2 us -> 82 us
    all_to_all x1, waiting for transfers between devices: 14.7 us -> 20.5 us  [shards(): arrived = lax.all_to_all(message, 'z', 0, 0, tiled=True)]
    ppermute x12, waiting for transfers between devices: 23 us -> 17.2 us  [moved(): return lax.ppermute(value, ('c', 'x', 'y'), pairs)]
    all_to_all x1, starting transfers between devices: 6.16 us -> 3.87 us  [shards(): returned = lax.all_to_all(back, 'z', 0, 0, tiled=True)]
  transfers between devices with their start and end apart: 16 -> 16, of which waited for: 11 -> 9; matrix products, arithmetic and copies ran while one was open for 0% -> 0% of each run, Pallas kernels for 2% -> 2%
where the time goes in v7:
time: 167 us; the launch traced here: 166 us
  starting transfers between devices  82 us (49%)
  waiting for transfers between devices  59 us (35%)
  Pallas kernels  12.2 us (7%)
  blocking collectives  9.32 us (6%)
  local copies, waits for them, and re-layouts  2.6 us (2%)
    ppermute x12, starting transfers between devices, moved(): return lax.ppermute(value, ('c', 'x', 'y'), pairs)  37 us
    all_to_all x1, starting transfers between devices, shards(): arrived = lax.all_to_all(message, 'z', 0, 0, tiled=True)  29.4 us
    all_to_all x1, waiting for transfers between devices, shards(): arrived = lax.all_to_all(message, 'z', 0, 0, tiled=True)  20.5 us
    ppermute x12, waiting for transfers between devices, moved(): return lax.ppermute(value, ('c', 'x', 'y'), pairs)  17.2 us
    all_to_all x1, waiting for transfers between devices, shards(): full = lax.all_to_all(copies, tensor, 0, 0, tiled=True)  14.3 us
    pallas_call x11, Pallas kernels, call(): pl.pallas_call(kernel, out_shape=outs, in_specs=[pl.BlockSpec(memory_spac...  12.2 us
    all_to_all x1, waiting for transfers between devices, shards(): returned = lax.all_to_all(back, 'z', 0, 0, tiled=True)  7 us
    all_to_all x1, starting transfers between devices, shards(): shares = lax.all_to_all(mid, tensor, 0, 0, tiled=True)  6.91 us
  transfers between devices with their start and end apart: 16, of which 9 were waited for; matrix products, arithmetic and copies ran while one was open for 0% of the time, Pallas kernels for 2%

profile of v7, /device:TPU:1, one launch (start us, length us, event | category | flops | bytes accessed | tf_op | source)
XLA Modules:
  0.0 165.6 jit_solution(8902271869951739626)
XLA Ops:
  2.1 29.4 %all-to-all-start = ((bf16[32,24,128]{2,1,0:T(8,128)(2,1)}), bf16[32,24,128]{2,1,0:T(8,128)(2,1)}, u32[]{:S(2)}, u32[]{:S(2)}) async-start(bf16[32,24,128]{2,1,0:T(8,128)(2,1)} %get-tuple-element.50), calls=%async_computation | async-start | bytes 393216 | tf_op jit(solution)/shard_map/all_to_all | solution.py:278
  35.7 3.2 %collective-permute-start = (bf16[4,152,256]{2,1,0:T(8,128)(2,1)S(1)}, bf16[4,152,256]{2,1,0:T(8,128)(2,1)S(1)}, u32[]{:S(2)}, u32[]{:S(2)}) collective-permute-start(bf16[4,152,256]{2,1,0:T(8,128)(2,1)S(1)} %get-tuple-element.53), channel_id=1, source_target_pairs={{0,4},{1,5},{2,6},{3,7},{4,8},{5,9},{6,10},{7,11},{8,12},{9,13},{1... | collective-permute-start | bytes 933896 | tf_op jit(solution)/shard_map/ppermute | solution.py:235
  38.9 4.5 %collective-permute-start.1 = (bf16[4,152,256]{2,1,0:T(8,128)(2,1)S(1)}, bf16[4,152,256]{2,1,0:T(8,128)(2,1)S(1)}, u32[]{:S(2)}, u32[]{:S(2)}) collective-permute-start(bf16[4,152,256]{2,1,0:T(8,128)(2,1)S(1)} %get-tuple-element.54), channel_id=1, source_target_pairs={{0,8},{1,9},{2,10},{3,11},{4,12},{5,13},{6,14},{7,15},{8,0},{9,1},... | collective-permute-start | bytes 933896 | tf_op jit(solution)/shard_map/ppermute | solution.py:235
  43.5 3.0 %collective-permute-start.2 = (bf16[4,152,256]{2,1,0:T(8,128)(2,1)S(1)}, bf16[4,152,256]{2,1,0:T(8,128)(2,1)S(1)}, u32[]{:S(2)}, u32[]{:S(2)}) collective-permute-start(bf16[4,152,256]{2,1,0:T(8,128)(2,1)S(1)} %get-tuple-element.55), channel_id=1, source_target_pairs={{0,12},{1,13},{2,14},{3,15},{4,0},{5,1},{6,2},{7,3},{8,4},{9,5},{1... | collective-permute-start | bytes 933896 | tf_op jit(solution)/shard_map/ppermute | solution.py:235
  46.5 20.5 %all-to-all-done = bf16[32,24,128]{2,1,0:T(8,128)(2,1)} async-done(((bf16[32,24,128]{2,1,0:T(8,128)(2,1)}), bf16[32,24,128]{2,1,0:T(8,128)(2,1)}, u32[]{:S(2)}, u32[]{:S(2)}) %all-to-all-start) | async-done | bytes 196640 | tf_op jit(solution)/shard_map/all_to_all | solution.py:278
  67.0 4.3 %all-gather = bf16[64,24,128]{2,1,0:T(8,128)(2,1)S(1)} all-gather(bf16[32,24,128]{2,1,0:T(8,128)(2,1)} %all-to-all-done), channel_id=2, replica_groups=mesh['z'=32,'c'=2,'x'=4,'y'=4] {'c'}, dimensions={0}, use_global_device_ids=true | all-gather | bytes 589824 | tf_op jit(solution)/shard_map/all_gather | solution.py:289
  73.3 6.9 %all-to-all-start.1 = ((bf16[16,76,384]{2,1,0:T(8,128)(2,1)}), bf16[16,76,384]{2,1,0:T(8,128)(2,1)S(1)}, u32[]{:S(2)}, u32[]{:S(2)}) async-start(bf16[16,76,384]{2,1,0:T(8,128)(2,1)} %shard_map.93), calls=%async_computation.1 | async-start | bytes 1966080 | tf_op jit(solution)/shard_map/all_to_all | solution.py:302
  80.9 3.3 %collective-permute-start.3 = (bf16[152,256]{1,0:T(8,128)(2,1)S(1)}, bf16[152,256]{1,0:T(8,128)(2,1)S(1)}, u32[]{:S(2)}, u32[]{:S(2)}) collective-permute-start(bf16[152,256]{1,0:T(8,128)(2,1)S(1)} %get-tuple-element.67), channel_id=1, source_target_pairs={{0,1},{1,2},{2,3},{3,0},{4,5},{5,6},{6,7},{7,4},{8,9},{9,10},{10,1... | collective-permute-start | bytes 233480 | tf_op jit(solution)/shard_map/ppermute | solution.py:235
  84.2 4.3 %collective-permute-start.4 = (bf16[152,256]{1,0:T(8,128)(2,1)S(1)}, bf16[152,256]{1,0:T(8,128)(2,1)S(1)}, u32[]{:S(2)}, u32[]{:S(2)}) collective-permute-start(bf16[152,256]{1,0:T(8,128)(2,1)S(1)} %get-tuple-element.68), channel_id=1, source_target_pairs={{0,2},{1,3},{2,0},{3,1},{4,6},{5,7},{6,4},{7,5},{8,10},{9,11},{10,... | collective-permute-start | bytes 233480 | tf_op jit(solution)/shard_map/ppermute | solution.py:235
  88.5 3.1 %collective-permute-start.5 = (bf16[152,256]{1,0:T(8,128)(2,1)S(1)}, bf16[152,256]{1,0:T(8,128)(2,1)S(1)}, u32[]{:S(2)}, u32[]{:S(2)}) collective-permute-start(bf16[152,256]{1,0:T(8,128)(2,1)S(1)} %get-tuple-element.69), channel_id=1, source_target_pairs={{0,3},{1,0},{2,1},{3,2},{4,7},{5,4},{6,5},{7,6},{8,11},{9,8},{10,9... | collective-permute-start | bytes 233480 | tf_op jit(solution)/shard_map/ppermute | solution.py:235
  91.6 2.8 %collective-permute-done.3.rest_1_ = bf16[152,256]{1,0:T(8,128)(2,1)S(1)} collective-permute-done((bf16[152,256]{1,0:T(8,128)(2,1)S(1)}, bf16[152,256]{1,0:T(8,128)(2,1)S(1)}, u32[]{:S(2)}, u32[]{:S(2)}) %collective-permute-start.3) | collective-permute-done | bytes 77856 | tf_op jit(solution)/shard_map/ppermute | solution.py:235
  94.4 2.3 %collective-permute-done.4.rest_2_ = bf16[152,256]{1,0:T(8,128)(2,1)S(1)} collective-permute-done((bf16[152,256]{1,0:T(8,128)(2,1)S(1)}, bf16[152,256]{1,0:T(8,128)(2,1)S(1)}, u32[]{:S(2)}, u32[]{:S(2)}) %collective-permute-start.4) | collective-permute-done | bytes 77856 | tf_op jit(solution)/shard_map/ppermute | solution.py:235
  98.1 4.9 %all-to-all-start.2 = ((bf16[16,76,384]{2,1,0:T(8,128)(2,1)}), bf16[16,76,384]{2,1,0:T(8,128)(2,1)S(1)}, u32[]{:S(2)}, u32[]{:S(2)}) async-start(bf16[16,76,384]{2,1,0:T(8,128)(2,1)} %shard_map.95), calls=%async_computation.2 | async-start | bytes 1966080 | tf_op jit(solution)/shard_map/all_to_all | solution.py:321
  103.2 14.3 %all-to-all-done.2.full = bf16[16,76,384]{2,1,0:T(8,128)(2,1)S(1)} async-done(((bf16[16,76,384]{2,1,0:T(8,128)(2,1)}), bf16[16,76,384]{2,1,0:T(8,128)(2,1)S(1)}, u32[]{:S(2)}, u32[]{:S(2)}) %all-to-all-start.2) | async-done | bytes 933920 | tf_op jit(solution)/shard_map/all_to_all | solution.py:321
  118.2 5.0 %all-gather.1 = bf16[896,384]{1,0:T(8,128)(2,1)S(1)} all-gather(bf16[448,384]{1,0:T(8,128)(2,1)S(1)} %shard_map.97), channel_id=3, replica_groups=mesh['z'=32,'c'=2,'x'=4,'y'=4] {'c'}, dimensions={0}, use_global_device_ids=true | all-gather | bytes 1032192 | tf_op jit(solution)/shard_map/all_gather | solution.py:342
  124.3 3.9 %all-to-all-start.3 = ((bf16[32,24,128]{2,1,0:T(8,128)(2,1)}), bf16[32,24,128]{2,1,0:T(8,128)(2,1)S(1)}, u32[]{:S(2)}, u32[]{:S(2)}) async-start(bf16[32,24,128]{2,1,0:T(8,128)(2,1)} %shard_map.98), calls=%async_computation.3 | async-start | bytes 393216 | tf_op jit(solution)/shard_map/all_to_all | solution.py:346
  128.3 2.8 %collective-permute-start.8 = (bf16[152,256]{1,0:T(8,128)(2,1)S(1)}, bf16[152,256]{1,0:T(8,128)(2,1)S(1)}, u32[]{:S(2)}, u32[]{:S(2)}) collective-permute-start(bf16[152,256]{1,0:T(8,128)(2,1)S(1)} %shard_map.99), channel_id=1, source_target_pairs={{0,3},{1,0},{2,1},{3,2},{4,7},{5,4},{6,5},{7,6},{8,11},{9,8},{10,9... | collective-permute-start | bytes 233480 | tf_op jit(solution)/shard_map/ppermute | solution.py:235
  131.1 2.5 %collective-permute-start.7 = (bf16[152,256]{1,0:T(8,128)(2,1)S(1)}, bf16[152,256]{1,0:T(8,128)(2,1)S(1)}, u32[]{:S(2)}, u32[]{:S(2)}) collective-permute-start(bf16[152,256]{1,0:T(8,128)(2,1)S(1)} %shard_map.99), channel_id=1, source_target_pairs={{0,2},{1,3},{2,0},{3,1},{4,6},{5,7},{6,4},{7,5},{8,10},{9,11},{10,... | collective-permute-start | bytes 233480 | tf_op jit(solution)/shard_map/ppermute | solution.py:235
  135.6 2.4 %collective-permute-done.7 = bf16[152,256]{1,0:T(8,128)(2,1)S(1)} collective-permute-done((bf16[152,256]{1,0:T(8,128)(2,1)S(1)}, bf16[152,256]{1,0:T(8,128)(2,1)S(1)}, u32[]{:S(2)}, u32[]{:S(2)}) %collective-permute-start.7) | collective-permute-done | bytes 77856 | tf_op jit(solution)/shard_map/ppermute | solution.py:235
  140.3 3.0 %collective-permute-start.11 = (bf16[4,152,256]{2,1,0:T(8,128)(2,1)S(1)}, bf16[4,152,256]{2,1,0:T(8,128)(2,1)S(1)}, u32[]{:S(2)}, u32[]{:S(2)}) collective-permute-start(bf16[4,152,256]{2,1,0:T(8,128)(2,1)S(1)} %pad_maximum_fusion.rest_0_), channel_id=1, source_target_pairs={{0,12},{1,13},{2,14},{3,15},{4,0},{5,1},{6,2},{7,3},{8,4},{9,5},{1... | collective-permute-start | bytes 933896 | tf_op jit(solution)/shard_map/ppermute | solution.py:235
  143.4 3.0 %collective-permute-start.10 = (bf16[4,152,256]{2,1,0:T(8,128)(2,1)S(1)}, bf16[4,152,256]{2,1,0:T(8,128)(2,1)S(1)}, u32[]{:S(2)}, u32[]{:S(2)}) collective-permute-start(bf16[4,152,256]{2,1,0:T(8,128)(2,1)S(1)} %pad_maximum_fusion.rest_0_), channel_id=1, source_target_pairs={{0,8},{1,9},{2,10},{3,11},{4,12},{5,13},{6,14},{7,15},{8,0},{9,1},... | collective-permute-start | bytes 933896 | tf_op jit(solution)/shard_map/ppermute | solution.py:235
  148.7 4.1 %collective-permute-done.10.rest_2_ = bf16[4,152,256]{2,1,0:T(8,128)(2,1)S(1)} collective-permute-done((bf16[4,152,256]{2,1,0:T(8,128)(2,1)S(1)}, bf16[4,152,256]{2,1,0:T(8,128)(2,1)S(1)}, u32[]{:S(2)}, u32[]{:S(2)}) %collective-permute-start.10) | collective-permute-done | bytes 311328 | tf_op jit(solution)/shard_map/ppermute | solution.py:235
  152.8 3.3 %collective-permute-done.9.rest_1_ = bf16[4,152,256]{2,1,0:T(8,128)(2,1)S(1)} collective-permute-done((bf16[4,152,256]{2,1,0:T(8,128)(2,1)S(1)}, bf16[4,152,256]{2,1,0:T(8,128)(2,1)S(1)}, u32[]{:S(2)}, u32[]{:S(2)}) %collective-permute-start.9) | collective-permute-done | bytes 311328 | tf_op jit(solution)/shard_map/ppermute | solution.py:235
  157.6 7.0 %all-to-all-done.3.returned = bf16[32,24,128]{2,1,0:T(8,128)(2,1)S(1)} async-done(((bf16[32,24,128]{2,1,0:T(8,128)(2,1)}), bf16[32,24,128]{2,1,0:T(8,128)(2,1)S(1)}, u32[]{:S(2)}, u32[]{:S(2)}) %all-to-all-start.3) | async-done | bytes 196640 | tf_op jit(solution)/shard_map/all_to_all | solution.py:346
  (47 shorter events, 21.5 us)
Async XLA Ops:
  2.1 64.8 %all-to-all-start = ((bf16[32,24,128]{2,1,0:T(8,128)(2,1)}), bf16[32,24,128]{2,1,0:T(8,128)(2,1)}, u32[]{:S(2)}, u32[]{:S(2)}) async-start(bf16[32,24,128]{2,1,0:T(8,128)(2,1)} %get-tuple-element.50), calls=%async_computation | async-start | bytes 393216 | tf_op jit(solution)/shard_map/all_to_all | solution.py:278
  34.2 37.1 %copy-start.2 = (bf16[1,1216,448]{1,2,0:T(8,128)(2,1)S(1)}, bf16[1,1216,448]{1,2,0:T(8,128)(2,1)}, u32[]{:S(2)}) copy-start(bf16[1,1216,448]{1,2,0:T(8,128)(2,1)} %param.15) | copy-start | bytes 3268612
  35.7 35.6 %collective-permute-start = (bf16[4,152,256]{2,1,0:T(8,128)(2,1)S(1)}, bf16[4,152,256]{2,1,0:T(8,128)(2,1)S(1)}, u32[]{:S(2)}, u32[]{:S(2)}) collective-permute-start(bf16[4,152,256]{2,1,0:T(8,128)(2,1)S(1)} %get-tuple-element.53), channel_id=1, source_target_pairs={{0,4},{1,5},{2,6},{3,7},{4,8},{5,9},{6,10},{7,11},{8,12},{9,13},{1... | collective-permute-start | bytes 933896 | tf_op jit(solution)/shard_map/ppermute | solution.py:235
  38.9 32.3 %collective-permute-start.1 = (bf16[4,152,256]{2,1,0:T(8,128)(2,1)S(1)}, bf16[4,152,256]{2,1,0:T(8,128)(2,1)S(1)}, u32[]{:S(2)}, u32[]{:S(2)}) collective-permute-start(bf16[4,152,256]{2,1,0:T(8,128)(2,1)S(1)} %get-tuple-element.54), channel_id=1, source_target_pairs={{0,8},{1,9},{2,10},{3,11},{4,12},{5,13},{6,14},{7,15},{8,0},{9,1},... | collective-permute-start | bytes 933896 | tf_op jit(solution)/shard_map/ppermute | solution.py:235
  43.5 27.8 %collective-permute-start.2 = (bf16[4,152,256]{2,1,0:T(8,128)(2,1)S(1)}, bf16[4,152,256]{2,1,0:T(8,128)(2,1)S(1)}, u32[]{:S(2)}, u32[]{:S(2)}) collective-permute-start(bf16[4,152,256]{2,1,0:T(8,128)(2,1)S(1)} %get-tuple-element.55), channel_id=1, source_target_pairs={{0,12},{1,13},{2,14},{3,15},{4,0},{5,1},{6,2},{7,3},{8,4},{9,5},{1... | collective-permute-start | bytes 933896 | tf_op jit(solution)/shard_map/ppermute | solution.py:235
  73.3 23.5 %copy-start.11 = (bf16[1,384,76]{1,2,0:T(8,128)(2,1)S(1)}, bf16[1,384,76]{1,2,0:T(8,128)(2,1)}, u32[]{:S(2)}) copy-start(bf16[1,384,76]{1,2,0:T(8,128)(2,1)} %param.17) | copy-start | bytes 175108
  73.3 23.4 %all-to-all-start.1 = ((bf16[16,76,384]{2,1,0:T(8,128)(2,1)}), bf16[16,76,384]{2,1,0:T(8,128)(2,1)S(1)}, u32[]{:S(2)}, u32[]{:S(2)}) async-start(bf16[16,76,384]{2,1,0:T(8,128)(2,1)} %shard_map.93), calls=%async_computation.1 | async-start | bytes 1966080 | tf_op jit(solution)/shard_map/all_to_all | solution.py:302
  80.9 13.5 %collective-permute-start.3 = (bf16[152,256]{1,0:T(8,128)(2,1)S(1)}, bf16[152,256]{1,0:T(8,128)(2,1)S(1)}, u32[]{:S(2)}, u32[]{:S(2)}) collective-permute-start(bf16[152,256]{1,0:T(8,128)(2,1)S(1)} %get-tuple-element.67), channel_id=1, source_target_pairs={{0,1},{1,2},{2,3},{3,0},{4,5},{5,6},{6,7},{7,4},{8,9},{9,10},{10,1... | collective-permute-start | bytes 233480 | tf_op jit(solution)/shard_map/ppermute | solution.py:235
  84.2 12.5 %collective-permute-start.4 = (bf16[152,256]{1,0:T(8,128)(2,1)S(1)}, bf16[152,256]{1,0:T(8,128)(2,1)S(1)}, u32[]{:S(2)}, u32[]{:S(2)}) collective-permute-start(bf16[152,256]{1,0:T(8,128)(2,1)S(1)} %get-tuple-element.68), channel_id=1, source_target_pairs={{0,2},{1,3},{2,0},{3,1},{4,6},{5,7},{6,4},{7,5},{8,10},{9,11},{10,... | collective-permute-start | bytes 233480 | tf_op jit(solution)/shard_map/ppermute | solution.py:235
  88.5 8.2 %collective-permute-start.5 = (bf16[152,256]{1,0:T(8,128)(2,1)S(1)}, bf16[152,256]{1,0:T(8,128)(2,1)S(1)}, u32[]{:S(2)}, u32[]{:S(2)}) collective-permute-start(bf16[152,256]{1,0:T(8,128)(2,1)S(1)} %get-tuple-element.69), channel_id=1, source_target_pairs={{0,3},{1,0},{2,1},{3,2},{4,7},{5,4},{6,5},{7,6},{8,11},{9,8},{10,9... | collective-permute-start | bytes 233480 | tf_op jit(solution)/shard_map/ppermute | solution.py:235
  98.0 4.9 %copy-start.3 = (bf16[1,448,1216]{2,1,0:T(8,128)(2,1)S(1)}, bf16[1,448,1216]{2,1,0:T(8,128)(2,1)}, u32[]{:S(2)}) copy-start(bf16[1,448,1216]{2,1,0:T(8,128)(2,1)} %param.16) | copy-start | bytes 3268612
  98.1 19.3 %all-to-all-start.2 = ((bf16[16,76,384]{2,1,0:T(8,128)(2,1)}), bf16[16,76,384]{2,1,0:T(8,128)(2,1)S(1)}, u32[]{:S(2)}, u32[]{:S(2)}) async-start(bf16[16,76,384]{2,1,0:T(8,128)(2,1)} %shard_map.95), calls=%async_computation.2 | async-start | bytes 1966080 | tf_op jit(solution)/shard_map/all_to_all | solution.py:321
  118.2 10.0 %copy-start.6 = (bf16[256,152]{0,1:T(8,128)(2,1)S(1)}, bf16[256,152]{0,1:T(8,128)(2,1)}, u32[]{:S(2)}) copy-start(bf16[256,152]{0,1:T(8,128)(2,1)} %param.14) | copy-start | bytes 233476
  118.2 10.0 %copy-start.8 = (bf16[152,256]{1,0:T(8,128)(2,1)S(1)}, bf16[152,256]{1,0:T(8,128)(2,1)}, u32[]{:S(2)}) copy-start(bf16[152,256]{1,0:T(8,128)(2,1)} %copy-done.7) | copy-start | bytes 233476
  118.2 10.0 %copy-start.10 = (bf16[152,256]{1,0:T(8,128)(2,1)S(1)}, bf16[152,256]{1,0:T(8,128)(2,1)}, u32[]{:S(2)}) copy-start(bf16[152,256]{1,0:T(8,128)(2,1)} %copy-done.9) | copy-start | bytes 233476
  123.2 32.9 %copy-start.1 = (bf16[448,2432]{1,0:T(8,128)(2,1)S(1)}, bf16[448,2432]{1,0:T(8,128)(2,1)}, u32[]{:S(2)}) copy-start(bf16[448,2432]{1,0:T(8,128)(2,1)} %rest_4_.1) | copy-start | bytes 6537220
  124.3 40.3 %all-to-all-start.3 = ((bf16[32,24,128]{2,1,0:T(8,128)(2,1)}), bf16[32,24,128]{2,1,0:T(8,128)(2,1)S(1)}, u32[]{:S(2)}, u32[]{:S(2)}) async-start(bf16[32,24,128]{2,1,0:T(8,128)(2,1)} %shard_map.98), calls=%async_computation.3 | async-start | bytes 393216 | tf_op jit(solution)/shard_map/all_to_all | solution.py:346
  128.3 7.3 %collective-permute-start.8 = (bf16[152,256]{1,0:T(8,128)(2,1)S(1)}, bf16[152,256]{1,0:T(8,128)(2,1)S(1)}, u32[]{:S(2)}, u32[]{:S(2)}) collective-permute-start(bf16[152,256]{1,0:T(8,128)(2,1)S(1)} %shard_map.99), channel_id=1, source_target_pairs={{0,3},{1,0},{2,1},{3,2},{4,7},{5,4},{6,5},{7,6},{8,11},{9,8},{10,9... | collective-permute-start | bytes 233480 | tf_op jit(solution)/shard_map/ppermute | solution.py:235
  131.1 6.9 %collective-permute-start.7 = (bf16[152,256]{1,0:T(8,128)(2,1)S(1)}, bf16[152,256]{1,0:T(8,128)(2,1)S(1)}, u32[]{:S(2)}, u32[]{:S(2)}) collective-permute-start(bf16[152,256]{1,0:T(8,128)(2,1)S(1)} %shard_map.99), channel_id=1, source_target_pairs={{0,2},{1,3},{2,0},{3,1},{4,6},{5,7},{6,4},{7,5},{8,10},{9,11},{10,... | collective-permute-start | bytes 233480 | tf_op jit(solution)/shard_map/ppermute | solution.py:235
  133.6 6.6 %collective-permute-start.6 = (bf16[152,256]{1,0:T(8,128)(2,1)S(1)}, bf16[152,256]{1,0:T(8,128)(2,1)S(1)}, u32[]{:S(2)}, u32[]{:S(2)}) collective-permute-start(bf16[152,256]{1,0:T(8,128)(2,1)S(1)} %shard_map.99), channel_id=1, source_target_pairs={{0,1},{1,2},{2,3},{3,0},{4,5},{5,6},{6,7},{7,4},{8,9},{9,10},{10,1... | collective-permute-start | bytes 233480 | tf_op jit(solution)/shard_map/ppermute | solution.py:235
  140.3 24.3 %copy-start.5 = (bf16[256,256]{1,0:T(8,128)(2,1)S(1)}, bf16[256,256]{1,0:T(8,128)(2,1)}, u32[]{:S(2)}) copy-start(bf16[256,256]{1,0:T(8,128)(2,1)} %get-tuple-element.88.chooser) | copy-start | bytes 393220
  140.3 8.4 %collective-permute-start.11 = (bf16[4,152,256]{2,1,0:T(8,128)(2,1)S(1)}, bf16[4,152,256]{2,1,0:T(8,128)(2,1)S(1)}, u32[]{:S(2)}, u32[]{:S(2)}) collective-permute-start(bf16[4,152,256]{2,1,0:T(8,128)(2,1)S(1)} %pad_maximum_fusion.rest_0_), channel_id=1, source_target_pairs={{0,12},{1,13},{2,14},{3,15},{4,0},{5,1},{6,2},{7,3},{8,4},{9,5},{1... | collective-permute-start | bytes 933896 | tf_op jit(solution)/shard_map/ppermute | solution.py:235
  143.4 9.4 %collective-permute-start.10 = (bf16[4,152,256]{2,1,0:T(8,128)(2,1)S(1)}, bf16[4,152,256]{2,1,0:T(8,128)(2,1)S(1)}, u32[]{:S(2)}, u32[]{:S(2)}) collective-permute-start(bf16[4,152,256]{2,1,0:T(8,128)(2,1)S(1)} %pad_maximum_fusion.rest_0_), channel_id=1, source_target_pairs={{0,8},{1,9},{2,10},{3,11},{4,12},{5,13},{6,14},{7,15},{8,0},{9,1},... | collective-permute-start | bytes 933896 | tf_op jit(solution)/shard_map/ppermute | solution.py:235
  146.4 9.8 %collective-permute-start.9 = (bf16[4,152,256]{2,1,0:T(8,128)(2,1)S(1)}, bf16[4,152,256]{2,1,0:T(8,128)(2,1)S(1)}, u32[]{:S(2)}, u32[]{:S(2)}) collective-permute-start(bf16[4,152,256]{2,1,0:T(8,128)(2,1)S(1)} %pad_maximum_fusion.rest_0_), channel_id=1, source_target_pairs={{0,4},{1,5},{2,6},{3,7},{4,8},{5,9},{6,10},{7,11},{8,12},{9,13},{1... | collective-permute-start | bytes 933896 | tf_op jit(solution)/shard_map/ppermute | solution.py:235
  (4 other events, 5.2 us)

commit v8 on v7

--- a/solution.py
+++ b/solution.py
@@ -6,7 +6,6 @@
 from jax.sharding import Mesh, PartitionSpec as P
 
 CAP = 6
-LANES = 128
 ROOM = 60
 F32 = jnp.float32
 BF16 = jnp.bfloat16
@@ -36,27 +35,24 @@
     return lax.broadcasted_iota(jnp.int32, shape, dim)
 
 
-def packed(blocks, last):
-    rows = last.shape[0]
-    place = iota(last.shape, 0) & 7
-    groups = [
-        jnp.where(place >= CAP, pltpu.roll(last, CAP - 2 * j, 0), block).reshape(
-            rows // 8, 8, LANES
+def packed(rows):
+    count = rows.shape[0] // CAP
+    sides = [
+        jnp.concatenate(
+            [rows[count * (3 * side + i) : count * (3 * side + i + 1)] for i in range(3)], axis=1
         )
-        for j, block in enumerate(blocks)
+        for side in range(2)
     ]
-    return jnp.concatenate(groups, axis=1).astype(BF16)
+    return jnp.stack(sides, axis=1).astype(BF16)
 
 
 def unpacked(message):
     wide = message.astype(F32)
-    rows = wide.shape[0] * 8
-    blocks = [wide[:, 8 * j : 8 * j + 8, :].reshape(rows, LANES) for j in range(3)]
-    place = iota((rows, LANES), 0) & 7
-    moved = [pltpu.roll(block, rows - CAP + 2 * j, 0) for j, block in enumerate(blocks)]
-    last = jnp.where(place < 2, moved[0], jnp.where(place < 4, moved[1], moved[2]))
-    last = jnp.where(iota((rows, LANES), 1) >= LANES // 2, last, 0.0)
-    return [v.astype(BF16) for v in blocks + [last]]
+    width = wide.shape[2] // 3
+    rows = [
+        wide[:, side, width * i : width * (i + 1)] for side in range(2) for i in range(3)
+    ]
+    return jnp.concatenate(rows, axis=0).astype(BF16)
 
 
 def dispatch_kernel(routes, gates, grads_t, message, chooser):
@@ -69,8 +65,8 @@
     before = jnp.where(
         iota((tokens, tokens), 0) < iota((tokens, tokens), 1), 1.0, 0.0
     ).astype(BF16)
-    place = experts * 8 + dot(named, before, 1, 0).astype(jnp.int32) + 1
-    row = iota((held * 8, tokens), 0) + 1
+    place = experts + dot(named, before, 1, 0).astype(jnp.int32) * held + 1
+    row = iota((held * CAP, tokens), 0) + 1
     hit_first = jnp.sum(jnp.where(first, place, 0), axis=0, keepdims=True) == row
     hit_second = jnp.sum(jnp.where(second, place, 0), axis=0, keepdims=True) == row
     weight = gates[...]
@@ -81,27 +77,21 @@
     )
     chosen = jnp.where(hit_first | hit_second, 1.0, 0.0).astype(BF16)
     chooser[...] = chosen
-    width = grads_t.shape[0]
-    rows = dot(chosen, grads_t[...], 1, 1)
-    tail = dot(chosen, grads_t[width - LANES :, :], 1, 1) * gate
-    message[...] = packed(
-        [rows[:, LANES * j : LANES * (j + 1)] * gate for j in range(3)], tail
-    )
+    message[...] = packed(dot(chosen, grads_t[...], 1, 1) * gate)
 
 
 def down_kernel(arrived, down_t, mid, held_out, sems):
     cores, held = arrived.shape[0], arrived.shape[1]
-    blocks = unpacked(arrived[...].reshape(cores * held, 3 * 8, LANES))
-    slots, rows = cores * held * CAP, cores * held * 8
-    row = iota((slots, rows), 1)
-    core = jnp.where(row >= held * 8, 1, 0)
-    block = ((row - core * held * 8) >> 3) * 2 + core
-    pick = ((row & 7) < CAP) & (block * CAP + (row & 7) == iota((slots, rows), 0))
-    pick = jnp.where(pick, 1.0, 0.0).astype(BF16)
-    picked = dot(pick, jnp.concatenate(blocks, axis=1), 1, 0).astype(BF16)
-    width = down_t.shape[0]
-    weights = jnp.concatenate([down_t[: 3 * LANES, :], down_t[width - LANES :, :]], axis=0)
-    total = dot(weights, picked, 0, 1)
+    rows = unpacked(arrived[...].reshape((cores * held,) + arrived.shape[2:]))
+    slots, sources = rows.shape[0], cores * held
+    row = iota((slots, slots), 1)
+    rank = row // sources
+    source = row - rank * sources
+    core = jnp.where(source >= held, 1, 0)
+    slot = ((source - core * held) * 2 + core) * CAP + rank
+    pick = jnp.where(slot == iota((slots, slots), 0), 1.0, 0.0).astype(BF16)
+    picked = dot(pick, rows, 1, 0).astype(BF16)
+    total = dot(down_t[...], picked, 0, 1)
     piece = mid.shape[1]
     copies = []
     for part in range(mid.shape[0]):
@@ -146,31 +136,16 @@
     slots = halves.shape[2]
     core = core_id[0]
     both = (halves[0].astype(F32) + halves[1].astype(F32)).astype(BF16)
-    row = iota((held * 8, slots), 0)
-    slot = ((row >> 3) * 2 + core) * CAP + (row & 7)
-    pick = ((row & 7) < CAP) & (slot == iota((held * 8, slots), 1))
-    pick = jnp.where(pick, 1.0, 0.0).astype(BF16)
-    width = both.shape[0]
-    rows = dot(pick, both, 1, 1)
-    message[...] = packed(
-        [rows[:, LANES * j : LANES * (j + 1)] for j in range(3)],
-        dot(pick, both[width - LANES :], 1, 1),
-    )
+    row = iota((held * CAP, slots), 0)
+    rank = row // held
+    slot = ((row - rank * held) * 2 + core) * CAP + rank
+    pick = jnp.where(slot == iota((held * CAP, slots), 1), 1.0, 0.0).astype(BF16)
+    message[...] = packed(dot(pick, both, 1, 1))
 
 
 def combine_kernel(returned, chooser, dense_t, out_t):
-    blocks = unpacked(returned[...])
-    chosen = chooser[...]
-    width = out_t.shape[0]
-    for j in range(3):
-        low = LANES * j
-        out_t[low : low + LANES, :] = (
-            dense_t[low : low + LANES, :] + dot(blocks[j], chosen, 0, 0)
-        ).astype(BF16)
-    half = LANES // 2
-    out_t[3 * LANES :, :] = (
-        dense_t[3 * LANES :, :] + dot(blocks[3], chosen, 0, 0)[half:]
-    ).astype(BF16)
+    routed = dot(unpacked(returned[...]), chooser[...], 0, 0)
+    out_t[...] = (dense_t[...] + routed).astype(BF16)
 
 
 def wrapped(value, size):
@@ -250,8 +225,8 @@
     message, chooser = call(
         dispatch_kernel,
         (
-            jax.ShapeDtypeStruct((held, 24, LANES), BF16),
-            jax.ShapeDtypeStruct((held * 8, tokens), BF16),
+            jax.ShapeDtypeStruct((held, 2, 3 * width), BF16),
+            jax.ShapeDtypeStruct((held * CAP, tokens), BF16),
         ),
         routes.T,
         gates.T,
@@ -337,7 +312,7 @@
     )
     back = call(
         return_kernel,
-        jax.ShapeDtypeStruct((held, 24, LANES), BF16),
+        jax.ShapeDtypeStruct((held, 2, 3 * width), BF16),
         core.astype(jnp.int32).reshape(1),
         lax.all_gather(rows_t, "c", axis=0, tiled=False),
         spaces=[smem, vmem],

time: 167 us -> 164 us (0.982)
  waiting for transfers between devices: 59 us -> 56.4 us
where the time goes in v8:
time: 164 us; the launch traced here: 163 us
  starting transfers between devices  81.9 us (50%)
  waiting for transfers between devices  56.4 us (34%)
  Pallas kernels  12.9 us (8%)
  blocking collectives  9.1 us (6%)
  local copies, waits for them, and re-layouts  2.6 us (2%)
    ppermute x12, starting transfers between devices, moved(): return lax.ppermute(value, ('c', 'x', 'y'), pairs)  37 us
    all_to_all x1, starting transfers between devices, shards(): arrived = lax.all_to_all(message, 'z', 0, 0, tiled=True)  29.3 us
    all_to_all x1, waiting for transfers between devices, shards(): arrived = lax.all_to_all(message, 'z', 0, 0, tiled=True)  19.3 us
    ppermute x12, waiting for transfers between devices, moved(): return lax.ppermute(value, ('c', 'x', 'y'), pairs)  17.2 us
    all_to_all x1, waiting for transfers between devices, shards(): full = lax.all_to_all(copies, tensor, 0, 0, tiled=True)  14.2 us
    pallas_call x11, Pallas kernels, call(): pl.pallas_call(kernel, out_shape=outs, in_specs=[pl.BlockSpec(memory_spac...  12.9 us
    all_to_all x1, starting transfers between devices, shards(): shares = lax.all_to_all(mid, tensor, 0, 0, tiled=True)  6.9 us
    all_to_all x1, waiting for transfers between devices, shards(): returned = lax.all_to_all(back, 'z', 0, 0, tiled=True)  5.64 us
  transfers between devices with their start and end apart: 16, of which 9 were waited for; matrix products, arithmetic and copies ran while one was open for 0% of the time, Pallas kernels for 2%

profile of v8, /device:TPU:1, one launch (start us, length us, event | category | flops | bytes accessed | tf_op | source)
XLA Modules:
  0.0 163.4 jit_solution(2282663897558388537)
XLA Ops:
  0.0 2.3 %shard_map.91 = (bf16[32,2,1344]{2,1,0:T(2,128)(2,1)}, bf16[192,256]{1,0:T(8,128)(2,1)}) custom-call(s32[2,256]{1,0:T(2,128)} %bitcast.37, f32[2,256]{1,0:T(2,128)} %bitcast.38, bf16[448,256]{1,0:T(8,128)(2,1)} %bitcast.29), custom_call_target="tpu_custom_call" | custom-call | bytes 233472 | tf_op jit(solution)/shard_map/pallas_call | solution.py:17
  2.3 29.3 %all-to-all-start = ((bf16[32,2,1344]{2,1,0:T(2,128)(2,1)}), bf16[32,2,1344]{2,1,0:T(2,128)(2,1)S(1)}, u32[]{:S(2)}, u32[]{:S(2)}) async-start(bf16[32,2,1344]{2,1,0:T(2,128)(2,1)} %get-tuple-element.50), calls=%async_computation | async-start | bytes 360448 | tf_op jit(solution)/shard_map/all_to_all | solution.py:253
  35.8 3.2 %collective-permute-start = (bf16[4,152,256]{2,1,0:T(8,128)(2,1)S(1)}, bf16[4,152,256]{2,1,0:T(8,128)(2,1)S(1)}, u32[]{:S(2)}, u32[]{:S(2)}) collective-permute-start(bf16[4,152,256]{2,1,0:T(8,128)(2,1)S(1)} %get-tuple-element.53), channel_id=1, source_target_pairs={{0,4},{1,5},{2,6},{3,7},{4,8},{5,9},{6,10},{7,11},{8,12},{9,13},{1... | collective-permute-start | bytes 933896 | tf_op jit(solution)/shard_map/ppermute | solution.py:210
  39.0 4.5 %collective-permute-start.1 = (bf16[4,152,256]{2,1,0:T(8,128)(2,1)S(1)}, bf16[4,152,256]{2,1,0:T(8,128)(2,1)S(1)}, u32[]{:S(2)}, u32[]{:S(2)}) collective-permute-start(bf16[4,152,256]{2,1,0:T(8,128)(2,1)S(1)} %get-tuple-element.54), channel_id=1, source_target_pairs={{0,8},{1,9},{2,10},{3,11},{4,12},{5,13},{6,14},{7,15},{8,0},{9,1},... | collective-permute-start | bytes 933896 | tf_op jit(solution)/shard_map/ppermute | solution.py:210
  43.6 3.0 %collective-permute-start.2 = (bf16[4,152,256]{2,1,0:T(8,128)(2,1)S(1)}, bf16[4,152,256]{2,1,0:T(8,128)(2,1)S(1)}, u32[]{:S(2)}, u32[]{:S(2)}) collective-permute-start(bf16[4,152,256]{2,1,0:T(8,128)(2,1)S(1)} %get-tuple-element.55), channel_id=1, source_target_pairs={{0,12},{1,13},{2,14},{3,15},{4,0},{5,1},{6,2},{7,3},{8,4},{9,5},{1... | collective-permute-start | bytes 933896 | tf_op jit(solution)/shard_map/ppermute | solution.py:210
  46.5 19.3 %all-to-all-done = bf16[32,2,1344]{2,1,0:T(2,128)(2,1)S(1)} async-done(((bf16[32,2,1344]{2,1,0:T(2,128)(2,1)}), bf16[32,2,1344]{2,1,0:T(2,128)(2,1)S(1)}, u32[]{:S(2)}, u32[]{:S(2)}) %all-to-all-start) | async-done | bytes 172064 | tf_op jit(solution)/shard_map/all_to_all | solution.py:253
  65.8 4.1 %all-gather = bf16[64,2,1344]{2,1,0:T(2,128)(2,1)S(1)} all-gather(bf16[32,2,1344]{2,1,0:T(2,128)(2,1)S(1)} %all-to-all-done), channel_id=2, replica_groups=mesh['z'=32,'c'=2,'x'=4,'y'=4] {'c'}, dimensions={0}, use_global_device_ids=true | all-gather | bytes 516096 | tf_op jit(solution)/shard_map/all_gather | solution.py:264
  72.2 6.9 %all-to-all-start.1 = ((bf16[16,76,384]{2,1,0:T(8,128)(2,1)}), bf16[16,76,384]{2,1,0:T(8,128)(2,1)S(1)}, u32[]{:S(2)}, u32[]{:S(2)}) async-start(bf16[16,76,384]{2,1,0:T(8,128)(2,1)} %shard_map.93), calls=%async_computation.1 | async-start | bytes 1966080 | tf_op jit(solution)/shard_map/all_to_all | solution.py:277
  79.8 3.3 %collective-permute-start.3 = (bf16[152,256]{1,0:T(8,128)(2,1)S(1)}, bf16[152,256]{1,0:T(8,128)(2,1)S(1)}, u32[]{:S(2)}, u32[]{:S(2)}) collective-permute-start(bf16[152,256]{1,0:T(8,128)(2,1)S(1)} %get-tuple-element.67), channel_id=1, source_target_pairs={{0,1},{1,2},{2,3},{3,0},{4,5},{5,6},{6,7},{7,4},{8,9},{9,10},{10,1... | collective-permute-start | bytes 233480 | tf_op jit(solution)/shard_map/ppermute | solution.py:210
  83.1 4.3 %collective-permute-start.4 = (bf16[152,256]{1,0:T(8,128)(2,1)S(1)}, bf16[152,256]{1,0:T(8,128)(2,1)S(1)}, u32[]{:S(2)}, u32[]{:S(2)}) collective-permute-start(bf16[152,256]{1,0:T(8,128)(2,1)S(1)} %get-tuple-element.68), channel_id=1, source_target_pairs={{0,2},{1,3},{2,0},{3,1},{4,6},{5,7},{6,4},{7,5},{8,10},{9,11},{10,... | collective-permute-start | bytes 233480 | tf_op jit(solution)/shard_map/ppermute | solution.py:210
  87.4 3.1 %collective-permute-start.5 = (bf16[152,256]{1,0:T(8,128)(2,1)S(1)}, bf16[152,256]{1,0:T(8,128)(2,1)S(1)}, u32[]{:S(2)}, u32[]{:S(2)}) collective-permute-start(bf16[152,256]{1,0:T(8,128)(2,1)S(1)} %get-tuple-element.69), channel_id=1, source_target_pairs={{0,3},{1,0},{2,1},{3,2},{4,7},{5,4},{6,5},{7,6},{8,11},{9,8},{10,9... | collective-permute-start | bytes 233480 | tf_op jit(solution)/shard_map/ppermute | solution.py:210
  90.5 2.8 %collective-permute-done.3.rest_1_ = bf16[152,256]{1,0:T(8,128)(2,1)S(1)} collective-permute-done((bf16[152,256]{1,0:T(8,128)(2,1)S(1)}, bf16[152,256]{1,0:T(8,128)(2,1)S(1)}, u32[]{:S(2)}, u32[]{:S(2)}) %collective-permute-start.3) | collective-permute-done | bytes 77856 | tf_op jit(solution)/shard_map/ppermute | solution.py:210
  96.9 4.9 %all-to-all-start.2 = ((bf16[16,76,384]{2,1,0:T(8,128)(2,1)}), bf16[16,76,384]{2,1,0:T(8,128)(2,1)S(1)}, u32[]{:S(2)}, u32[]{:S(2)}) async-start(bf16[16,76,384]{2,1,0:T(8,128)(2,1)} %shard_map.95), calls=%async_computation.2 | async-start | bytes 1966080 | tf_op jit(solution)/shard_map/all_to_all | solution.py:296
  102.0 14.2 %all-to-all-done.2.full = bf16[16,76,384]{2,1,0:T(8,128)(2,1)S(1)} async-done(((bf16[16,76,384]{2,1,0:T(8,128)(2,1)}), bf16[16,76,384]{2,1,0:T(8,128)(2,1)S(1)}, u32[]{:S(2)}, u32[]{:S(2)}) %all-to-all-start.2) | async-done | bytes 933920 | tf_op jit(solution)/shard_map/all_to_all | solution.py:296
  117.1 5.0 %all-gather.1 = bf16[896,384]{1,0:T(8,128)(2,1)S(1)} all-gather(bf16[448,384]{1,0:T(8,128)(2,1)S(1)} %shard_map.97), channel_id=3, replica_groups=mesh['z'=32,'c'=2,'x'=4,'y'=4] {'c'}, dimensions={0}, use_global_device_ids=true | all-gather | bytes 1032192 | tf_op jit(solution)/shard_map/all_gather | solution.py:317
  123.3 3.9 %all-to-all-start.3 = ((bf16[32,2,1344]{2,1,0:T(2,128)(2,1)}), bf16[32,2,1344]{2,1,0:T(2,128)(2,1)S(1)}, u32[]{:S(2)}, u32[]{:S(2)}) async-start(bf16[32,2,1344]{2,1,0:T(2,128)(2,1)} %shard_map.98), calls=%async_computation.3 | async-start | bytes 360448 | tf_op jit(solution)/shard_map/all_to_all | solution.py:321
  127.3 2.8 %collective-permute-start.8 = (bf16[152,256]{1,0:T(8,128)(2,1)S(1)}, bf16[152,256]{1,0:T(8,128)(2,1)S(1)}, u32[]{:S(2)}, u32[]{:S(2)}) collective-permute-start(bf16[152,256]{1,0:T(8,128)(2,1)S(1)} %shard_map.99), channel_id=1, source_target_pairs={{0,3},{1,0},{2,1},{3,2},{4,7},{5,4},{6,5},{7,6},{8,11},{9,8},{10,9... | collective-permute-start | bytes 233480 | tf_op jit(solution)/shard_map/ppermute | solution.py:210
  130.1 2.5 %collective-permute-start.7 = (bf16[152,256]{1,0:T(8,128)(2,1)S(1)}, bf16[152,256]{1,0:T(8,128)(2,1)S(1)}, u32[]{:S(2)}, u32[]{:S(2)}) collective-permute-start(bf16[152,256]{1,0:T(8,128)(2,1)S(1)} %shard_map.99), channel_id=1, source_target_pairs={{0,2},{1,3},{2,0},{3,1},{4,6},{5,7},{6,4},{7,5},{8,10},{9,11},{10,... | collective-permute-start | bytes 233480 | tf_op jit(solution)/shard_map/ppermute | solution.py:210
  134.7 2.4 %collective-permute-done.7 = bf16[152,256]{1,0:T(8,128)(2,1)S(1)} collective-permute-done((bf16[152,256]{1,0:T(8,128)(2,1)S(1)}, bf16[152,256]{1,0:T(8,128)(2,1)S(1)}, u32[]{:S(2)}, u32[]{:S(2)}) %collective-permute-start.7) | collective-permute-done | bytes 77856 | tf_op jit(solution)/shard_map/ppermute | solution.py:210
  139.4 3.0 %collective-permute-start.11 = (bf16[4,152,256]{2,1,0:T(8,128)(2,1)S(1)}, bf16[4,152,256]{2,1,0:T(8,128)(2,1)S(1)}, u32[]{:S(2)}, u32[]{:S(2)}) collective-permute-start(bf16[4,152,256]{2,1,0:T(8,128)(2,1)S(1)} %pad_maximum_fusion.rest_0_), channel_id=1, source_target_pairs={{0,12},{1,13},{2,14},{3,15},{4,0},{5,1},{6,2},{7,3},{8,4},{9,5},{1... | collective-permute-start | bytes 933896 | tf_op jit(solution)/shard_map/ppermute | solution.py:210
  142.4 3.0 %collective-permute-start.10 = (bf16[4,152,256]{2,1,0:T(8,128)(2,1)S(1)}, bf16[4,152,256]{2,1,0:T(8,128)(2,1)S(1)}, u32[]{:S(2)}, u32[]{:S(2)}) collective-permute-start(bf16[4,152,256]{2,1,0:T(8,128)(2,1)S(1)} %pad_maximum_fusion.rest_0_), channel_id=1, source_target_pairs={{0,8},{1,9},{2,10},{3,11},{4,12},{5,13},{6,14},{7,15},{8,0},{9,1},... | collective-permute-start | bytes 933896 | tf_op jit(solution)/shard_map/ppermute | solution.py:210
  147.7 4.1 %collective-permute-done.10.rest_2_ = bf16[4,152,256]{2,1,0:T(8,128)(2,1)S(1)} collective-permute-done((bf16[4,152,256]{2,1,0:T(8,128)(2,1)S(1)}, bf16[4,152,256]{2,1,0:T(8,128)(2,1)S(1)}, u32[]{:S(2)}, u32[]{:S(2)}) %collective-permute-start.10) | collective-permute-done | bytes 311328 | tf_op jit(solution)/shard_map/ppermute | solution.py:210
  151.9 3.3 %collective-permute-done.9.rest_1_ = bf16[4,152,256]{2,1,0:T(8,128)(2,1)S(1)} collective-permute-done((bf16[4,152,256]{2,1,0:T(8,128)(2,1)S(1)}, bf16[4,152,256]{2,1,0:T(8,128)(2,1)S(1)}, u32[]{:S(2)}, u32[]{:S(2)}) %collective-permute-start.9) | collective-permute-done | bytes 311328 | tf_op jit(solution)/shard_map/ppermute | solution.py:210
  156.7 5.6 %all-to-all-done.3.returned = bf16[32,2,1344]{2,1,0:T(2,128)(2,1)S(1)} async-done(((bf16[32,2,1344]{2,1,0:T(2,128)(2,1)}), bf16[32,2,1344]{2,1,0:T(2,128)(2,1)S(1)}, u32[]{:S(2)}, u32[]{:S(2)}) %all-to-all-start.3) | async-done | bytes 172064 | tf_op jit(solution)/shard_map/all_to_all | solution.py:321
  (47 shorter events, 22.2 us)
Async XLA Ops:
  2.3 63.5 %all-to-all-start = ((bf16[32,2,1344]{2,1,0:T(2,128)(2,1)}), bf16[32,2,1344]{2,1,0:T(2,128)(2,1)S(1)}, u32[]{:S(2)}, u32[]{:S(2)}) async-start(bf16[32,2,1344]{2,1,0:T(2,128)(2,1)} %get-tuple-element.50), calls=%async_computation | async-start | bytes 360448 | tf_op jit(solution)/shard_map/all_to_all | solution.py:253
  34.3 35.7 %copy-start.2 = (bf16[1,1216,448]{1,2,0:T(8,128)(2,1)S(1)}, bf16[1,1216,448]{1,2,0:T(8,128)(2,1)}, u32[]{:S(2)}) copy-start(bf16[1,1216,448]{1,2,0:T(8,128)(2,1)} %param.15) | copy-start | bytes 3268612
  35.8 34.1 %collective-permute-start = (bf16[4,152,256]{2,1,0:T(8,128)(2,1)S(1)}, bf16[4,152,256]{2,1,0:T(8,128)(2,1)S(1)}, u32[]{:S(2)}, u32[]{:S(2)}) collective-permute-start(bf16[4,152,256]{2,1,0:T(8,128)(2,1)S(1)} %get-tuple-element.53), channel_id=1, source_target_pairs={{0,4},{1,5},{2,6},{3,7},{4,8},{5,9},{6,10},{7,11},{8,12},{9,13},{1... | collective-permute-start | bytes 933896 | tf_op jit(solution)/shard_map/ppermute | solution.py:210
  39.0 30.9 %collective-permute-start.1 = (bf16[4,152,256]{2,1,0:T(8,128)(2,1)S(1)}, bf16[4,152,256]{2,1,0:T(8,128)(2,1)S(1)}, u32[]{:S(2)}, u32[]{:S(2)}) collective-permute-start(bf16[4,152,256]{2,1,0:T(8,128)(2,1)S(1)} %get-tuple-element.54), channel_id=1, source_target_pairs={{0,8},{1,9},{2,10},{3,11},{4,12},{5,13},{6,14},{7,15},{8,0},{9,1},... | collective-permute-start | bytes 933896 | tf_op jit(solution)/shard_map/ppermute | solution.py:210
  43.6 26.4 %collective-permute-start.2 = (bf16[4,152,256]{2,1,0:T(8,128)(2,1)S(1)}, bf16[4,152,256]{2,1,0:T(8,128)(2,1)S(1)}, u32[]{:S(2)}, u32[]{:S(2)}) collective-permute-start(bf16[4,152,256]{2,1,0:T(8,128)(2,1)S(1)} %get-tuple-element.55), channel_id=1, source_target_pairs={{0,12},{1,13},{2,14},{3,15},{4,0},{5,1},{6,2},{7,3},{8,4},{9,5},{1... | collective-permute-start | bytes 933896 | tf_op jit(solution)/shard_map/ppermute | solution.py:210
  72.2 23.5 %copy-start.11 = (bf16[1,384,76]{1,2,0:T(8,128)(2,1)S(1)}, bf16[1,384,76]{1,2,0:T(8,128)(2,1)}, u32[]{:S(2)}) copy-start(bf16[1,384,76]{1,2,0:T(8,128)(2,1)} %param.17) | copy-start | bytes 175108
  72.2 23.4 %all-to-all-start.1 = ((bf16[16,76,384]{2,1,0:T(8,128)(2,1)}), bf16[16,76,384]{2,1,0:T(8,128)(2,1)S(1)}, u32[]{:S(2)}, u32[]{:S(2)}) async-start(bf16[16,76,384]{2,1,0:T(8,128)(2,1)} %shard_map.93), calls=%async_computation.1 | async-start | bytes 1966080 | tf_op jit(solution)/shard_map/all_to_all | solution.py:277
  79.8 13.5 %collective-permute-start.3 = (bf16[152,256]{1,0:T(8,128)(2,1)S(1)}, bf16[152,256]{1,0:T(8,128)(2,1)S(1)}, u32[]{:S(2)}, u32[]{:S(2)}) collective-permute-start(bf16[152,256]{1,0:T(8,128)(2,1)S(1)} %get-tuple-element.67), channel_id=1, source_target_pairs={{0,1},{1,2},{2,3},{3,0},{4,5},{5,6},{6,7},{7,4},{8,9},{9,10},{10,1... | collective-permute-start | bytes 233480 | tf_op jit(solution)/shard_map/ppermute | solution.py:210
  83.1 12.5 %collective-permute-start.4 = (bf16[152,256]{1,0:T(8,128)(2,1)S(1)}, bf16[152,256]{1,0:T(8,128)(2,1)S(1)}, u32[]{:S(2)}, u32[]{:S(2)}) collective-permute-start(bf16[152,256]{1,0:T(8,128)(2,1)S(1)} %get-tuple-element.68), channel_id=1, source_target_pairs={{0,2},{1,3},{2,0},{3,1},{4,6},{5,7},{6,4},{7,5},{8,10},{9,11},{10,... | collective-permute-start | bytes 233480 | tf_op jit(solution)/shard_map/ppermute | solution.py:210
  87.4 8.2 %collective-permute-start.5 = (bf16[152,256]{1,0:T(8,128)(2,1)S(1)}, bf16[152,256]{1,0:T(8,128)(2,1)S(1)}, u32[]{:S(2)}, u32[]{:S(2)}) collective-permute-start(bf16[152,256]{1,0:T(8,128)(2,1)S(1)} %get-tuple-element.69), channel_id=1, source_target_pairs={{0,3},{1,0},{2,1},{3,2},{4,7},{5,4},{6,5},{7,6},{8,11},{9,8},{10,9... | collective-permute-start | bytes 233480 | tf_op jit(solution)/shard_map/ppermute | solution.py:210
  96.9 4.9 %copy-start.3 = (bf16[1,448,1216]{2,1,0:T(8,128)(2,1)S(1)}, bf16[1,448,1216]{2,1,0:T(8,128)(2,1)}, u32[]{:S(2)}) copy-start(bf16[1,448,1216]{2,1,0:T(8,128)(2,1)} %param.16) | copy-start | bytes 3268612
  96.9 19.3 %all-to-all-start.2 = ((bf16[16,76,384]{2,1,0:T(8,128)(2,1)}), bf16[16,76,384]{2,1,0:T(8,128)(2,1)S(1)}, u32[]{:S(2)}, u32[]{:S(2)}) async-start(bf16[16,76,384]{2,1,0:T(8,128)(2,1)} %shard_map.95), calls=%async_computation.2 | async-start | bytes 1966080 | tf_op jit(solution)/shard_map/all_to_all | solution.py:296
  117.0 10.2 %copy-start.6 = (bf16[256,152]{0,1:T(8,128)(2,1)S(1)}, bf16[256,152]{0,1:T(8,128)(2,1)}, u32[]{:S(2)}) copy-start(bf16[256,152]{0,1:T(8,128)(2,1)} %param.14) | copy-start | bytes 233476
  117.1 10.2 %copy-start.8 = (bf16[152,256]{1,0:T(8,128)(2,1)S(1)}, bf16[152,256]{1,0:T(8,128)(2,1)}, u32[]{:S(2)}) copy-start(bf16[152,256]{1,0:T(8,128)(2,1)} %copy-done.7) | copy-start | bytes 233476
  117.1 10.2 %copy-start.10 = (bf16[152,256]{1,0:T(8,128)(2,1)S(1)}, bf16[152,256]{1,0:T(8,128)(2,1)}, u32[]{:S(2)}) copy-start(bf16[152,256]{1,0:T(8,128)(2,1)} %copy-done.9) | copy-start | bytes 233476
  122.1 33.1 %copy-start.1 = (bf16[448,2432]{1,0:T(8,128)(2,1)S(1)}, bf16[448,2432]{1,0:T(8,128)(2,1)}, u32[]{:S(2)}) copy-start(bf16[448,2432]{1,0:T(8,128)(2,1)} %rest_4_.1) | copy-start | bytes 6537220
  123.3 39.0 %all-to-all-start.3 = ((bf16[32,2,1344]{2,1,0:T(2,128)(2,1)}), bf16[32,2,1344]{2,1,0:T(2,128)(2,1)S(1)}, u32[]{:S(2)}, u32[]{:S(2)}) async-start(bf16[32,2,1344]{2,1,0:T(2,128)(2,1)} %shard_map.98), calls=%async_computation.3 | async-start | bytes 360448 | tf_op jit(solution)/shard_map/all_to_all | solution.py:321
  127.3 7.3 %collective-permute-start.8 = (bf16[152,256]{1,0:T(8,128)(2,1)S(1)}, bf16[152,256]{1,0:T(8,128)(2,1)S(1)}, u32[]{:S(2)}, u32[]{:S(2)}) collective-permute-start(bf16[152,256]{1,0:T(8,128)(2,1)S(1)} %shard_map.99), channel_id=1, source_target_pairs={{0,3},{1,0},{2,1},{3,2},{4,7},{5,4},{6,5},{7,6},{8,11},{9,8},{10,9... | collective-permute-start | bytes 233480 | tf_op jit(solution)/shard_map/ppermute | solution.py:210
  130.1 6.9 %collective-permute-start.7 = (bf16[152,256]{1,0:T(8,128)(2,1)S(1)}, bf16[152,256]{1,0:T(8,128)(2,1)S(1)}, u32[]{:S(2)}, u32[]{:S(2)}) collective-permute-start(bf16[152,256]{1,0:T(8,128)(2,1)S(1)} %shard_map.99), channel_id=1, source_target_pairs={{0,2},{1,3},{2,0},{3,1},{4,6},{5,7},{6,4},{7,5},{8,10},{9,11},{10,... | collective-permute-start | bytes 233480 | tf_op jit(solution)/shard_map/ppermute | solution.py:210
  132.7 6.6 %collective-permute-start.6 = (bf16[152,256]{1,0:T(8,128)(2,1)S(1)}, bf16[152,256]{1,0:T(8,128)(2,1)S(1)}, u32[]{:S(2)}, u32[]{:S(2)}) collective-permute-start(bf16[152,256]{1,0:T(8,128)(2,1)S(1)} %shard_map.99), channel_id=1, source_target_pairs={{0,1},{1,2},{2,3},{3,0},{4,5},{5,6},{6,7},{7,4},{8,9},{9,10},{10,1... | collective-permute-start | bytes 233480 | tf_op jit(solution)/shard_map/ppermute | solution.py:210
  139.4 23.0 %copy-start.5 = (bf16[192,256]{1,0:T(8,128)(2,1)S(1)}, bf16[192,256]{1,0:T(8,128)(2,1)}, u32[]{:S(2)}) copy-start(bf16[192,256]{1,0:T(8,128)(2,1)} %get-tuple-element.88.chooser) | copy-start | bytes 294916
  139.4 8.4 %collective-permute-start.11 = (bf16[4,152,256]{2,1,0:T(8,128)(2,1)S(1)}, bf16[4,152,256]{2,1,0:T(8,128)(2,1)S(1)}, u32[]{:S(2)}, u32[]{:S(2)}) collective-permute-start(bf16[4,152,256]{2,1,0:T(8,128)(2,1)S(1)} %pad_maximum_fusion.rest_0_), channel_id=1, source_target_pairs={{0,12},{1,13},{2,14},{3,15},{4,0},{5,1},{6,2},{7,3},{8,4},{9,5},{1... | collective-permute-start | bytes 933896 | tf_op jit(solution)/shard_map/ppermute | solution.py:210
  142.4 9.4 %collective-permute-start.10 = (bf16[4,152,256]{2,1,0:T(8,128)(2,1)S(1)}, bf16[4,152,256]{2,1,0:T(8,128)(2,1)S(1)}, u32[]{:S(2)}, u32[]{:S(2)}) collective-permute-start(bf16[4,152,256]{2,1,0:T(8,128)(2,1)S(1)} %pad_maximum_fusion.rest_0_), channel_id=1, source_target_pairs={{0,8},{1,9},{2,10},{3,11},{4,12},{5,13},{6,14},{7,15},{8,0},{9,1},... | collective-permute-start | bytes 933896 | tf_op jit(solution)/shard_map/ppermute | solution.py:210
  145.4 9.8 %collective-permute-start.9 = (bf16[4,152,256]{2,1,0:T(8,128)(2,1)S(1)}, bf16[4,152,256]{2,1,0:T(8,128)(2,1)S(1)}, u32[]{:S(2)}, u32[]{:S(2)}) collective-permute-start(bf16[4,152,256]{2,1,0:T(8,128)(2,1)S(1)} %pad_maximum_fusion.rest_0_), channel_id=1, source_target_pairs={{0,4},{1,5},{2,6},{3,7},{4,8},{5,9},{6,10},{7,11},{8,12},{9,13},{1... | collective-permute-start | bytes 933896 | tf_op jit(solution)/shard_map/ppermute | solution.py:210
  (4 other events, 5.2 us)

commit v9 on v8

--- a/solution.py
+++ b/solution.py
@@ -35,11 +35,17 @@
     return lax.broadcasted_iota(jnp.int32, shape, dim)
 
 
+LANES = 128
+
+
 def packed(rows):
-    count = rows.shape[0] // CAP
+    count, cut = rows.shape[0] // CAP, rows.shape[1] // LANES * LANES
+    split = [rows[count * i : count * (i + 1)] for i in range(CAP)]
     sides = [
         jnp.concatenate(
-            [rows[count * (3 * side + i) : count * (3 * side + i + 1)] for i in range(3)], axis=1
+            [row[:, :cut] for row in split[3 * side : 3 * side + 3]]
+            + [row[:, cut:] for row in split[3 * side : 3 * side + 3]],
+            axis=1,
         )
         for side in range(2)
     ]
@@ -49,9 +55,14 @@
 def unpacked(message):
     wide = message.astype(F32)
     width = wide.shape[2] // 3
-    rows = [
-        wide[:, side, width * i : width * (i + 1)] for side in range(2) for i in range(3)
-    ]
+    cut = width // LANES * LANES
+    tail = width - cut
+    rows = []
+    for side in range(2):
+        for i in range(3):
+            low = 3 * cut + tail * i
+            main = wide[:, side, cut * i : cut * (i + 1)]
+            rows.append(jnp.concatenate([main, wide[:, side, low : low + tail]], axis=1))
     return jnp.concatenate(rows, axis=0).astype(BF16)
 
 

time: 164 us -> 165 us (level)
  no operation moved by 1% of the time
where the time goes in v9:
time: 165 us; the launch traced here: 164 us
  starting transfers between devices  81.9 us (50%)
  waiting for transfers between devices  56.4 us (34%)
  Pallas kernels  13.2 us (8%)
  blocking collectives  9.11 us (6%)
  local copies, waits for them, and re-layouts  2.6 us (2%)
    ppermute x12, starting transfers between devices, moved(): return lax.ppermute(value, ('c', 'x', 'y'), pairs)  37 us
    all_to_all x1, starting transfers between devices, shards(): arrived = lax.all_to_all(message, 'z', 0, 0, tiled=True)  29.3 us
    all_to_all x1, waiting for transfers between devices, shards(): arrived = lax.all_to_all(message, 'z', 0, 0, tiled=True)  19.3 us
    ppermute x12, waiting for transfers between devices, moved(): return lax.ppermute(value, ('c', 'x', 'y'), pairs)  17.2 us
    all_to_all x1, waiting for transfers between devices, shards(): full = lax.all_to_all(copies, tensor, 0, 0, tiled=True)  14.3 us
    pallas_call x11, Pallas kernels, call(): pl.pallas_call(kernel, out_shape=outs, in_specs=[pl.BlockSpec(memory_spac...  13.2 us
    all_to_all x1, starting transfers between devices, shards(): shares = lax.all_to_all(mid, tensor, 0, 0, tiled=True)  6.9 us
    all_to_all x1, waiting for transfers between devices, shards(): returned = lax.all_to_all(back, 'z', 0, 0, tiled=True)  5.64 us
  transfers between devices with their start and end apart: 16, of which 9 were waited for; matrix products, arithmetic and copies ran while one was open for 0% of the time, Pallas kernels for 2%

profile of v9, /device:TPU:1, one launch (start us, length us, event | category | flops | bytes accessed | tf_op | source)
XLA Modules:
  0.0 163.7 jit_solution(9038630180330779096)
XLA Ops:
  2.3 29.3 %all-to-all-start = ((bf16[32,2,1344]{2,1,0:T(2,128)(2,1)}), bf16[32,2,1344]{2,1,0:T(2,128)(2,1)S(1)}, u32[]{:S(2)}, u32[]{:S(2)}) async-start(bf16[32,2,1344]{2,1,0:T(2,128)(2,1)} %get-tuple-element.50), calls=%async_computation | async-start | bytes 360448 | tf_op jit(solution)/shard_map/all_to_all | solution.py:264
  35.8 3.2 %collective-permute-start = (bf16[4,152,256]{2,1,0:T(8,128)(2,1)S(1)}, bf16[4,152,256]{2,1,0:T(8,128)(2,1)S(1)}, u32[]{:S(2)}, u32[]{:S(2)}) collective-permute-start(bf16[4,152,256]{2,1,0:T(8,128)(2,1)S(1)} %get-tuple-element.53), channel_id=1, source_target_pairs={{0,4},{1,5},{2,6},{3,7},{4,8},{5,9},{6,10},{7,11},{8,12},{9,13},{1... | collective-permute-start | bytes 933896 | tf_op jit(solution)/shard_map/ppermute | solution.py:221
  39.0 4.5 %collective-permute-start.1 = (bf16[4,152,256]{2,1,0:T(8,128)(2,1)S(1)}, bf16[4,152,256]{2,1,0:T(8,128)(2,1)S(1)}, u32[]{:S(2)}, u32[]{:S(2)}) collective-permute-start(bf16[4,152,256]{2,1,0:T(8,128)(2,1)S(1)} %get-tuple-element.54), channel_id=1, source_target_pairs={{0,8},{1,9},{2,10},{3,11},{4,12},{5,13},{6,14},{7,15},{8,0},{9,1},... | collective-permute-start | bytes 933896 | tf_op jit(solution)/shard_map/ppermute | solution.py:221
  43.5 3.0 %collective-permute-start.2 = (bf16[4,152,256]{2,1,0:T(8,128)(2,1)S(1)}, bf16[4,152,256]{2,1,0:T(8,128)(2,1)S(1)}, u32[]{:S(2)}, u32[]{:S(2)}) collective-permute-start(bf16[4,152,256]{2,1,0:T(8,128)(2,1)S(1)} %get-tuple-element.55), channel_id=1, source_target_pairs={{0,12},{1,13},{2,14},{3,15},{4,0},{5,1},{6,2},{7,3},{8,4},{9,5},{1... | collective-permute-start | bytes 933896 | tf_op jit(solution)/shard_map/ppermute | solution.py:221
  46.5 19.3 %all-to-all-done = bf16[32,2,1344]{2,1,0:T(2,128)(2,1)S(1)} async-done(((bf16[32,2,1344]{2,1,0:T(2,128)(2,1)}), bf16[32,2,1344]{2,1,0:T(2,128)(2,1)S(1)}, u32[]{:S(2)}, u32[]{:S(2)}) %all-to-all-start) | async-done | bytes 172064 | tf_op jit(solution)/shard_map/all_to_all | solution.py:264
  65.8 4.1 %all-gather = bf16[64,2,1344]{2,1,0:T(2,128)(2,1)S(1)} all-gather(bf16[32,2,1344]{2,1,0:T(2,128)(2,1)S(1)} %all-to-all-done), channel_id=2, replica_groups=mesh['z'=32,'c'=2,'x'=4,'y'=4] {'c'}, dimensions={0}, use_global_device_ids=true | all-gather | bytes 516096 | tf_op jit(solution)/shard_map/all_gather | solution.py:275
  69.9 2.5 %shard_map.93 = bf16[16,76,384]{2,1,0:T(8,128)(2,1)} custom-call(bf16[2,32,2,1344]{3,2,1,0:T(2,128)(2,1)S(1)} %bitcast.26, bf16[448,1216]{1,0:T(8,128)(2,1)S(1)} %bitcast.27), custom_call_target="tpu_custom_call" | custom-call | bytes 1433600 | tf_op jit(solution)/shard_map/pallas_call | solution.py:17
  72.5 6.9 %all-to-all-start.1 = ((bf16[16,76,384]{2,1,0:T(8,128)(2,1)}), bf16[16,76,384]{2,1,0:T(8,128)(2,1)S(1)}, u32[]{:S(2)}, u32[]{:S(2)}) async-start(bf16[16,76,384]{2,1,0:T(8,128)(2,1)} %shard_map.93), calls=%async_computation.1 | async-start | bytes 1966080 | tf_op jit(solution)/shard_map/all_to_all | solution.py:288
  80.1 3.3 %collective-permute-start.3 = (bf16[152,256]{1,0:T(8,128)(2,1)S(1)}, bf16[152,256]{1,0:T(8,128)(2,1)S(1)}, u32[]{:S(2)}, u32[]{:S(2)}) collective-permute-start(bf16[152,256]{1,0:T(8,128)(2,1)S(1)} %get-tuple-element.67), channel_id=1, source_target_pairs={{0,1},{1,2},{2,3},{3,0},{4,5},{5,6},{6,7},{7,4},{8,9},{9,10},{10,1... | collective-permute-start | bytes 233480 | tf_op jit(solution)/shard_map/ppermute | solution.py:221
  83.3 4.3 %collective-permute-start.4 = (bf16[152,256]{1,0:T(8,128)(2,1)S(1)}, bf16[152,256]{1,0:T(8,128)(2,1)S(1)}, u32[]{:S(2)}, u32[]{:S(2)}) collective-permute-start(bf16[152,256]{1,0:T(8,128)(2,1)S(1)} %get-tuple-element.68), channel_id=1, source_target_pairs={{0,2},{1,3},{2,0},{3,1},{4,6},{5,7},{6,4},{7,5},{8,10},{9,11},{10,... | collective-permute-start | bytes 233480 | tf_op jit(solution)/shard_map/ppermute | solution.py:221
  87.7 3.1 %collective-permute-start.5 = (bf16[152,256]{1,0:T(8,128)(2,1)S(1)}, bf16[152,256]{1,0:T(8,128)(2,1)S(1)}, u32[]{:S(2)}, u32[]{:S(2)}) collective-permute-start(bf16[152,256]{1,0:T(8,128)(2,1)S(1)} %get-tuple-element.69), channel_id=1, source_target_pairs={{0,3},{1,0},{2,1},{3,2},{4,7},{5,4},{6,5},{7,6},{8,11},{9,8},{10,9... | collective-permute-start | bytes 233480 | tf_op jit(solution)/shard_map/ppermute | solution.py:221
  90.8 2.8 %collective-permute-done.3.rest_1_ = bf16[152,256]{1,0:T(8,128)(2,1)S(1)} collective-permute-done((bf16[152,256]{1,0:T(8,128)(2,1)S(1)}, bf16[152,256]{1,0:T(8,128)(2,1)S(1)}, u32[]{:S(2)}, u32[]{:S(2)}) %collective-permute-start.3) | collective-permute-done | bytes 77856 | tf_op jit(solution)/shard_map/ppermute | solution.py:221
  97.2 4.9 %all-to-all-start.2 = ((bf16[16,76,384]{2,1,0:T(8,128)(2,1)}), bf16[16,76,384]{2,1,0:T(8,128)(2,1)S(1)}, u32[]{:S(2)}, u32[]{:S(2)}) async-start(bf16[16,76,384]{2,1,0:T(8,128)(2,1)} %shard_map.95), calls=%async_computation.2 | async-start | bytes 1966080 | tf_op jit(solution)/shard_map/all_to_all | solution.py:307
  102.3 14.3 %all-to-all-done.2.full = bf16[16,76,384]{2,1,0:T(8,128)(2,1)S(1)} async-done(((bf16[16,76,384]{2,1,0:T(8,128)(2,1)}), bf16[16,76,384]{2,1,0:T(8,128)(2,1)S(1)}, u32[]{:S(2)}, u32[]{:S(2)}) %all-to-all-start.2) | async-done | bytes 933920 | tf_op jit(solution)/shard_map/all_to_all | solution.py:307
  117.4 5.0 %all-gather.1 = bf16[896,384]{1,0:T(8,128)(2,1)S(1)} all-gather(bf16[448,384]{1,0:T(8,128)(2,1)S(1)} %shard_map.97), channel_id=3, replica_groups=mesh['z'=32,'c'=2,'x'=4,'y'=4] {'c'}, dimensions={0}, use_global_device_ids=true | all-gather | bytes 1032192 | tf_op jit(solution)/shard_map/all_gather | solution.py:328
  123.6 3.9 %all-to-all-start.3 = ((bf16[32,2,1344]{2,1,0:T(2,128)(2,1)}), bf16[32,2,1344]{2,1,0:T(2,128)(2,1)S(1)}, u32[]{:S(2)}, u32[]{:S(2)}) async-start(bf16[32,2,1344]{2,1,0:T(2,128)(2,1)} %shard_map.98), calls=%async_computation.3 | async-start | bytes 360448 | tf_op jit(solution)/shard_map/all_to_all | solution.py:332
  127.6 2.8 %collective-permute-start.8 = (bf16[152,256]{1,0:T(8,128)(2,1)S(1)}, bf16[152,256]{1,0:T(8,128)(2,1)S(1)}, u32[]{:S(2)}, u32[]{:S(2)}) collective-permute-start(bf16[152,256]{1,0:T(8,128)(2,1)S(1)} %shard_map.99), channel_id=1, source_target_pairs={{0,3},{1,0},{2,1},{3,2},{4,7},{5,4},{6,5},{7,6},{8,11},{9,8},{10,9... | collective-permute-start | bytes 233480 | tf_op jit(solution)/shard_map/ppermute | solution.py:221
  130.4 2.5 %collective-permute-start.7 = (bf16[152,256]{1,0:T(8,128)(2,1)S(1)}, bf16[152,256]{1,0:T(8,128)(2,1)S(1)}, u32[]{:S(2)}, u32[]{:S(2)}) collective-permute-start(bf16[152,256]{1,0:T(8,128)(2,1)S(1)} %shard_map.99), channel_id=1, source_target_pairs={{0,2},{1,3},{2,0},{3,1},{4,6},{5,7},{6,4},{7,5},{8,10},{9,11},{10,... | collective-permute-start | bytes 233480 | tf_op jit(solution)/shard_map/ppermute | solution.py:221
  134.9 2.4 %collective-permute-done.7 = bf16[152,256]{1,0:T(8,128)(2,1)S(1)} collective-permute-done((bf16[152,256]{1,0:T(8,128)(2,1)S(1)}, bf16[152,256]{1,0:T(8,128)(2,1)S(1)}, u32[]{:S(2)}, u32[]{:S(2)}) %collective-permute-start.7) | collective-permute-done | bytes 77856 | tf_op jit(solution)/shard_map/ppermute | solution.py:221
  139.6 3.0 %collective-permute-start.11 = (bf16[4,152,256]{2,1,0:T(8,128)(2,1)S(1)}, bf16[4,152,256]{2,1,0:T(8,128)(2,1)S(1)}, u32[]{:S(2)}, u32[]{:S(2)}) collective-permute-start(bf16[4,152,256]{2,1,0:T(8,128)(2,1)S(1)} %pad_maximum_fusion.rest_0_), channel_id=1, source_target_pairs={{0,12},{1,13},{2,14},{3,15},{4,0},{5,1},{6,2},{7,3},{8,4},{9,5},{1... | collective-permute-start | bytes 933896 | tf_op jit(solution)/shard_map/ppermute | solution.py:221
  142.7 3.0 %collective-permute-start.10 = (bf16[4,152,256]{2,1,0:T(8,128)(2,1)S(1)}, bf16[4,152,256]{2,1,0:T(8,128)(2,1)S(1)}, u32[]{:S(2)}, u32[]{:S(2)}) collective-permute-start(bf16[4,152,256]{2,1,0:T(8,128)(2,1)S(1)} %pad_maximum_fusion.rest_0_), channel_id=1, source_target_pairs={{0,8},{1,9},{2,10},{3,11},{4,12},{5,13},{6,14},{7,15},{8,0},{9,1},... | collective-permute-start | bytes 933896 | tf_op jit(solution)/shard_map/ppermute | solution.py:221
  148.0 4.1 %collective-permute-done.10.rest_2_ = bf16[4,152,256]{2,1,0:T(8,128)(2,1)S(1)} collective-permute-done((bf16[4,152,256]{2,1,0:T(8,128)(2,1)S(1)}, bf16[4,152,256]{2,1,0:T(8,128)(2,1)S(1)}, u32[]{:S(2)}, u32[]{:S(2)}) %collective-permute-start.10) | collective-permute-done | bytes 311328 | tf_op jit(solution)/shard_map/ppermute | solution.py:221
  152.1 3.3 %collective-permute-done.9.rest_1_ = bf16[4,152,256]{2,1,0:T(8,128)(2,1)S(1)} collective-permute-done((bf16[4,152,256]{2,1,0:T(8,128)(2,1)S(1)}, bf16[4,152,256]{2,1,0:T(8,128)(2,1)S(1)}, u32[]{:S(2)}, u32[]{:S(2)}) %collective-permute-start.9) | collective-permute-done | bytes 311328 | tf_op jit(solution)/shard_map/ppermute | solution.py:221
  156.9 5.6 %all-to-all-done.3.returned = bf16[32,2,1344]{2,1,0:T(2,128)(2,1)S(1)} async-done(((bf16[32,2,1344]{2,1,0:T(2,128)(2,1)}), bf16[32,2,1344]{2,1,0:T(2,128)(2,1)S(1)}, u32[]{:S(2)}, u32[]{:S(2)}) %all-to-all-start.3) | async-done | bytes 172064 | tf_op jit(solution)/shard_map/all_to_all | solution.py:332
  (47 shorter events, 22.3 us)
Async XLA Ops:
  2.3 63.5 %all-to-all-start = ((bf16[32,2,1344]{2,1,0:T(2,128)(2,1)}), bf16[32,2,1344]{2,1,0:T(2,128)(2,1)S(1)}, u32[]{:S(2)}, u32[]{:S(2)}) async-start(bf16[32,2,1344]{2,1,0:T(2,128)(2,1)} %get-tuple-element.50), calls=%async_computation | async-start | bytes 360448 | tf_op jit(solution)/shard_map/all_to_all | solution.py:264
  34.2 35.7 %copy-start.2 = (bf16[1,1216,448]{1,2,0:T(8,128)(2,1)S(1)}, bf16[1,1216,448]{1,2,0:T(8,128)(2,1)}, u32[]{:S(2)}) copy-start(bf16[1,1216,448]{1,2,0:T(8,128)(2,1)} %param.15) | copy-start | bytes 3268612
  35.8 34.1 %collective-permute-start = (bf16[4,152,256]{2,1,0:T(8,128)(2,1)S(1)}, bf16[4,152,256]{2,1,0:T(8,128)(2,1)S(1)}, u32[]{:S(2)}, u32[]{:S(2)}) collective-permute-start(bf16[4,152,256]{2,1,0:T(8,128)(2,1)S(1)} %get-tuple-element.53), channel_id=1, source_target_pairs={{0,4},{1,5},{2,6},{3,7},{4,8},{5,9},{6,10},{7,11},{8,12},{9,13},{1... | collective-permute-start | bytes 933896 | tf_op jit(solution)/shard_map/ppermute | solution.py:221
  39.0 30.9 %collective-permute-start.1 = (bf16[4,152,256]{2,1,0:T(8,128)(2,1)S(1)}, bf16[4,152,256]{2,1,0:T(8,128)(2,1)S(1)}, u32[]{:S(2)}, u32[]{:S(2)}) collective-permute-start(bf16[4,152,256]{2,1,0:T(8,128)(2,1)S(1)} %get-tuple-element.54), channel_id=1, source_target_pairs={{0,8},{1,9},{2,10},{3,11},{4,12},{5,13},{6,14},{7,15},{8,0},{9,1},... | collective-permute-start | bytes 933896 | tf_op jit(solution)/shard_map/ppermute | solution.py:221
  43.5 26.4 %collective-permute-start.2 = (bf16[4,152,256]{2,1,0:T(8,128)(2,1)S(1)}, bf16[4,152,256]{2,1,0:T(8,128)(2,1)S(1)}, u32[]{:S(2)}, u32[]{:S(2)}) collective-permute-start(bf16[4,152,256]{2,1,0:T(8,128)(2,1)S(1)} %get-tuple-element.55), channel_id=1, source_target_pairs={{0,12},{1,13},{2,14},{3,15},{4,0},{5,1},{6,2},{7,3},{8,4},{9,5},{1... | collective-permute-start | bytes 933896 | tf_op jit(solution)/shard_map/ppermute | solution.py:221
  72.4 23.5 %copy-start.11 = (bf16[1,384,76]{1,2,0:T(8,128)(2,1)S(1)}, bf16[1,384,76]{1,2,0:T(8,128)(2,1)}, u32[]{:S(2)}) copy-start(bf16[1,384,76]{1,2,0:T(8,128)(2,1)} %param.17) | copy-start | bytes 175108
  72.5 23.4 %all-to-all-start.1 = ((bf16[16,76,384]{2,1,0:T(8,128)(2,1)}), bf16[16,76,384]{2,1,0:T(8,128)(2,1)S(1)}, u32[]{:S(2)}, u32[]{:S(2)}) async-start(bf16[16,76,384]{2,1,0:T(8,128)(2,1)} %shard_map.93), calls=%async_computation.1 | async-start | bytes 1966080 | tf_op jit(solution)/shard_map/all_to_all | solution.py:288
  80.1 13.5 %collective-permute-start.3 = (bf16[152,256]{1,0:T(8,128)(2,1)S(1)}, bf16[152,256]{1,0:T(8,128)(2,1)S(1)}, u32[]{:S(2)}, u32[]{:S(2)}) collective-permute-start(bf16[152,256]{1,0:T(8,128)(2,1)S(1)} %get-tuple-element.67), channel_id=1, source_target_pairs={{0,1},{1,2},{2,3},{3,0},{4,5},{5,6},{6,7},{7,4},{8,9},{9,10},{10,1... | collective-permute-start | bytes 233480 | tf_op jit(solution)/shard_map/ppermute | solution.py:221
  83.3 12.5 %collective-permute-start.4 = (bf16[152,256]{1,0:T(8,128)(2,1)S(1)}, bf16[152,256]{1,0:T(8,128)(2,1)S(1)}, u32[]{:S(2)}, u32[]{:S(2)}) collective-permute-start(bf16[152,256]{1,0:T(8,128)(2,1)S(1)} %get-tuple-element.68), channel_id=1, source_target_pairs={{0,2},{1,3},{2,0},{3,1},{4,6},{5,7},{6,4},{7,5},{8,10},{9,11},{10,... | collective-permute-start | bytes 233480 | tf_op jit(solution)/shard_map/ppermute | solution.py:221
  87.7 8.2 %collective-permute-start.5 = (bf16[152,256]{1,0:T(8,128)(2,1)S(1)}, bf16[152,256]{1,0:T(8,128)(2,1)S(1)}, u32[]{:S(2)}, u32[]{:S(2)}) collective-permute-start(bf16[152,256]{1,0:T(8,128)(2,1)S(1)} %get-tuple-element.69), channel_id=1, source_target_pairs={{0,3},{1,0},{2,1},{3,2},{4,7},{5,4},{6,5},{7,6},{8,11},{9,8},{10,9... | collective-permute-start | bytes 233480 | tf_op jit(solution)/shard_map/ppermute | solution.py:221
  97.2 4.9 %copy-start.3 = (bf16[1,448,1216]{2,1,0:T(8,128)(2,1)S(1)}, bf16[1,448,1216]{2,1,0:T(8,128)(2,1)}, u32[]{:S(2)}) copy-start(bf16[1,448,1216]{2,1,0:T(8,128)(2,1)} %param.16) | copy-start | bytes 3268612
  97.2 19.3 %all-to-all-start.2 = ((bf16[16,76,384]{2,1,0:T(8,128)(2,1)}), bf16[16,76,384]{2,1,0:T(8,128)(2,1)S(1)}, u32[]{:S(2)}, u32[]{:S(2)}) async-start(bf16[16,76,384]{2,1,0:T(8,128)(2,1)} %shard_map.95), calls=%async_computation.2 | async-start | bytes 1966080 | tf_op jit(solution)/shard_map/all_to_all | solution.py:307
  117.3 10.2 %copy-start.6 = (bf16[256,152]{0,1:T(8,128)(2,1)S(1)}, bf16[256,152]{0,1:T(8,128)(2,1)}, u32[]{:S(2)}) copy-start(bf16[256,152]{0,1:T(8,128)(2,1)} %param.14) | copy-start | bytes 233476
  117.3 10.2 %copy-start.8 = (bf16[152,256]{1,0:T(8,128)(2,1)S(1)}, bf16[152,256]{1,0:T(8,128)(2,1)}, u32[]{:S(2)}) copy-start(bf16[152,256]{1,0:T(8,128)(2,1)} %copy-done.7) | copy-start | bytes 233476
  117.3 10.2 %copy-start.10 = (bf16[152,256]{1,0:T(8,128)(2,1)S(1)}, bf16[152,256]{1,0:T(8,128)(2,1)}, u32[]{:S(2)}) copy-start(bf16[152,256]{1,0:T(8,128)(2,1)} %copy-done.9) | copy-start | bytes 233476
  122.4 33.1 %copy-start.1 = (bf16[448,2432]{1,0:T(8,128)(2,1)S(1)}, bf16[448,2432]{1,0:T(8,128)(2,1)}, u32[]{:S(2)}) copy-start(bf16[448,2432]{1,0:T(8,128)(2,1)} %rest_4_.1) | copy-start | bytes 6537220
  123.6 39.0 %all-to-all-start.3 = ((bf16[32,2,1344]{2,1,0:T(2,128)(2,1)}), bf16[32,2,1344]{2,1,0:T(2,128)(2,1)S(1)}, u32[]{:S(2)}, u32[]{:S(2)}) async-start(bf16[32,2,1344]{2,1,0:T(2,128)(2,1)} %shard_map.98), calls=%async_computation.3 | async-start | bytes 360448 | tf_op jit(solution)/shard_map/all_to_all | solution.py:332
  127.6 7.3 %collective-permute-start.8 = (bf16[152,256]{1,0:T(8,128)(2,1)S(1)}, bf16[152,256]{1,0:T(8,128)(2,1)S(1)}, u32[]{:S(2)}, u32[]{:S(2)}) collective-permute-start(bf16[152,256]{1,0:T(8,128)(2,1)S(1)} %shard_map.99), channel_id=1, source_target_pairs={{0,3},{1,0},{2,1},{3,2},{4,7},{5,4},{6,5},{7,6},{8,11},{9,8},{10,9... | collective-permute-start | bytes 233480 | tf_op jit(solution)/shard_map/ppermute | solution.py:221
  130.4 6.9 %collective-permute-start.7 = (bf16[152,256]{1,0:T(8,128)(2,1)S(1)}, bf16[152,256]{1,0:T(8,128)(2,1)S(1)}, u32[]{:S(2)}, u32[]{:S(2)}) collective-permute-start(bf16[152,256]{1,0:T(8,128)(2,1)S(1)} %shard_map.99), channel_id=1, source_target_pairs={{0,2},{1,3},{2,0},{3,1},{4,6},{5,7},{6,4},{7,5},{8,10},{9,11},{10,... | collective-permute-start | bytes 233480 | tf_op jit(solution)/shard_map/ppermute | solution.py:221
  132.9 6.6 %collective-permute-start.6 = (bf16[152,256]{1,0:T(8,128)(2,1)S(1)}, bf16[152,256]{1,0:T(8,128)(2,1)S(1)}, u32[]{:S(2)}, u32[]{:S(2)}) collective-permute-start(bf16[152,256]{1,0:T(8,128)(2,1)S(1)} %shard_map.99), channel_id=1, source_target_pairs={{0,1},{1,2},{2,3},{3,0},{4,5},{5,6},{6,7},{7,4},{8,9},{9,10},{10,1... | collective-permute-start | bytes 233480 | tf_op jit(solution)/shard_map/ppermute | solution.py:221
  139.6 23.0 %copy-start.5 = (bf16[192,256]{1,0:T(8,128)(2,1)S(1)}, bf16[192,256]{1,0:T(8,128)(2,1)}, u32[]{:S(2)}) copy-start(bf16[192,256]{1,0:T(8,128)(2,1)} %get-tuple-element.88.chooser) | copy-start | bytes 294916
  139.6 8.4 %collective-permute-start.11 = (bf16[4,152,256]{2,1,0:T(8,128)(2,1)S(1)}, bf16[4,152,256]{2,1,0:T(8,128)(2,1)S(1)}, u32[]{:S(2)}, u32[]{:S(2)}) collective-permute-start(bf16[4,152,256]{2,1,0:T(8,128)(2,1)S(1)} %pad_maximum_fusion.rest_0_), channel_id=1, source_target_pairs={{0,12},{1,13},{2,14},{3,15},{4,0},{5,1},{6,2},{7,3},{8,4},{9,5},{1... | collective-permute-start | bytes 933896 | tf_op jit(solution)/shard_map/ppermute | solution.py:221
  142.7 9.4 %collective-permute-start.10 = (bf16[4,152,256]{2,1,0:T(8,128)(2,1)S(1)}, bf16[4,152,256]{2,1,0:T(8,128)(2,1)S(1)}, u32[]{:S(2)}, u32[]{:S(2)}) collective-permute-start(bf16[4,152,256]{2,1,0:T(8,128)(2,1)S(1)} %pad_maximum_fusion.rest_0_), channel_id=1, source_target_pairs={{0,8},{1,9},{2,10},{3,11},{4,12},{5,13},{6,14},{7,15},{8,0},{9,1},... | collective-permute-start | bytes 933896 | tf_op jit(solution)/shard_map/ppermute | solution.py:221
  145.7 9.8 %collective-permute-start.9 = (bf16[4,152,256]{2,1,0:T(8,128)(2,1)S(1)}, bf16[4,152,256]{2,1,0:T(8,128)(2,1)S(1)}, u32[]{:S(2)}, u32[]{:S(2)}) collective-permute-start(bf16[4,152,256]{2,1,0:T(8,128)(2,1)S(1)} %pad_maximum_fusion.rest_0_), channel_id=1, source_target_pairs={{0,4},{1,5},{2,6},{3,7},{4,8},{5,9},{6,10},{7,11},{8,12},{9,13},{1... | collective-permute-start | bytes 933896 | tf_op jit(solution)/shard_map/ppermute | solution.py:221
  (4 other events, 5.2 us)
